TPU v7x, 32 devices: a whole 2x2x4 slice. The times are simulated.
32 devices in a mesh: grp: 2 (over x), chol: 16 (over z, y, core).
Axes of the slice: x: 2, y: 2, z: 4, core: 2. Of those that a mesh axis runs over, the one named last changes fastest.
Arguments:
- chol_vectors: bfloat16 [2048, 32768], P(None, 'chol'), may hold values from -0.03125 to 0.03125
- mean_greens: bfloat16 [32768], P('chol'), may hold values from -6 to 6
- greens: bfloat16 [512, 32768], P(('grp', 'chol')), parts along dimension 0, may hold values from -6 to 6
- walker_order: int32 [512], P('grp'), parts along dimension 0, may hold values from 0 to 255, each once
- noise_field: float32 [512, 2048], P(('grp', 'chol')), parts along dimension 0, may hold values from -6 to 6
Outputs:
- shifted_field: float32 [512, 2048], P(('grp', 'chol')), parts along dimension 0
There are 2 independent parts, one for each index of `grp`. A program takes and returns all parts, laid end to end along the dimension named above; an argument that names none is the same for every part. Nothing has to cross between parts.
Inputs may be any that keep to these rules, and one draw needn't show every extreme that they name: `walker_order`: each row of greens appears once.
All inputs are finite; a program needn't handle non-finite values.
Results may differ from a plain program's by a relative error of at most 0.0012.
Values may be sent and summed in bfloat16 or wider, within the bound.
No kernel may reach another device: no remote copies, remote signals or barrier semaphores. Data moves between devices by JAX's collectives and lax.ppermute only.
A program may use at most 64 MiB of HBM per device.

v0:
```python
import jax
import jax.numpy as jnp
from jax import lax
from jax.sharding import PartitionSpec as P


def contract(left, right):
    return lax.dot_general(
        left, right, (((1,), (1,)), ((), ())), preferred_element_type=jnp.float32
    )


def per_device(chol_vectors, mean_greens, greens, walker_order, noise_field):
    pair_rows = lax.all_to_all(greens, "chol", split_axis=1, concat_axis=0, tiled=True)
    mean_part = jnp.dot(chol_vectors, mean_greens, preferred_element_type=jnp.float32)
    mean_field = lax.psum(mean_part, "chol")
    picked = jnp.take(pair_rows, walker_order, axis=0)
    raw_bias = lax.psum_scatter(
        contract(picked, chol_vectors), "chol", scatter_dimension=0, tiled=True
    )
    shift = jnp.tanh(raw_bias) - mean_field[None, :]
    return noise_field - shift


def solution(mesh):
    placed = (
        P(None, "chol"),
        P("chol"),
        P(("grp", "chol"), None),
        P("grp"),
        P(("grp", "chol"), None),
    )
    return jax.shard_map(
        per_device, mesh=mesh, in_specs=placed, out_specs=P(("grp", "chol"), None), check_vma=False
    )
```

profile of v0, /device:TPU:0, one launch (start us, length us, event | category | flops | bytes accessed | tf_op | source)
XLA Modules:
  0.0 120.4 jit_solution(17142150962512619396)
XLA Ops:
  6.5 2.3 %copy.9 = bf16[2,16,8,2048]{3,2,0,1:T(8,128)(2,1)} copy(bf16[2,16,8,2048]{3,2,1,0:T(8,128)(2,1)} %bitcast.12) | data formatting | bytes 2097152 | tf_op jit(solution)/shard_map/all_to_all | solution.py:14
  8.8 7.4 %all-to-all-start = ((bf16[16,16,2048]{2,0,1:T(8,128)(2,1)}), bf16[16,16,2048]{2,0,1:T(8,128)(2,1)S(1)}, u32[]{:S(2)}, u32[]{:S(2)}) async-start(bf16[16,16,2048]{2,0,1:T(8,128)(2,1)} %bitcast.10), calls=%async_computation | async-start | bytes 2097152 | tf_op jit(solution)/shard_map/all_to_all | solution.py:14
  16.2 0.0 reduce-scatter.2.cloned.1.call-start
  16.3 0.7 compare_select_fusion
  17.0 0.7 compare_and_fusion
  17.7 21.5 %all-to-all-done = bf16[16,16,2048]{2,0,1:T(8,128)(2,1)S(1)} async-done(((bf16[16,16,2048]{2,0,1:T(8,128)(2,1)}), bf16[16,16,2048]{2,0,1:T(8,128)(2,1)S(1)}, u32[]{:S(2)}, u32[]{:S(2)}) %all-to-all-start) | async-done | bytes 1048608 | tf_op jit(solution)/shard_map/all_to_all | solution.py:14
  39.2 1.4 %gather_fusion = bf16[256,2048]{1,0:T(8,128)(2,1)S(1)} fusion(bf16[256,2048]{1,0:T(8,128)(2,1)S(1)} %bitcast.11, s32[1024]{0:T(1024)S(1)} %pad_clamp_fusion), kind=kCustom, calls=%fused_computation | custom fusion | bytes 2098176 | tf_op jit(solution)/shard_map/jit(_take)/gather | solution.py:17
  40.5 0.0 copy-start.1
  40.6 7.2 %fusion = f32[256,2048]{1,0:T(8,128)} fusion(bf16[2048,2048]{1,0:T(8,128)(2,1)} %param.5, bf16[256,2048]{1,0:T(8,128)(2,1)S(1)} %gather_fusion, pred[256]{0:T(512)(128)(4,1)S(1)} %compare_and_fusion), kind=kOutput, calls=%fused_computation.2 | convolution fusion | flops 2148007936 | bytes 11534592 | tf_op jit(solution)/shard_map/dot_general | solution.py:8
  47.7 0.0 copy-start
  47.7 0.0 reduce-scatter.2.cloned.1.call-update
  47.7 0.0 copy-done.1
  47.8 5.7 %fusion.5 = f32[1,2048]{1,0:T(1,128)S(1)} fusion(bf16[2048,2048]{1,0:T(8,128)(2,1)} %param.5, bf16[2048,1]{0,1:T(2,128)(2,1)S(1)} %reshape.18), kind=kOutput, calls=%fused_computation.11 | convolution fusion | flops 8388608 | bytes 8400896 | tf_op jit(solution)/shard_map/dot_general | solution.py:15
  53.4 35.6 %psum.7 = f32[2048]{0:T(1024)S(1)} all-reduce(f32[2048]{0:T(1024)S(1)} %bitcast.13), channel_id=1, replica_groups=mesh['grp'=2,'chol'=16] {'chol'}, use_global_device_ids=true, to_apply=%region_1.2 | all-reduce | flops 2048 | bytes 16384 | tf_op jit(solution)/shard_map/psum | solution.py:16
  89.1 22.9 %reduce-scatter.2.cloned.1.call-done = f32[16,2048]{1,0:T(8,128)} async-done(((f32[256,2048]{1,0:T(8,128)}), f32[16,2048]{1,0:T(8,128)}) %reduce-scatter.2.cloned.1.call-update) | async-done | bytes 131088 | tf_op jit(solution)/shard_map/reduce_scatter | solution.py:18
  112.0 0.0 copy-done
  112.0 1.6 %subtract_subtract_fusion = f32[16,2048]{1,0:T(8,128)} fusion(f32[16,2048]{1,0:T(8,128)S(1)} %copy-done, f32[16,2048]{1,0:T(8,128)} %reduce-scatter.2.cloned.1.call-done, f32[2048]{0:T(1024)S(1)} %psum.7), kind=kLoop, calls=%fused_computation.6 | loop fusion | flops 65536 | bytes 401408 | tf_op jit(solution)/shard_map/sub | solution.py:22
  (2 shorter events, 0.0 us)
Async XLA Ops:
  8.8 30.3 %all-to-all-start = ((bf16[16,16,2048]{2,0,1:T(8,128)(2,1)}), bf16[16,16,2048]{2,0,1:T(8,128)(2,1)S(1)}, u32[]{:S(2)}, u32[]{:S(2)}) async-start(bf16[16,16,2048]{2,0,1:T(8,128)(2,1)} %bitcast.10), calls=%async_computation | async-start | bytes 2097152 | tf_op jit(solution)/shard_map/all_to_all | solution.py:14
  16.2 95.7 %reduce-scatter.2.cloned.1.call-start = ((), (), s32[]{:S(2)}) async-start(), calls=%async_computation.2 | async-start | bytes 2228224 | tf_op jit(solution)/shard_map/reduce_scatter | solution.py:18
  40.5 7.2 %copy-start.1 = (bf16[2048]{0:T(1024)(128)(2,1)S(1)}, bf16[2048]{0:T(1024)(128)(2,1)}, u32[]{:S(2)}) copy-start(bf16[2048]{0:T(1024)(128)(2,1)} %param.6) | copy-start | bytes 12292
  47.7 64.2 %copy-start = (f32[16,2048]{1,0:T(8,128)S(1)}, f32[16,2048]{1,0:T(8,128)}, u32[]{:S(2)}) copy-start(f32[16,2048]{1,0:T(8,128)} %param.9) | copy-start | bytes 393220
Sparse Core Ops, SparseCore 0:
  47.9 64.0 reduce-scatter.1
where the time goes:
time: 121 us; the launch traced here: 120 us
  waiting for transfers between devices  44.4 us (37%)
  blocking collectives  35.6 us (29%)
  between operations  13.4 us (11%)
  matrix products  12.8 us (11%)
  starting transfers between devices  7.43 us (6%)
  local copies, waits for them, and re-layouts  3.69 us (3%)
  other arithmetic  2.96 us (2%)
    psum x1, blocking collectives, per_device(): mean_field = lax.psum(mean_part, 'chol')  35.6 us
    reduce_scatter x1, waiting for transfers between devices, per_device(): lax.psum_scatter(contract(picked, chol_vectors), 'chol', scatter_dimensio...  22.9 us
    all_to_all x1, waiting for transfers between devices, per_device(): lax.all_to_all(greens, 'chol', split_axis=1, concat_axis=0, tiled=True)  21.5 us
    all_to_all x1, starting transfers between devices, per_device(): lax.all_to_all(greens, 'chol', split_axis=1, concat_axis=0, tiled=True)  7.39 us
    dot_general x1, matrix products, contract(): lax.dot_general(left, right, (((1,), (1,)), ((), ())), preferred_element_...  7.16 us
    dot_general x1, matrix products, per_device(): jnp.dot(chol_vectors, mean_greens, preferred_element_type=jnp.float32)  5.67 us
  transfers between devices with their start and end apart: 2, of which 2 were waited for; matrix products, arithmetic and copies ran while one was open for 6% of the time, Pallas kernels for 0%

commit v1 on v0

v1 whole, which is shorter than its diff:
```python
import functools

import jax
import jax.numpy as jnp
from jax import lax
from jax.experimental import pallas as pl
from jax.experimental.pallas import tpu as pltpu
from jax.sharding import PartitionSpec as P

F32, BF16 = jnp.float32, jnp.bfloat16
VMEM_BYTES = 56 * 2**20


def stage_radices(chips):
    radices = []
    while chips > 1:
        radix = 4 if chips % 4 == 0 else 2
        radices.append(radix)
        chips //= radix
    return radices


def swap(x, mask, n):
    return lax.ppermute(x, "chol", [(i, i ^ mask) for i in range(n)])


def bias_kernel(index_ref, rows_ref, chol_ref, keep_ref, send_ref, picked):
    half = keep_ref.shape[0]

    @pl.when(pl.program_id(0) == 0)
    def _():
        walkers = rows_ref.shape[0]
        chosen = index_ref[...] == lax.broadcasted_iota(jnp.int32, (2 * half, walkers), 1)
        picked[...] = jnp.dot(
            chosen.astype(BF16), rows_ref[...], preferred_element_type=F32
        ).astype(BF16)

    part = lax.dot_general(
        picked[...], chol_ref[...], (((1,), (1,)), ((), ())), preferred_element_type=F32
    )
    keep_ref[...] = part[:half]
    send_ref[...] = part[half:].astype(BF16)


def partial_bias(index, rows, chol, tile):
    slots, (nchol, pairs) = index.shape[0], chol.shape
    half = slots // 2
    return pl.pallas_call(
        bias_kernel,
        grid=(nchol // tile,),
        in_specs=[
            pl.BlockSpec((slots, 1), lambda g: (0, 0)),
            pl.BlockSpec(rows.shape, lambda g: (0, 0)),
            pl.BlockSpec((tile, pairs), lambda g: (g, 0)),
        ],
        out_specs=[pl.BlockSpec((half, tile), lambda g: (0, g))] * 2,
        out_shape=[
            jax.ShapeDtypeStruct((half, nchol), F32),
            jax.ShapeDtypeStruct((half, nchol), BF16),
        ],
        scratch_shapes=[pltpu.VMEM((slots, pairs), BF16)],
        compiler_params=pltpu.CompilerParams(vmem_limit_bytes=VMEM_BYTES),
        cost_estimate=pl.CostEstimate(
            flops=2 * slots * pairs * (nchol + rows.shape[0]),
            bytes_accessed=2 * nchol * pairs + 2 * rows.size + 6 * half * nchol,
            transcendentals=0,
        ),
    )(index, rows, chol)


def reduce_over_chips(held, radices, bit, n):
    if not radices:
        return held
    radix, rest = radices[0], radices[1:]
    later = 1
    for r in rest:
        later *= r
    rows, g = held.shape[-2:]
    held = held.reshape(radix, later, rows, g)
    shift = radix.bit_length() - 1
    total = held[0]
    if later > 1:
        onward = total[1:] + sum(
            swap(held[m, 1:].astype(BF16), m << bit, n).astype(F32) for m in range(1, radix)
        )
    mine = total[0] + sum(
        swap(held[m, 0].astype(BF16), m << bit, n).astype(F32) for m in range(1, radix)
    )
    if later == 1:
        return mine
    return reduce_over_chips(
        jnp.concatenate([mine[None], onward], axis=0), rest, bit + shift, n
    )


def per_device(n, chol_vectors, mean_greens, greens, walker_order, noise_field):
    me = lax.axis_index("chol")
    own = greens.shape[0]
    chips = n // 2
    radices = stage_radices(chips)

    mean_field = jnp.dot(chol_vectors, mean_greens, preferred_element_type=F32)
    for bit in range(n.bit_length() - 1):
        mean_field = mean_field + swap(mean_field, 1 << bit, n)

    place = jnp.arange(n, dtype=jnp.int32)
    relative, weight, left = place // chips, 2, place % chips
    for stage, radix in enumerate(radices):
        later = 1
        for r in radices[stage + 1 :]:
            later *= r
        relative = relative + weight * (left // later)
        left, weight = left % later, weight * radix
    owners = jnp.bitwise_xor(relative, me)
    slots = (owners[:, None] * own + jnp.arange(own, dtype=jnp.int32)[None, :]).reshape(-1)
    index = walker_order[slots]

    rows = lax.all_to_all(greens, "chol", split_axis=1, concat_axis=0, tiled=True)
    keep, send = partial_bias(index[:, None], rows, chol_vectors, 512)
    held = keep + swap(send, 1, n).astype(F32)
    raw_bias = reduce_over_chips(held.reshape(chips, own, -1), radices, 1, n).reshape(own, -1)
    shift = jnp.tanh(raw_bias) - mean_field[None, :]
    return noise_field - shift


def solution(mesh):
    placed = (
        P(None, "chol"),
        P("chol"),
        P(("grp", "chol"), None),
        P("grp"),
        P(("grp", "chol"), None),
    )
    return jax.shard_map(
        functools.partial(per_device, mesh.shape["chol"]),
        mesh=mesh,
        in_specs=placed,
        out_specs=P(("grp", "chol"), None),
        check_vma=False,
    )
```

time: 121 us -> 76.7 us (0.63)
  blocking collectives: 35.6 us -> 0 us
  starting transfers between devices: 7.43 us -> 21.6 us
  between operations: 13.4 us -> 0.1 us
  waiting for transfers between devices: 44.4 us -> 33.3 us
  Pallas kernels: 0 us -> 7.25 us
  matrix products: 12.8 us -> 5.64 us
  local copies, waits for them, and re-layouts: 3.69 us -> 6.21 us
    psum x1 -> x0, blocking collectives: 35.6 us -> none  [per_device(): mean_field = lax.psum(mean_part, 'chol')]
    reduce_scatter x1 -> x0, waiting for transfers between devices: 22.9 us -> none  [per_device(): lax.psum_scatter(contract(picked, chol_vectors), 'chol', scatter_dimensio...]
    ppermute x0 -> x12, starting transfers between devices: none -> 14.1 us  [swap(): return lax.ppermute(x, 'chol', [(i, i ^ mask) for i in range(n)])]
    ppermute x0 -> x12, waiting for transfers between devices: none -> 13.3 us  [swap(): return lax.ppermute(x, 'chol', [(i, i ^ mask) for i in range(n)])]
    pallas_call x0 -> x1, Pallas kernels: none -> 7.25 us  [partial_bias(): pl.pallas_call(bias_kernel, grid=(nchol // tile,), in_specs=[pl.BlockSpec...]
    dot_general x2 -> x1, matrix products: 12.8 us -> 5.64 us  [per_device(): mean_field = jnp.dot(chol_vectors, mean_greens, preferred_element_type=F32)]
    all_to_all x1, waiting for transfers between devices: 21.5 us -> 20 us  [per_device(): lax.all_to_all(greens, 'chol', split_axis=1, concat_axis=0, tiled=True)]
    another operation x0 -> x1, other arithmetic: none -> 1.39 us
  transfers between devices with their start and end apart: 2 -> 13, of which waited for: 2 -> 8; matrix products, arithmetic and copies ran while one was open for 6% -> 11% of each run, Pallas kernels for 0% -> 0%
where the time goes in v1:
time: 76.7 us; the launch traced here: 76.4 us
  waiting for transfers between devices  33.3 us (43%)
  starting transfers between devices  21.6 us (28%)
  Pallas kernels  7.25 us (9%)
  local copies, waits for them, and re-layouts  6.21 us (8%)
  matrix products  5.64 us (7%)
  other arithmetic  2.25 us (3%)
    all_to_all x1, waiting for transfers between devices, per_device(): lax.all_to_all(greens, 'chol', split_axis=1, concat_axis=0, tiled=True)  20 us
    ppermute x12, starting transfers between devices, swap(): return lax.ppermute(x, 'chol', [(i, i ^ mask) for i in range(n)])  14.1 us
    ppermute x12, waiting for transfers between devices, swap(): return lax.ppermute(x, 'chol', [(i, i ^ mask) for i in range(n)])  13.3 us
    all_to_all x1, starting transfers between devices, per_device(): lax.all_to_all(greens, 'chol', split_axis=1, concat_axis=0, tiled=True)  7.52 us
    pallas_call x1, Pallas kernels, partial_bias(): pl.pallas_call(bias_kernel, grid=(nchol // tile,), in_specs=[pl.BlockSpec...  7.25 us
    dot_general x1, matrix products, per_device(): mean_field = jnp.dot(chol_vectors, mean_greens, preferred_element_type=F32)  5.64 us
    all_to_all x1, local copies, waits for them, and re-layouts, per_device(): lax.all_to_all(greens, 'chol', split_axis=1, concat_axis=0, tiled=True)  2.34 us
    gather x1, local copies, waits for them, and re-layouts, per_device(): index = walker_order[slots]  1.95 us
  transfers between devices with their start and end apart: 13, of which 8 were waited for; matrix products, arithmetic and copies ran while one was open for 11% of the time, Pallas kernels for 0%

profile of v1, /device:TPU:0, one launch (start us, length us, event | category | flops | bytes accessed | tf_op | source)
XLA Modules:
  0.0 76.4 jit_solution(11182347290228218345)
XLA Ops:
  0.0 0.0 copy-start
  0.0 2.3 %copy.11 = bf16[2,16,8,2048]{3,2,0,1:T(8,128)(2,1)} copy(bf16[2,16,8,2048]{3,2,1,0:T(8,128)(2,1)} %bitcast.37) | data formatting | bytes 2097152 | tf_op jit(solution)/shard_map/all_to_all | solution.py:118
  2.3 0.0 copy-start.3
  2.3 7.5 %all-to-all-start = ((bf16[16,16,2048]{2,0,1:T(8,128)(2,1)}), bf16[16,16,2048]{2,0,1:T(8,128)(2,1)S(1)}, u32[]{:S(2)}, u32[]{:S(2)}) async-start(bf16[16,16,2048]{2,0,1:T(8,128)(2,1)} %bitcast.34), calls=%async_computation | async-start | bytes 2097152 | tf_op jit(solution)/shard_map/all_to_all | solution.py:118
  9.9 0.1 iota_add_fusion
  10.0 0.1 add.124
  10.1 0.0 copy-done
  10.1 1.9 %gather_fusion = s32[256]{0:T(256)S(1)} fusion(s32[256]{0:T(256)S(1)} %copy-done, s32[1024]{0:T(1024)S(1)} %pad_clamp_fusion), kind=kCustom, calls=%fused_computation | custom fusion | bytes 3072 | tf_op jit(solution)/shard_map/gather | solution.py:116
  12.0 0.8 %copy.8.index_ref = s32[256,1]{1,0:T(8,128)} copy(s32[256,1]{0,1:T(1,128)S(1)} %bitcast.41) | data formatting | bytes 2048 | tf_op jit(solution)/shard_map/broadcast_in_dim | solution.py:119
  12.8 20.0 %all-to-all-done = bf16[16,16,2048]{2,0,1:T(8,128)(2,1)S(1)} async-done(((bf16[16,16,2048]{2,0,1:T(8,128)(2,1)}), bf16[16,16,2048]{2,0,1:T(8,128)(2,1)S(1)}, u32[]{:S(2)}, u32[]{:S(2)}) %all-to-all-start) | async-done | bytes 1048608 | tf_op jit(solution)/shard_map/all_to_all | solution.py:118
  32.8 0.0 copy-start.1
  32.8 1.0 %copy-done.1 = bf16[16,16,2048]{2,0,1:T(8,128)(2,1)} copy-done((bf16[16,16,2048]{2,0,1:T(8,128)(2,1)}, bf16[16,16,2048]{2,0,1:T(8,128)(2,1)S(1)}, u32[]{:S(2)}) %copy-start.1) | copy-done | bytes 1048600
  33.8 7.2 %shard_map.55 = (f32[128,2048]{1,0:T(8,128)}, bf16[128,2048]{1,0:T(8,128)(2,1)}) custom-call(s32[256,1]{1,0:T(8,128)} %copy.8.index_ref, bf16[256,2048]{1,0:T(8,128)(2,1)} %bitcast.35, bf16[2048,2048]{1,0:T(8,128)(2,1)} %chol_ref.1), custom_call_target="tpu_custom_call" | custom-call | flops 2415919104 | bytes 11010048 | tf_op jit(solution)/shard_map/pallas_call | solution.py:48
  41.1 0.0 copy-start.2
  41.1 0.6 collective-permute-start
  41.7 1.7 %collective-permute-done = bf16[128,2048]{1,0:T(8,128)(2,1)S(1)} collective-permute-done((bf16[128,2048]{1,0:T(8,128)(2,1)}, bf16[128,2048]{1,0:T(8,128)(2,1)S(1)}, u32[]{:S(2)}, u32[]{:S(2)}) %collective-permute-start) | collective-permute-done | bytes 524320 | tf_op jit(solution)/shard_map/ppermute | solution.py:24
  43.4 1.4 %fusion.10 = (bf16[128,2048]{1,0:T(8,128)(2,1)S(1)}, f32[128,2048]{1,0:T(8,128)S(1)}) fusion(f32[128,2048]{1,0:T(8,128)} %get-tuple-element.7, bf16[128,2048]{1,0:T(8,128)(2,1)S(1)} %collective-permute-done), kind=kLoop, calls=%fused_computation.35 | loop fusion | flops 786432 | bytes 3145728 | tf_op jit(solution)/shard_map/convert.5
  44.8 4.4 %collective-permute-start.6 = (bf16[1,16,2048]{2,1,0:T(8,128)(2,1)S(1)}, bf16[1,16,2048]{2,1,0:T(8,128)(2,1)S(1)}, u32[]{:S(2)}, u32[]{:S(2)}) collective-permute-start(bf16[1,16,2048]{2,1,0:T(8,128)(2,1)S(1)} %get-tuple-element.12), channel_id=1, source_target_pairs={{0,6},{1,7},{2,4},{3,5},{4,2},{5,3},{6,0},{7,1},{8,14},{9,15},{10,... | collective-permute-start | bytes 196616 | tf_op jit(solution)/shard_map/ppermute | solution.py:24
  49.3 0.0 collective-permute-start.5
  49.3 0.6 collective-permute-start.4
  49.9 0.0 copy-done.3
  49.9 2.9 %collective-permute-start.3 = (bf16[16,2048]{1,0:T(8,128)(2,1)S(1)}, bf16[16,2048]{1,0:T(8,128)(2,1)S(1)}, u32[]{:S(2)}, u32[]{:S(2)}) collective-permute-start(bf16[16,2048]{1,0:T(8,128)(2,1)S(1)} %get-tuple-element.15), channel_id=1, source_target_pairs={{0,6},{1,7},{2,4},{3,5},{4,2},{5,3},{6,0},{7,1},{8,14},{9,15},{10,... | collective-permute-start | bytes 196616 | tf_op jit(solution)/shard_map/ppermute | solution.py:24
  52.9 0.0 collective-permute-start.2
  52.9 0.0 collective-permute-done.6
  52.9 0.6 collective-permute-start.1
  53.5 0.4 collective-permute-done.5
  53.9 0.3 collective-permute-done.4
  54.3 2.6 %collective-permute-start.7 = (bf16[16,2048]{1,0:T(8,128)(2,1)S(1)}, bf16[16,2048]{1,0:T(8,128)(2,1)S(1)}, u32[]{:S(2)}, u32[]{:S(2)}) collective-permute-start(bf16[16,2048]{1,0:T(8,128)(2,1)S(1)} %fusion.6), channel_id=1, source_target_pairs={{0,8},{1,9},{2,10},{3,11},{4,12},{5,13},{6,14},{7,15},{8,0},{9,1},... | collective-permute-start | bytes 196616 | tf_op jit(solution)/shard_map/ppermute | solution.py:24
  56.9 5.6 %fusion.11 = f32[1,2048]{1,0:T(1,128)S(1)} fusion(bf16[2048,2048]{1,0:T(8,128)(2,1)} %chol_ref.1, bf16[2048,1]{0,1:T(2,128)(2,1)S(1)} %reshape.150), kind=kOutput, calls=%fused_computation.36 | convolution fusion | flops 8388608 | bytes 8400896 | tf_op jit(solution)/shard_map/dot_general | solution.py:102
  62.6 0.0 collective-permute-start.8
  62.6 1.2 %collective-permute-done.8 = f32[2048]{0:T(1024)S(1)} collective-permute-done((f32[2048]{0:T(1024)S(1)}, f32[2048]{0:T(1024)S(1)}, u32[]{:S(2)}, u32[]{:S(2)}) %collective-permute-start.8) | collective-permute-done | bytes 8224 | tf_op jit(solution)/shard_map/ppermute | solution.py:24
  63.7 1.1 %collective-permute-start.9 = (f32[2048]{0:T(1024)S(1)}, f32[2048]{0:T(1024)S(1)}, u32[]{:S(2)}, u32[]{:S(2)}) collective-permute-start(f32[2048]{0:T(1024)S(1)} %add.135), channel_id=1, source_target_pairs={{0,2},{1,3},{2,0},{3,1},{4,6},{5,7},{6,4},{7,5},{8,10},{9,11},{10,... | collective-permute-start | bytes 24584 | tf_op jit(solution)/shard_map/ppermute | solution.py:24
  64.9 2.5 %collective-permute-done.9 = f32[2048]{0:T(1024)S(1)} collective-permute-done((f32[2048]{0:T(1024)S(1)}, f32[2048]{0:T(1024)S(1)}, u32[]{:S(2)}, u32[]{:S(2)}) %collective-permute-start.9) | collective-permute-done | bytes 8224 | tf_op jit(solution)/shard_map/ppermute | solution.py:24
  67.4 0.8 %collective-permute-start.10 = (f32[2048]{0:T(1024)S(1)}, f32[2048]{0:T(1024)S(1)}, u32[]{:S(2)}, u32[]{:S(2)}) collective-permute-start(f32[2048]{0:T(1024)S(1)} %add.136), channel_id=1, source_target_pairs={{0,4},{1,5},{2,6},{3,7},{4,0},{5,1},{6,2},{7,3},{8,12},{9,13},{10,... | collective-permute-start | bytes 24584 | tf_op jit(solution)/shard_map/ppermute | solution.py:24
  68.2 2.9 %collective-permute-done.10 = f32[2048]{0:T(1024)S(1)} collective-permute-done((f32[2048]{0:T(1024)S(1)}, f32[2048]{0:T(1024)S(1)}, u32[]{:S(2)}, u32[]{:S(2)}) %collective-permute-start.10) | collective-permute-done | bytes 8224 | tf_op jit(solution)/shard_map/ppermute | solution.py:24
  71.1 0.4 collective-permute-start.11
  71.4 4.2 %collective-permute-done.11 = f32[2048]{0:T(1024)S(1)} collective-permute-done((f32[2048]{0:T(1024)S(1)}, f32[2048]{0:T(1024)S(1)}, u32[]{:S(2)}, u32[]{:S(2)}) %collective-permute-start.11) | collective-permute-done | bytes 8224 | tf_op jit(solution)/shard_map/ppermute | solution.py:24
  75.6 0.0 collective-permute-done.3
  75.6 0.0 collective-permute-done.2
  75.6 0.0 collective-permute-done.1
  75.6 0.0 collective-permute-done.7
  75.6 0.0 copy-done.2
  75.7 0.7 fusion.5
  (10 shorter events, 0.1 us)
Async XLA Ops:
  0.0 10.1 %copy-start = (s32[256]{0:T(256)S(1)}, s32[256]{0:T(256)}, u32[]{:S(2)}) copy-start(s32[256]{0:T(256)} %param.8) | copy-start | bytes 3076
  2.3 47.6 %copy-start.3 = (bf16[2048]{0:T(1024)(128)(2,1)S(1)}, bf16[2048]{0:T(1024)(128)(2,1)}, u32[]{:S(2)}) copy-start(bf16[2048]{0:T(1024)(128)(2,1)} %param.6) | copy-start | bytes 12292
  2.3 30.5 %all-to-all-start = ((bf16[16,16,2048]{2,0,1:T(8,128)(2,1)}), bf16[16,16,2048]{2,0,1:T(8,128)(2,1)S(1)}, u32[]{:S(2)}, u32[]{:S(2)}) async-start(bf16[16,16,2048]{2,0,1:T(8,128)(2,1)} %bitcast.34), calls=%async_computation | async-start | bytes 2097152 | tf_op jit(solution)/shard_map/all_to_all | solution.py:118
  32.8 1.0 %copy-start.1 = (bf16[16,16,2048]{2,0,1:T(8,128)(2,1)}, bf16[16,16,2048]{2,0,1:T(8,128)(2,1)S(1)}, u32[]{:S(2)}) copy-start(bf16[16,16,2048]{2,0,1:T(8,128)(2,1)S(1)} %all-to-all-done) | copy-start | bytes 3145732
  41.1 34.6 %copy-start.2 = (f32[16,2048]{1,0:T(8,128)S(1)}, f32[16,2048]{1,0:T(8,128)}, u32[]{:S(2)}) copy-start(f32[16,2048]{1,0:T(8,128)} %param.9) | copy-start | bytes 393220
  41.1 2.4 %collective-permute-start = (bf16[128,2048]{1,0:T(8,128)(2,1)}, bf16[128,2048]{1,0:T(8,128)(2,1)S(1)}, u32[]{:S(2)}, u32[]{:S(2)}) collective-permute-start(bf16[128,2048]{1,0:T(8,128)(2,1)} %get-tuple-element.8), channel_id=1, source_target_pairs={{0,1},{1,0},{2,3},{3,2},{4,5},{5,4},{6,7},{7,6},{8,9},{9,8},{10,11... | collective-permute-start | bytes 1572872 | tf_op jit(solution)/shard_map/ppermute | solution.py:24
  44.8 8.0 %collective-permute-start.6 = (bf16[1,16,2048]{2,1,0:T(8,128)(2,1)S(1)}, bf16[1,16,2048]{2,1,0:T(8,128)(2,1)S(1)}, u32[]{:S(2)}, u32[]{:S(2)}) collective-permute-start(bf16[1,16,2048]{2,1,0:T(8,128)(2,1)S(1)} %get-tuple-element.12), channel_id=1, source_target_pairs={{0,6},{1,7},{2,4},{3,5},{4,2},{5,3},{6,0},{7,1},{8,14},{9,15},{10,... | collective-permute-start | bytes 196616 | tf_op jit(solution)/shard_map/ppermute | solution.py:24
  49.3 4.7 %collective-permute-start.5 = (bf16[1,16,2048]{2,1,0:T(8,128)(2,1)S(1)}, bf16[1,16,2048]{2,1,0:T(8,128)(2,1)S(1)}, u32[]{:S(2)}, u32[]{:S(2)}) collective-permute-start(bf16[1,16,2048]{2,1,0:T(8,128)(2,1)S(1)} %get-tuple-element.13), channel_id=1, source_target_pairs={{0,4},{1,5},{2,6},{3,7},{4,0},{5,1},{6,2},{7,3},{8,12},{9,13},{10,... | collective-permute-start | bytes 196616 | tf_op jit(solution)/shard_map/ppermute | solution.py:24
  49.3 5.0 %collective-permute-start.4 = (bf16[1,16,2048]{2,1,0:T(8,128)(2,1)S(1)}, bf16[1,16,2048]{2,1,0:T(8,128)(2,1)S(1)}, u32[]{:S(2)}, u32[]{:S(2)}) collective-permute-start(bf16[1,16,2048]{2,1,0:T(8,128)(2,1)S(1)} %get-tuple-element.14), channel_id=1, source_target_pairs={{0,2},{1,3},{2,0},{3,1},{4,6},{5,7},{6,4},{7,5},{8,10},{9,11},{10,... | collective-permute-start | bytes 196616 | tf_op jit(solution)/shard_map/ppermute | solution.py:24
  49.9 25.7 %collective-permute-start.3 = (bf16[16,2048]{1,0:T(8,128)(2,1)S(1)}, bf16[16,2048]{1,0:T(8,128)(2,1)S(1)}, u32[]{:S(2)}, u32[]{:S(2)}) collective-permute-start(bf16[16,2048]{1,0:T(8,128)(2,1)S(1)} %get-tuple-element.15), channel_id=1, source_target_pairs={{0,6},{1,7},{2,4},{3,5},{4,2},{5,3},{6,0},{7,1},{8,14},{9,15},{10,... | collective-permute-start | bytes 196616 | tf_op jit(solution)/shard_map/ppermute | solution.py:24
  52.9 22.8 %collective-permute-start.2 = (bf16[16,2048]{1,0:T(8,128)(2,1)S(1)}, bf16[16,2048]{1,0:T(8,128)(2,1)S(1)}, u32[]{:S(2)}, u32[]{:S(2)}) collective-permute-start(bf16[16,2048]{1,0:T(8,128)(2,1)S(1)} %get-tuple-element.16), channel_id=1, source_target_pairs={{0,4},{1,5},{2,6},{3,7},{4,0},{5,1},{6,2},{7,3},{8,12},{9,13},{10,... | collective-permute-start | bytes 196616 | tf_op jit(solution)/shard_map/ppermute | solution.py:24
  52.9 22.8 %collective-permute-start.1 = (bf16[16,2048]{1,0:T(8,128)(2,1)S(1)}, bf16[16,2048]{1,0:T(8,128)(2,1)S(1)}, u32[]{:S(2)}, u32[]{:S(2)}) collective-permute-start(bf16[16,2048]{1,0:T(8,128)(2,1)S(1)} %get-tuple-element.11), channel_id=1, source_target_pairs={{0,2},{1,3},{2,0},{3,1},{4,6},{5,7},{6,4},{7,5},{8,10},{9,11},{10,... | collective-permute-start | bytes 196616 | tf_op jit(solution)/shard_map/ppermute | solution.py:24
  54.3 21.3 %collective-permute-start.7 = (bf16[16,2048]{1,0:T(8,128)(2,1)S(1)}, bf16[16,2048]{1,0:T(8,128)(2,1)S(1)}, u32[]{:S(2)}, u32[]{:S(2)}) collective-permute-start(bf16[16,2048]{1,0:T(8,128)(2,1)S(1)} %fusion.6), channel_id=1, source_target_pairs={{0,8},{1,9},{2,10},{3,11},{4,12},{5,13},{6,14},{7,15},{8,0},{9,1},... | collective-permute-start | bytes 196616 | tf_op jit(solution)/shard_map/ppermute | solution.py:24
  62.6 1.2 %collective-permute-start.8 = (f32[2048]{0:T(1024)S(1)}, f32[2048]{0:T(1024)S(1)}, u32[]{:S(2)}, u32[]{:S(2)}) collective-permute-start(f32[2048]{0:T(1024)S(1)} %bitcast.38), channel_id=1, source_target_pairs={{0,1},{1,0},{2,3},{3,2},{4,5},{5,4},{6,7},{7,6},{8,9},{9,8},{10,11... | collective-permute-start | bytes 24584 | tf_op jit(solution)/shard_map/ppermute | solution.py:24
  63.7 3.7 %collective-permute-start.9 = (f32[2048]{0:T(1024)S(1)}, f32[2048]{0:T(1024)S(1)}, u32[]{:S(2)}, u32[]{:S(2)}) collective-permute-start(f32[2048]{0:T(1024)S(1)} %add.135), channel_id=1, source_target_pairs={{0,2},{1,3},{2,0},{3,1},{4,6},{5,7},{6,4},{7,5},{8,10},{9,11},{10,... | collective-permute-start | bytes 24584 | tf_op jit(solution)/shard_map/ppermute | solution.py:24
  67.4 3.7 %collective-permute-start.10 = (f32[2048]{0:T(1024)S(1)}, f32[2048]{0:T(1024)S(1)}, u32[]{:S(2)}, u32[]{:S(2)}) collective-permute-start(f32[2048]{0:T(1024)S(1)} %add.136), channel_id=1, source_target_pairs={{0,4},{1,5},{2,6},{3,7},{4,0},{5,1},{6,2},{7,3},{8,12},{9,13},{10,... | collective-permute-start | bytes 24584 | tf_op jit(solution)/shard_map/ppermute | solution.py:24
  71.1 4.5 %collective-permute-start.11 = (f32[2048]{0:T(1024)S(1)}, f32[2048]{0:T(1024)S(1)}, u32[]{:S(2)}, u32[]{:S(2)}) collective-permute-start(f32[2048]{0:T(1024)S(1)} %add.137), channel_id=1, source_target_pairs={{0,8},{1,9},{2,10},{3,11},{4,12},{5,13},{6,14},{7,15},{8,0},{9,1},... | collective-permute-start | bytes 24584 | tf_op jit(solution)/shard_map/ppermute | solution.py:24

commit v2 on v1

v2 whole, which is shorter than its diff:
```python
import functools

import jax
import jax.numpy as jnp
from jax import lax
from jax.experimental import pallas as pl
from jax.experimental.pallas import tpu as pltpu
from jax.sharding import PartitionSpec as P

F32, F16, BF16 = jnp.float32, jnp.float16, jnp.bfloat16
DIRECT_CHIPS = 8


def stage_radices(chips):
    radices = []
    while chips > 1:
        radix = 4 if chips % 4 == 0 else 2
        radices.append(radix)
        chips //= radix
    return radices


def swap(x, mask, n):
    return lax.ppermute(x, "chol", [(i, i ^ mask) for i in range(n)])


def split_kernel(greens_ref, *refs):
    outs, sems = refs[:-1], refs[-1]
    me = lax.axis_index("chol")
    own, pairs = outs[0].shape[0] // 2, outs[0].shape[1]
    copies = []
    for m in reversed(range(len(outs))):
        for j in range(2):
            there = jnp.bitwise_xor(me, 2 * m + j)
            copy = pltpu.make_async_copy(
                greens_ref.at[:, pl.ds(pl.multiple_of(there * pairs, pairs), pairs)],
                outs[m].at[pl.ds(j * own, own)],
                sems.at[m, j],
            )
            copy.start()
            copies.append(copy)
    for copy in copies:
        copy.wait()


def split_by_chip(greens, chips):
    own, total = greens.shape
    shape = (2 * own, total // (2 * chips))
    return pl.pallas_call(
        split_kernel,
        in_specs=[pl.BlockSpec(memory_space=pl.ANY)],
        out_specs=[pl.BlockSpec(memory_space=pl.ANY)] * chips,
        out_shape=[jax.ShapeDtypeStruct(shape, greens.dtype)] * chips,
        scratch_shapes=[pltpu.SemaphoreType.DMA((chips, 2))],
        cost_estimate=pl.CostEstimate(flops=0, bytes_accessed=4 * greens.size, transcendentals=0),
    )(greens)


def collect_walkers(greens, chips, n):
    own = greens.shape[0]
    sent = split_by_chip(greens, chips)
    got = {0: sent[0]}
    for m in reversed(range(1, chips)):
        got[m] = swap(sent[m], 2 * m, n)
    near, far = range(chips // 2), range(chips // 2, chips)
    passed = [
        swap(jnp.concatenate([got[m][own:] for m in part]), 1, n) for part in (near, far)
    ]
    return jnp.concatenate([got[m][:own] for m in range(chips)] + passed)


def bias_kernel(tile, index_ref, rows_ref, chol_ref, mean_ref, noise_ref, keep_ref, send_ref, base_ref, picked):
    half, nchol = keep_ref.shape
    walkers = rows_ref.shape[0]
    chosen = index_ref[...] == lax.broadcasted_iota(jnp.int32, (2 * half, walkers), 1)
    picked[...] = jnp.dot(
        chosen.astype(BF16), rows_ref[...], preferred_element_type=F32
    ).astype(BF16)
    base_ref[...] = noise_ref[...] + mean_ref[...]

    @pl.loop(0, nchol // tile)
    def _(t):
        at = pl.ds(pl.multiple_of(t * tile, tile), tile)
        part = lax.dot_general(
            picked[...], chol_ref[at, :], (((1,), (1,)), ((), ())), preferred_element_type=F32
        )
        keep_ref[:, at] = part[:half]
        send_ref[:, at] = part[half:].astype(BF16)


def partial_bias(index, rows, chol, mean_field, noise, tile):
    slots, (nchol, pairs) = index.shape[0], chol.shape
    half = slots // 2
    return pl.pallas_call(
        functools.partial(bias_kernel, tile),
        in_specs=[pl.BlockSpec(memory_space=pltpu.VMEM)] * 5,
        out_specs=[pl.BlockSpec(memory_space=pltpu.VMEM)] * 3,
        out_shape=[
            jax.ShapeDtypeStruct((half, nchol), F32),
            jax.ShapeDtypeStruct((half, nchol), BF16),
            jax.ShapeDtypeStruct(noise.shape, F32),
        ],
        scratch_shapes=[pltpu.VMEM((slots, pairs), BF16)],
        compiler_params=pltpu.CompilerParams(vmem_limit_bytes=28 * 2**20),
        cost_estimate=pl.CostEstimate(
            flops=2 * slots * pairs * (nchol + rows.shape[0]),
            bytes_accessed=2 * nchol * pairs + 2 * rows.size + 6 * half * nchol,
            transcendentals=0,
        ),
    )(index, rows, chol, mean_field, noise)


def reduce_over_chips(held, radices, bit, n):
    if not radices:
        return held
    radix, rest = radices[0], radices[1:]
    later = 1
    for r in rest:
        later *= r
    rows, g = held.shape[-2:]
    held = held.reshape(radix, later, rows, g)
    shift = radix.bit_length() - 1
    total = held[0]
    if later > 1:
        onward = total[1:] + sum(
            swap(held[m, 1:].astype(F16), m << bit, n).astype(F32) for m in range(1, radix)
        )
    mine = total[0] + sum(
        swap(held[m, 0].astype(F16), m << bit, n).astype(F32) for m in range(1, radix)
    )
    if later == 1:
        return mine
    return reduce_over_chips(
        jnp.concatenate([mine[None], onward], axis=0), rest, bit + shift, n
    )


def per_device(n, chol_vectors, mean_greens, greens, walker_order, noise_field):
    me = lax.axis_index("chol")
    own = greens.shape[0]
    chips = n // 2
    radices = stage_radices(chips)

    mean_field = jnp.dot(chol_vectors, mean_greens, preferred_element_type=F32)
    for bit in range(n.bit_length() - 1):
        mean_field = mean_field + swap(mean_field, 1 << bit, n)

    place = jnp.arange(n, dtype=jnp.int32)
    relative, weight, left = place // chips, 2, place % chips
    for stage, radix in enumerate(radices):
        later = 1
        for r in radices[stage + 1 :]:
            later *= r
        relative = relative + weight * (left // later)
        left, weight = left % later, weight * radix
    owners = jnp.bitwise_xor(relative, me)
    index = walker_order.reshape(n, own)[owners].reshape(-1)

    if chips <= DIRECT_CHIPS:
        rows = collect_walkers(greens, chips, n)
        source = jnp.bitwise_xor(index // own, me)
        index = ((source % 2) * chips + source // 2) * own + index % own
    else:
        rows = lax.all_to_all(greens, "chol", split_axis=1, concat_axis=0, tiled=True)
    keep, send, base = partial_bias(
        index[:, None], rows, chol_vectors, mean_field[None, :], noise_field, 512
    )
    held = keep + swap(send, 1, n).astype(F32)
    raw_bias = reduce_over_chips(held.reshape(chips, own, -1), radices, 1, n).reshape(own, -1)
    return base - jnp.tanh(raw_bias)


def solution(mesh):
    placed = (
        P(None, "chol"),
        P("chol"),
        P(("grp", "chol"), None),
        P("grp"),
        P(("grp", "chol"), None),
    )
    return jax.shard_map(
        functools.partial(per_device, mesh.shape["chol"]),
        mesh=mesh,
        in_specs=placed,
        out_specs=P(("grp", "chol"), None),
        check_vma=False,
    )
```

time: 76.7 us -> 99.8 us (1.30)
  Pallas kernels: 7.25 us -> 36.4 us
  waiting for transfers between devices: 33.3 us -> 26.3 us
  starting transfers between devices: 21.6 us -> 24.7 us
  local copies, waits for them, and re-layouts: 6.21 us -> 5.04 us
  other arithmetic: 2.25 us -> 1.23 us
    pallas_call x1 -> x2, Pallas kernels: 7.25 us -> 36.4 us  [the longest x1 33 us: split_by_chip(): pl.pallas_call(split_kernel, in_specs=[pl.BlockSpec(memory_space=pl.ANY)]...]
    all_to_all x1 -> x0, waiting for transfers between devices: 20 us -> none  [per_device(): lax.all_to_all(greens, 'chol', split_axis=1, concat_axis=0, tiled=True)]
    ppermute x12 -> x21, waiting for transfers between devices: 13.3 us -> 26.3 us  [swap(): return lax.ppermute(x, 'chol', [(i, i ^ mask) for i in range(n)])]
    ppermute x12 -> x21, starting transfers between devices: 14.1 us -> 24.7 us  [swap(): return lax.ppermute(x, 'chol', [(i, i ^ mask) for i in range(n)])]
    all_to_all x1 -> x0, starting transfers between devices: 7.52 us -> none  [per_device(): lax.all_to_all(greens, 'chol', split_axis=1, concat_axis=0, tiled=True)]
    unnamed x9 -> x16, local copies, waits for them, and re-layouts: 1.01 us -> 4.11 us
    all_to_all x1 -> x0, local copies, waits for them, and re-layouts: 2.34 us -> none  [per_device(): lax.all_to_all(greens, 'chol', split_axis=1, concat_axis=0, tiled=True)]
    gather x1, local copies, waits for them, and re-layouts: 1.95 us -> 0.57 us  [per_device(): index = walker_order.reshape(n, own)[owners].reshape(-1)]
  transfers between devices with their start and end apart: 13 -> 21, of which waited for: 8 -> 10; matrix products, arithmetic and copies ran while one was open for 11% -> 8% of each run, Pallas kernels for 0% -> 0%
where the time goes in v2:
time: 99.8 us; the launch traced here: 99.6 us
  Pallas kernels  36.4 us (36%)
  waiting for transfers between devices  26.3 us (26%)
  starting transfers between devices  24.7 us (25%)
  matrix products  5.64 us (6%)
  local copies, waits for them, and re-layouts  5.04 us (5%)
  other arithmetic  1.23 us (1%)
    pallas_call x1, Pallas kernels, split_by_chip(): pl.pallas_call(split_kernel, in_specs=[pl.BlockSpec(memory_space=pl.ANY)]...  33 us
    ppermute x21, waiting for transfers between devices, swap(): return lax.ppermute(x, 'chol', [(i, i ^ mask) for i in range(n)])  26.3 us
    ppermute x21, starting transfers between devices, swap(): return lax.ppermute(x, 'chol', [(i, i ^ mask) for i in range(n)])  24.7 us
    dot_general x1, matrix products, per_device(): mean_field = jnp.dot(chol_vectors, mean_greens, preferred_element_type=F32)  5.64 us
    unnamed x16, local copies, waits for them, and re-layouts  4.11 us
    pallas_call x1, Pallas kernels, partial_bias(): pl.pallas_call(functools.partial(bias_kernel, tile), in_specs=[pl.BlockSp...  3.44 us
  transfers between devices with their start and end apart: 21, of which 10 were waited for; matrix products, arithmetic and copies ran while one was open for 8% of the time, Pallas kernels for 0%

profile of v2, /device:TPU:0, one launch (start us, length us, event | category | flops | bytes accessed | tf_op | source)
XLA Modules:
  0.0 99.6 jit_solution(16377712853577295945)
XLA Ops:
  0.0 33.0 %shard_map.55 = (bf16[32,2048]{1,0:T(8,128)(2,1)}, bf16[32,2048]{1,0:T(8,128)(2,1)}, bf16[32,2048]{1,0:T(8,128)(2,1)}, bf16[32,2048]{1,0:T(8,128)(2,1)}, bf16[32...) custom-call(bf16[16,32768]{1,0:T(8,128)(2,1)} %greens_ref.1), custom_call_target="tpu_custom_call" | custom-call | bytes 2097152 | tf_op jit(solution)/shard_map/pallas_call | solution.py:49
  33.0 0.0 copy-start.2
  33.0 0.0 copy-start.6
  33.0 0.0 copy-start.5
  33.1 0.0 copy-start.4
  33.1 3.0 %collective-permute-start = (bf16[32,2048]{1,0:T(8,128)(2,1)}, bf16[32,2048]{1,0:T(8,128)(2,1)S(1)}, u32[]{:S(2)}, u32[]{:S(2)}) collective-permute-start(bf16[32,2048]{1,0:T(8,128)(2,1)} %get-tuple-element.17), channel_id=1, source_target_pairs={{0,2},{1,3},{2,0},{3,1},{4,6},{5,7},{6,4},{7,5},{8,10},{9,11},{10,... | collective-permute-start | bytes 393224 | tf_op jit(solution)/shard_map/ppermute | solution.py:24
  36.1 1.6 %collective-permute-start.1 = (bf16[32,2048]{1,0:T(8,128)(2,1)}, bf16[32,2048]{1,0:T(8,128)(2,1)S(1)}, u32[]{:S(2)}, u32[]{:S(2)}) collective-permute-start(bf16[32,2048]{1,0:T(8,128)(2,1)} %get-tuple-element.18), channel_id=1, source_target_pairs={{0,4},{1,5},{2,6},{3,7},{4,0},{5,1},{6,2},{7,3},{8,12},{9,13},{10,... | collective-permute-start | bytes 393224 | tf_op jit(solution)/shard_map/ppermute | solution.py:24
  37.7 0.0 collective-permute-start.2
  37.7 3.0 %collective-permute-start.3 = (bf16[32,2048]{1,0:T(8,128)(2,1)}, bf16[32,2048]{1,0:T(8,128)(2,1)S(1)}, u32[]{:S(2)}, u32[]{:S(2)}) collective-permute-start(bf16[32,2048]{1,0:T(8,128)(2,1)} %get-tuple-element.20), channel_id=1, source_target_pairs={{0,8},{1,9},{2,10},{3,11},{4,12},{5,13},{6,14},{7,15},{8,0},{9,1},... | collective-permute-start | bytes 393224 | tf_op jit(solution)/shard_map/ppermute | solution.py:24
  40.7 0.7 reshape.382
  41.3 5.6 %fusion.30 = f32[1,2048]{1,0:T(1,128)S(1)} fusion(bf16[2048,2048]{1,0:T(8,128)(2,1)} %chol_ref.1, bf16[2048,1]{0,1:T(2,128)(2,1)S(1)} %reshape.382), kind=kOutput, calls=%fused_computation.76 | convolution fusion | flops 8388608 | bytes 8400896 | tf_op jit(solution)/shard_map/dot_general | solution.py:144
  47.0 0.0 collective-permute-start.9
  47.0 0.0 copy-done.2
  47.0 1.1 %collective-permute-done.9 = f32[2048]{0:T(1024)S(1)} collective-permute-done((f32[2048]{0:T(1024)S(1)}, f32[2048]{0:T(1024)S(1)}, u32[]{:S(2)}, u32[]{:S(2)}) %collective-permute-start.9) | collective-permute-done | bytes 8224 | tf_op jit(solution)/shard_map/ppermute | solution.py:24
  48.2 1.5 %collective-permute-start.10 = (f32[2048]{0:T(1024)S(1)}, f32[2048]{0:T(1024)S(1)}, u32[]{:S(2)}, u32[]{:S(2)}) collective-permute-start(f32[2048]{0:T(1024)S(1)} %add.177), channel_id=1, source_target_pairs={{0,2},{1,3},{2,0},{3,1},{4,6},{5,7},{6,4},{7,5},{8,10},{9,11},{10,... | collective-permute-start | bytes 24584 | tf_op jit(solution)/shard_map/ppermute | solution.py:24
  49.7 2.1 %collective-permute-done.10 = f32[2048]{0:T(1024)S(1)} collective-permute-done((f32[2048]{0:T(1024)S(1)}, f32[2048]{0:T(1024)S(1)}, u32[]{:S(2)}, u32[]{:S(2)}) %collective-permute-start.10) | collective-permute-done | bytes 8224 | tf_op jit(solution)/shard_map/ppermute | solution.py:24
  51.8 1.6 %collective-permute-start.11 = (f32[2048]{0:T(1024)S(1)}, f32[2048]{0:T(1024)S(1)}, u32[]{:S(2)}, u32[]{:S(2)}) collective-permute-start(f32[2048]{0:T(1024)S(1)} %add.178), channel_id=1, source_target_pairs={{0,4},{1,5},{2,6},{3,7},{4,0},{5,1},{6,2},{7,3},{8,12},{9,13},{10,... | collective-permute-start | bytes 24584 | tf_op jit(solution)/shard_map/ppermute | solution.py:24
  53.4 0.0 copy-done.3
  53.4 0.1 reshape.371
  53.5 0.6 gather_fusion
  54.1 0.1 reshape.384
  54.2 1.3 %collective-permute-done.11 = f32[2048]{0:T(1024)S(1)} collective-permute-done((f32[2048]{0:T(1024)S(1)}, f32[2048]{0:T(1024)S(1)}, u32[]{:S(2)}, u32[]{:S(2)}) %collective-permute-start.11) | collective-permute-done | bytes 8224 | tf_op jit(solution)/shard_map/ppermute | solution.py:24
  55.5 0.0 copy-done.6
  55.5 1.3 %collective-permute-start.4 = (bf16[32,2048]{1,0:T(8,128)(2,1)S(1)}, bf16[32,2048]{1,0:T(8,128)(2,1)S(1)}, u32[]{:S(2)}, u32[]{:S(2)}) collective-permute-start(bf16[32,2048]{1,0:T(8,128)(2,1)S(1)} %copy-done.6), channel_id=1, source_target_pairs={{0,10},{1,11},{2,8},{3,9},{4,14},{5,15},{6,12},{7,13},{8,2},{9,3},... | collective-permute-start | bytes 393224 | tf_op jit(solution)/shard_map/ppermute | solution.py:24
  56.8 0.0 collective-permute-done
  56.8 0.0 copy-done.5
  56.8 3.7 %collective-permute-start.5 = (bf16[32,2048]{1,0:T(8,128)(2,1)S(1)}, bf16[32,2048]{1,0:T(8,128)(2,1)S(1)}, u32[]{:S(2)}, u32[]{:S(2)}) collective-permute-start(bf16[32,2048]{1,0:T(8,128)(2,1)S(1)} %copy-done.5), channel_id=1, source_target_pairs={{0,12},{1,13},{2,14},{3,15},{4,8},{5,9},{6,10},{7,11},{8,4},{9,5},... | collective-permute-start | bytes 393224 | tf_op jit(solution)/shard_map/ppermute | solution.py:24
  60.5 0.0 collective-permute-done.1
  60.5 0.0 copy-done.4
  60.5 0.1 collective-permute-start.6
  60.6 0.0 collective-permute-done.2
  60.6 1.0 collective-permute-start.12
  61.6 0.0 collective-permute-done.3
  61.7 0.1 collective-permute-start.7
  61.8 8.6 %collective-permute-done.4 = bf16[32,2048]{1,0:T(8,128)(2,1)S(1)} collective-permute-done((bf16[32,2048]{1,0:T(8,128)(2,1)S(1)}, bf16[32,2048]{1,0:T(8,128)(2,1)S(1)}, u32[]{:S(2)}, u32[]{:S(2)}) %collective-permute-start.4) | collective-permute-done | bytes 131104 | tf_op jit(solution)/shard_map/ppermute | solution.py:24
  70.3 0.0 collective-permute-done.5
  70.4 0.0 collective-permute-done.6
  70.4 0.1 collective-permute-start.8
  70.5 0.2 fusion.4.index_ref
  70.8 4.2 %collective-permute-done.12 = f32[2048]{0:T(1024)S(1)} collective-permute-done((f32[2048]{0:T(1024)S(1)}, f32[2048]{0:T(1024)S(1)}, u32[]{:S(2)}, u32[]{:S(2)}) %collective-permute-start.12) | collective-permute-done | bytes 8224 | tf_op jit(solution)/shard_map/ppermute | solution.py:24
  75.0 0.0 collective-permute-done.7
  75.0 0.0 collective-permute-done.8
  75.1 0.0 copy-start
  75.1 3.4 %copy-done = bf16[2048,2048]{1,0:T(8,128)(2,1)S(1)} copy-done((bf16[2048,2048]{1,0:T(8,128)(2,1)S(1)}, bf16[2048,2048]{1,0:T(8,128)(2,1)}, u32[]{:S(2)}) %copy-start) | copy-done | bytes 8388632
  78.5 3.4 %shard_map.56 = (f32[128,2048]{1,0:T(8,128)S(1)}, bf16[128,2048]{1,0:T(8,128)(2,1)S(1)}, f32[16,2048]{1,0:T(8,128)S(1)}) custom-call(s32[256,1]{1,0:T(8,128)S(1)} %fusion.4.index_ref, bf16[256,2048]{1,0:T(8,128)(2,1)S(1)} %constant_dynamic-update-slice_fusion.rows_ref, bf16[2048,2048]{1,0:T(8,128)(2,1)S(1)} %copy-done, f32[1,2048]{1,0:T(1,128)S(1)} %bitcast.29, ...), custom_call_target="tpu_custom_call" | custom-call | flops 2415919104 | bytes 11010048 | tf_op jit(solution)/shard_map/pallas_call | solution.py:94
  81.9 0.1 collective-permute-start.13
  82.0 1.9 %collective-permute-done.13 = bf16[128,2048]{1,0:T(8,128)(2,1)S(1)} collective-permute-done((bf16[128,2048]{1,0:T(8,128)(2,1)S(1)}, bf16[128,2048]{1,0:T(8,128)(2,1)S(1)}, u32[]{:S(2)}, u32[]{:S(2)}) %collective-permute-start.13) | collective-permute-done | bytes 524320 | tf_op jit(solution)/shard_map/ppermute | solution.py:24
  83.9 0.2 fusion.21
  84.1 0.1 slice_bitcast_fusion.6
  84.1 0.6 collective-permute-start.17
  84.7 3.0 %collective-permute-start.18 = (f16[1,16,2048]{2,1,0:T(8,128)(2,1)S(1)}, f16[1,16,2048]{2,1,0:T(8,128)(2,1)S(1)}, u32[]{:S(2)}, u32[]{:S(2)}) collective-permute-start(f16[1,16,2048]{2,1,0:T(8,128)(2,1)S(1)} %get-tuple-element.31), channel_id=1, source_target_pairs={{0,4},{1,5},{2,6},{3,7},{4,0},{5,1},{6,2},{7,3},{8,12},{9,13},{10,... | collective-permute-start | bytes 196616 | tf_op jit(solution)/shard_map/ppermute | solution.py:24
  87.7 0.0 collective-permute-start.19
  87.7 1.5 %collective-permute-start.14 = (f16[16,2048]{1,0:T(8,128)(2,1)S(1)}, f16[16,2048]{1,0:T(8,128)(2,1)S(1)}, u32[]{:S(2)}, u32[]{:S(2)}) collective-permute-start(f16[16,2048]{1,0:T(8,128)(2,1)S(1)} %get-tuple-element.29), channel_id=1, source_target_pairs={{0,2},{1,3},{2,0},{3,1},{4,6},{5,7},{6,4},{7,5},{8,10},{9,11},{10,... | collective-permute-start | bytes 196616 | tf_op jit(solution)/shard_map/ppermute | solution.py:24
  89.2 2.0 %collective-permute-start.15 = (f16[16,2048]{1,0:T(8,128)(2,1)S(1)}, f16[16,2048]{1,0:T(8,128)(2,1)S(1)}, u32[]{:S(2)}, u32[]{:S(2)}) collective-permute-start(f16[16,2048]{1,0:T(8,128)(2,1)S(1)} %get-tuple-element.34), channel_id=1, source_target_pairs={{0,4},{1,5},{2,6},{3,7},{4,0},{5,1},{6,2},{7,3},{8,12},{9,13},{10,... | collective-permute-start | bytes 196616 | tf_op jit(solution)/shard_map/ppermute | solution.py:24
  91.2 0.0 collective-permute-done.17
  91.2 0.2 collective-permute-start.16
  91.4 0.0 collective-permute-done.18
  91.4 1.5 %collective-permute-done.19 = f16[1,16,2048]{2,1,0:T(8,128)(2,1)S(1)} collective-permute-done((f16[1,16,2048]{2,1,0:T(8,128)(2,1)S(1)}, f16[1,16,2048]{2,1,0:T(8,128)(2,1)S(1)}, u32[]{:S(2)}, u32[]{:S(2)}) %collective-permute-start.19) | collective-permute-done | bytes 65568 | tf_op jit(solution)/shard_map/ppermute | solution.py:24
  93.0 0.5 collective-permute-start.20
  93.4 0.0 collective-permute-done.14
  93.4 0.5 collective-permute-done.15
  93.9 2.6 %collective-permute-done.16 = f16[16,2048]{1,0:T(8,128)(2,1)S(1)} collective-permute-done((f16[16,2048]{1,0:T(8,128)(2,1)S(1)}, f16[16,2048]{1,0:T(8,128)(2,1)S(1)}, u32[]{:S(2)}, u32[]{:S(2)}) %collective-permute-start.16) | collective-permute-done | bytes 65568 | tf_op jit(solution)/shard_map/ppermute | solution.py:24
  96.5 2.4 %collective-permute-done.20 = f16[16,2048]{1,0:T(8,128)(2,1)S(1)} collective-permute-done((f16[16,2048]{1,0:T(8,128)(2,1)S(1)}, f16[16,2048]{1,0:T(8,128)(2,1)S(1)}, u32[]{:S(2)}, u32[]{:S(2)}) %collective-permute-start.20) | collective-permute-done | bytes 65568 | tf_op jit(solution)/shard_map/ppermute | solution.py:24
  98.9 0.7 fusion.9
  (22 shorter events, 0.2 us)
Async XLA Ops:
  0.0 53.4 %copy-start.3 = (s32[256]{0:T(256)S(1)}, s32[256]{0:T(256)}, u32[]{:S(2)}) copy-start(s32[256]{0:T(256)} %param.8) | copy-start | bytes 3076
  0.0 75.1 %copy-start.1 = (f32[16,2048]{1,0:T(8,128)S(1)}, f32[16,2048]{1,0:T(8,128)}, u32[]{:S(2)}) copy-start(f32[16,2048]{1,0:T(8,128)} %noise_ref.1) | copy-start | bytes 393220
  33.0 14.0 %copy-start.2 = (bf16[32,2048]{1,0:T(8,128)(2,1)S(1)}, bf16[32,2048]{1,0:T(8,128)(2,1)}, u32[]{:S(2)}) copy-start(bf16[32,2048]{1,0:T(8,128)(2,1)} %get-tuple-element.16) | copy-start | bytes 393220
  33.0 22.5 %copy-start.6 = (bf16[32,2048]{1,0:T(8,128)(2,1)S(1)}, bf16[32,2048]{1,0:T(8,128)(2,1)}, u32[]{:S(2)}) copy-start(bf16[32,2048]{1,0:T(8,128)(2,1)} %get-tuple-element.21) | copy-start | bytes 393220
  33.0 23.7 %copy-start.5 = (bf16[32,2048]{1,0:T(8,128)(2,1)S(1)}, bf16[32,2048]{1,0:T(8,128)(2,1)}, u32[]{:S(2)}) copy-start(bf16[32,2048]{1,0:T(8,128)(2,1)} %get-tuple-element.22) | copy-start | bytes 393220
  33.1 27.5 %copy-start.4 = (bf16[32,2048]{1,0:T(8,128)(2,1)S(1)}, bf16[32,2048]{1,0:T(8,128)(2,1)}, u32[]{:S(2)}) copy-start(bf16[32,2048]{1,0:T(8,128)(2,1)} %get-tuple-element.23) | copy-start | bytes 393220
  33.1 23.7 %collective-permute-start = (bf16[32,2048]{1,0:T(8,128)(2,1)}, bf16[32,2048]{1,0:T(8,128)(2,1)S(1)}, u32[]{:S(2)}, u32[]{:S(2)}) collective-permute-start(bf16[32,2048]{1,0:T(8,128)(2,1)} %get-tuple-element.17), channel_id=1, source_target_pairs={{0,2},{1,3},{2,0},{3,1},{4,6},{5,7},{6,4},{7,5},{8,10},{9,11},{10,... | collective-permute-start | bytes 393224 | tf_op jit(solution)/shard_map/ppermute | solution.py:24
  36.1 24.4 %collective-permute-start.1 = (bf16[32,2048]{1,0:T(8,128)(2,1)}, bf16[32,2048]{1,0:T(8,128)(2,1)S(1)}, u32[]{:S(2)}, u32[]{:S(2)}) collective-permute-start(bf16[32,2048]{1,0:T(8,128)(2,1)} %get-tuple-element.18), channel_id=1, source_target_pairs={{0,4},{1,5},{2,6},{3,7},{4,0},{5,1},{6,2},{7,3},{8,12},{9,13},{10,... | collective-permute-start | bytes 393224 | tf_op jit(solution)/shard_map/ppermute | solution.py:24
  37.7 23.0 %collective-permute-start.2 = (bf16[32,2048]{1,0:T(8,128)(2,1)}, bf16[32,2048]{1,0:T(8,128)(2,1)S(1)}, u32[]{:S(2)}, u32[]{:S(2)}) collective-permute-start(bf16[32,2048]{1,0:T(8,128)(2,1)} %get-tuple-element.19), channel_id=1, source_target_pairs={{0,6},{1,7},{2,4},{3,5},{4,2},{5,3},{6,0},{7,1},{8,14},{9,15},{10,... | collective-permute-start | bytes 393224 | tf_op jit(solution)/shard_map/ppermute | solution.py:24
  37.7 24.0 %collective-permute-start.3 = (bf16[32,2048]{1,0:T(8,128)(2,1)}, bf16[32,2048]{1,0:T(8,128)(2,1)S(1)}, u32[]{:S(2)}, u32[]{:S(2)}) collective-permute-start(bf16[32,2048]{1,0:T(8,128)(2,1)} %get-tuple-element.20), channel_id=1, source_target_pairs={{0,8},{1,9},{2,10},{3,11},{4,12},{5,13},{6,14},{7,15},{8,0},{9,1},... | collective-permute-start | bytes 393224 | tf_op jit(solution)/shard_map/ppermute | solution.py:24
  47.0 1.2 %collective-permute-start.9 = (f32[2048]{0:T(1024)S(1)}, f32[2048]{0:T(1024)S(1)}, u32[]{:S(2)}, u32[]{:S(2)}) collective-permute-start(f32[2048]{0:T(1024)S(1)} %bitcast.31), channel_id=1, source_target_pairs={{0,1},{1,0},{2,3},{3,2},{4,5},{5,4},{6,7},{7,6},{8,9},{9,8},{10,11... | collective-permute-start | bytes 24584 | tf_op jit(solution)/shard_map/ppermute | solution.py:24
  48.2 3.7 %collective-permute-start.10 = (f32[2048]{0:T(1024)S(1)}, f32[2048]{0:T(1024)S(1)}, u32[]{:S(2)}, u32[]{:S(2)}) collective-permute-start(f32[2048]{0:T(1024)S(1)} %add.177), channel_id=1, source_target_pairs={{0,2},{1,3},{2,0},{3,1},{4,6},{5,7},{6,4},{7,5},{8,10},{9,11},{10,... | collective-permute-start | bytes 24584 | tf_op jit(solution)/shard_map/ppermute | solution.py:24
  51.8 3.7 %collective-permute-start.11 = (f32[2048]{0:T(1024)S(1)}, f32[2048]{0:T(1024)S(1)}, u32[]{:S(2)}, u32[]{:S(2)}) collective-permute-start(f32[2048]{0:T(1024)S(1)} %add.178), channel_id=1, source_target_pairs={{0,4},{1,5},{2,6},{3,7},{4,0},{5,1},{6,2},{7,3},{8,12},{9,13},{10,... | collective-permute-start | bytes 24584 | tf_op jit(solution)/shard_map/ppermute | solution.py:24
  55.5 14.8 %collective-permute-start.4 = (bf16[32,2048]{1,0:T(8,128)(2,1)S(1)}, bf16[32,2048]{1,0:T(8,128)(2,1)S(1)}, u32[]{:S(2)}, u32[]{:S(2)}) collective-permute-start(bf16[32,2048]{1,0:T(8,128)(2,1)S(1)} %copy-done.6), channel_id=1, source_target_pairs={{0,10},{1,11},{2,8},{3,9},{4,14},{5,15},{6,12},{7,13},{8,2},{9,3},... | collective-permute-start | bytes 393224 | tf_op jit(solution)/shard_map/ppermute | solution.py:24
  56.8 13.6 %collective-permute-start.5 = (bf16[32,2048]{1,0:T(8,128)(2,1)S(1)}, bf16[32,2048]{1,0:T(8,128)(2,1)S(1)}, u32[]{:S(2)}, u32[]{:S(2)}) collective-permute-start(bf16[32,2048]{1,0:T(8,128)(2,1)S(1)} %copy-done.5), channel_id=1, source_target_pairs={{0,12},{1,13},{2,14},{3,15},{4,8},{5,9},{6,10},{7,11},{8,4},{9,5},... | collective-permute-start | bytes 393224 | tf_op jit(solution)/shard_map/ppermute | solution.py:24
  60.5 9.8 %collective-permute-start.6 = (bf16[32,2048]{1,0:T(8,128)(2,1)S(1)}, bf16[32,2048]{1,0:T(8,128)(2,1)S(1)}, u32[]{:S(2)}, u32[]{:S(2)}) collective-permute-start(bf16[32,2048]{1,0:T(8,128)(2,1)S(1)} %copy-done.4), channel_id=1, source_target_pairs={{0,14},{1,15},{2,12},{3,13},{4,10},{5,11},{6,8},{7,9},{8,6},{9,7},... | collective-permute-start | bytes 393224 | tf_op jit(solution)/shard_map/ppermute | solution.py:24
  60.6 14.4 %collective-permute-start.12 = (f32[2048]{0:T(1024)S(1)}, f32[2048]{0:T(1024)S(1)}, u32[]{:S(2)}, u32[]{:S(2)}) collective-permute-start(f32[2048]{0:T(1024)S(1)} %add.179), channel_id=1, source_target_pairs={{0,8},{1,9},{2,10},{3,11},{4,12},{5,13},{6,14},{7,15},{8,0},{9,1},... | collective-permute-start | bytes 24584 | tf_op jit(solution)/shard_map/ppermute | solution.py:24
  61.7 13.4 %collective-permute-start.7 = (bf16[64,2048]{1,0:T(8,128)(2,1)S(1)}, bf16[64,2048]{1,0:T(8,128)(2,1)S(1)}, u32[]{:S(2)}, u32[]{:S(2)}) collective-permute-start(bf16[64,2048]{1,0:T(8,128)(2,1)S(1)} %pad_maximum_fusion), channel_id=1, source_target_pairs={{0,1},{1,0},{2,3},{3,2},{4,5},{5,4},{6,7},{7,6},{8,9},{9,8},{10,11... | collective-permute-start | bytes 786440 | tf_op jit(solution)/shard_map/ppermute | solution.py:24
  70.4 4.6 %collective-permute-start.8 = (bf16[64,2048]{1,0:T(8,128)(2,1)S(1)}, bf16[64,2048]{1,0:T(8,128)(2,1)S(1)}, u32[]{:S(2)}, u32[]{:S(2)}) collective-permute-start(bf16[64,2048]{1,0:T(8,128)(2,1)S(1)} %pad_maximum_fusion.1), channel_id=1, source_target_pairs={{0,1},{1,0},{2,3},{3,2},{4,5},{5,4},{6,7},{7,6},{8,9},{9,8},{10,11... | collective-permute-start | bytes 786440 | tf_op jit(solution)/shard_map/ppermute | solution.py:24
  75.1 3.4 %copy-start = (bf16[2048,2048]{1,0:T(8,128)(2,1)S(1)}, bf16[2048,2048]{1,0:T(8,128)(2,1)}, u32[]{:S(2)}) copy-start(bf16[2048,2048]{1,0:T(8,128)(2,1)} %chol_ref.1) | copy-start | bytes 25165828
  81.9 2.0 %collective-permute-start.13 = (bf16[128,2048]{1,0:T(8,128)(2,1)S(1)}, bf16[128,2048]{1,0:T(8,128)(2,1)S(1)}, u32[]{:S(2)}, u32[]{:S(2)}) collective-permute-start(bf16[128,2048]{1,0:T(8,128)(2,1)S(1)} %get-tuple-element.26), channel_id=1, source_target_pairs={{0,1},{1,0},{2,3},{3,2},{4,5},{5,4},{6,7},{7,6},{8,9},{9,8},{10,11... | collective-permute-start | bytes 1572872 | tf_op jit(solution)/shard_map/ppermute | solution.py:24
  84.1 7.1 %collective-permute-start.17 = (f16[1,16,2048]{2,1,0:T(8,128)(2,1)S(1)}, f16[1,16,2048]{2,1,0:T(8,128)(2,1)S(1)}, u32[]{:S(2)}, u32[]{:S(2)}) collective-permute-start(f16[1,16,2048]{2,1,0:T(8,128)(2,1)S(1)} %get-tuple-element.32), channel_id=1, source_target_pairs={{0,2},{1,3},{2,0},{3,1},{4,6},{5,7},{6,4},{7,5},{8,10},{9,11},{10,... | collective-permute-start | bytes 196616 | tf_op jit(solution)/shard_map/ppermute | solution.py:24
  84.7 6.7 %collective-permute-start.18 = (f16[1,16,2048]{2,1,0:T(8,128)(2,1)S(1)}, f16[1,16,2048]{2,1,0:T(8,128)(2,1)S(1)}, u32[]{:S(2)}, u32[]{:S(2)}) collective-permute-start(f16[1,16,2048]{2,1,0:T(8,128)(2,1)S(1)} %get-tuple-element.31), channel_id=1, source_target_pairs={{0,4},{1,5},{2,6},{3,7},{4,0},{5,1},{6,2},{7,3},{8,12},{9,13},{10,... | collective-permute-start | bytes 196616 | tf_op jit(solution)/shard_map/ppermute | solution.py:24
  87.7 5.2 %collective-permute-start.19 = (f16[1,16,2048]{2,1,0:T(8,128)(2,1)S(1)}, f16[1,16,2048]{2,1,0:T(8,128)(2,1)S(1)}, u32[]{:S(2)}, u32[]{:S(2)}) collective-permute-start(f16[1,16,2048]{2,1,0:T(8,128)(2,1)S(1)} %get-tuple-element.30), channel_id=1, source_target_pairs={{0,6},{1,7},{2,4},{3,5},{4,2},{5,3},{6,0},{7,1},{8,14},{9,15},{10,... | collective-permute-start | bytes 196616 | tf_op jit(solution)/shard_map/ppermute | solution.py:24
  87.7 5.7 %collective-permute-start.14 = (f16[16,2048]{1,0:T(8,128)(2,1)S(1)}, f16[16,2048]{1,0:T(8,128)(2,1)S(1)}, u32[]{:S(2)}, u32[]{:S(2)}) collective-permute-start(f16[16,2048]{1,0:T(8,128)(2,1)S(1)} %get-tuple-element.29), channel_id=1, source_target_pairs={{0,2},{1,3},{2,0},{3,1},{4,6},{5,7},{6,4},{7,5},{8,10},{9,11},{10,... | collective-permute-start | bytes 196616 | tf_op jit(solution)/shard_map/ppermute | solution.py:24
  89.2 4.7 %collective-permute-start.15 = (f16[16,2048]{1,0:T(8,128)(2,1)S(1)}, f16[16,2048]{1,0:T(8,128)(2,1)S(1)}, u32[]{:S(2)}, u32[]{:S(2)}) collective-permute-start(f16[16,2048]{1,0:T(8,128)(2,1)S(1)} %get-tuple-element.34), channel_id=1, source_target_pairs={{0,4},{1,5},{2,6},{3,7},{4,0},{5,1},{6,2},{7,3},{8,12},{9,13},{10,... | collective-permute-start | bytes 196616 | tf_op jit(solution)/shard_map/ppermute | solution.py:24
  91.2 5.2 %collective-permute-start.16 = (f16[16,2048]{1,0:T(8,128)(2,1)S(1)}, f16[16,2048]{1,0:T(8,128)(2,1)S(1)}, u32[]{:S(2)}, u32[]{:S(2)}) collective-permute-start(f16[16,2048]{1,0:T(8,128)(2,1)S(1)} %get-tuple-element.33), channel_id=1, source_target_pairs={{0,6},{1,7},{2,4},{3,5},{4,2},{5,3},{6,0},{7,1},{8,14},{9,15},{10,... | collective-permute-start | bytes 196616 | tf_op jit(solution)/shard_map/ppermute | solution.py:24
  93.0 5.9 %collective-permute-start.20 = (f16[16,2048]{1,0:T(8,128)(2,1)S(1)}, f16[16,2048]{1,0:T(8,128)(2,1)S(1)}, u32[]{:S(2)}, u32[]{:S(2)}) collective-permute-start(f16[16,2048]{1,0:T(8,128)(2,1)S(1)} %fusion.16), channel_id=1, source_target_pairs={{0,8},{1,9},{2,10},{3,11},{4,12},{5,13},{6,14},{7,15},{8,0},{9,1},... | collective-permute-start | bytes 196616 | tf_op jit(solution)/shard_map/ppermute | solution.py:24

commit v3 on v2

v3 whole, which is shorter than its diff:
```python
import functools

import jax
import jax.numpy as jnp
from jax import lax
from jax.experimental import pallas as pl
from jax.experimental.pallas import tpu as pltpu
from jax.sharding import PartitionSpec as P

F32, F16, BF16 = jnp.float32, jnp.float16, jnp.bfloat16
DIRECT_CHIPS = 8


def stage_radices(chips):
    radices = []
    while chips > 1:
        radix = 4 if chips % 4 == 0 else 2
        radices.append(radix)
        chips //= radix
    return radices


def swap(x, mask, n):
    return lax.ppermute(x, "chol", [(i, i ^ mask) for i in range(n)])


def split_kernel(greens_ref, *outs):
    me = lax.axis_index("chol")
    own, pairs = greens_ref.shape[0], outs[0].shape[1]
    for m, out in enumerate(outs):
        for j in range(2):
            there = pl.multiple_of(jnp.bitwise_xor(me, 2 * m + j) * pairs, pairs)
            out[pl.ds(j * own, own), :] = greens_ref[:, pl.ds(there, pairs)]


def split_by_chip(greens, chips):
    own, total = greens.shape
    shape = (2 * own, total // (2 * chips))
    return pl.pallas_call(
        split_kernel,
        in_specs=[pl.BlockSpec(memory_space=pltpu.VMEM)],
        out_specs=[pl.BlockSpec(memory_space=pltpu.VMEM)] * chips,
        out_shape=[jax.ShapeDtypeStruct(shape, greens.dtype)] * chips,
        compiler_params=pltpu.CompilerParams(vmem_limit_bytes=8 * 2**20),
        cost_estimate=pl.CostEstimate(flops=0, bytes_accessed=4 * greens.size, transcendentals=0),
    )(greens)


def after(x, *others):
    return lax.optimization_barrier((x,) + others)[0]


def collect_walkers(greens, chips, n):
    own = greens.shape[0]
    sent = split_by_chip(greens, chips)
    got = [sent[0]]
    free = 2
    for m in range(1, chips):
        ended = m - chips // 2 - free + 1
        message = sent[m] if ended < 1 else after(sent[m], got[ended])
        got.append(swap(message, 2 * m, n))
    near, far = got[: chips // 2], got[chips // 2 :]
    passed = [swap(jnp.concatenate([x[own:] for x in part]), 1, n) for part in (near, far)]
    return jnp.concatenate([x[:own] for x in got] + passed), near[-1]


def mean_kernel(parts, chol_ref, mean_ref, part_ref, staged_ref, sems):
    step = chol_ref.shape[0] // parts
    copies = []
    for t in range(parts):
        at = pl.ds(t * step, step)
        copies.append(pltpu.make_async_copy(chol_ref.at[at], staged_ref.at[at], sems.at[t]))
        copies[-1].start()
    mean = jnp.broadcast_to(mean_ref[...], (8, mean_ref.shape[1]))
    for t, copy in enumerate(copies):
        copy.wait()
        at = pl.ds(t * step, step)
        part = lax.dot_general(
            mean, staged_ref[at, :], (((1,), (1,)), ((), ())), preferred_element_type=F32
        )
        part_ref[:, at] = part[:1]


def mean_part(chol, mean, parts=8):
    return pl.pallas_call(
        functools.partial(mean_kernel, parts),
        in_specs=[pl.BlockSpec(memory_space=pl.ANY), pl.BlockSpec(memory_space=pltpu.VMEM)],
        out_specs=[pl.BlockSpec(memory_space=pltpu.VMEM)] * 2,
        out_shape=[
            jax.ShapeDtypeStruct((1, chol.shape[0]), F32),
            jax.ShapeDtypeStruct(chol.shape, chol.dtype),
        ],
        scratch_shapes=[pltpu.SemaphoreType.DMA((parts,))],
        compiler_params=pltpu.CompilerParams(vmem_limit_bytes=20 * 2**20),
        cost_estimate=pl.CostEstimate(
            flops=16 * chol.size, bytes_accessed=2 * chol.size, transcendentals=0
        ),
    )(chol, mean)


def bias_kernel(tile, index_ref, rows_ref, chol_ref, keep_ref, send_ref, picked):
    half, nchol = keep_ref.shape
    walkers = rows_ref.shape[0]
    chosen = index_ref[...] == lax.broadcasted_iota(jnp.int32, (2 * half, walkers), 1)
    picked[...] = jnp.dot(
        chosen.astype(BF16), rows_ref[...], preferred_element_type=F32
    ).astype(BF16)

    @pl.loop(0, nchol // tile)
    def _(t):
        at = pl.ds(pl.multiple_of(t * tile, tile), tile)
        part = lax.dot_general(
            picked[...], chol_ref[at, :], (((1,), (1,)), ((), ())), preferred_element_type=F32
        )
        keep_ref[:, at] = part[:half]
        send_ref[:, at] = part[half:].astype(BF16)


def partial_bias(index, rows, chol, tile):
    slots, (nchol, pairs) = index.shape[0], chol.shape
    half = slots // 2
    return pl.pallas_call(
        functools.partial(bias_kernel, tile),
        in_specs=[pl.BlockSpec(memory_space=pltpu.VMEM)] * 3,
        out_specs=[pl.BlockSpec(memory_space=pltpu.VMEM)] * 2,
        out_shape=[
            jax.ShapeDtypeStruct((half, nchol), F32),
            jax.ShapeDtypeStruct((half, nchol), BF16),
        ],
        scratch_shapes=[pltpu.VMEM((slots, pairs), BF16)],
        compiler_params=pltpu.CompilerParams(vmem_limit_bytes=28 * 2**20),
        cost_estimate=pl.CostEstimate(
            flops=2 * slots * pairs * (nchol + rows.shape[0]),
            bytes_accessed=2 * nchol * pairs + 2 * rows.size + 6 * half * nchol,
            transcendentals=0,
        ),
    )(index, rows, chol)


def swap_both(x, extra, mask, n):
    got = swap(jnp.concatenate([x, extra], axis=-1).astype(F16), mask, n).astype(F32)
    return got[..., : x.shape[-1]], got[..., x.shape[-1] :]


def reduce_over_chips(held, mean, radices, bit, n):
    radix, rest = radices[0], radices[1:]
    later = held.shape[0] // radix
    held = held.reshape((radix, later) + held.shape[1:])
    masks = [m << bit for m in range(radix)]
    mine, near = held[0, 0], [held[m, 0] for m in range(1, radix)]
    if later == 1:
        for m in range(1, radix):
            got, got_mean = swap_both(near[m - 1], mean, masks[m], n)
            mine, mean = mine + got, mean + got_mean
        return mine, mean
    onward, more = held[0, 1:], mean
    for m in range(1, radix):
        if later == 2:
            got, got_mean = swap_both(held[m, 1], mean, masks[m], n)
            got = got[None]
        else:
            got = swap(held[m, 1:].astype(F16), masks[m], n).astype(F32)
            got_mean = swap(mean, masks[m], n)
        onward, more = onward + got, more + got_mean
    near, onward = lax.optimization_barrier(([x.astype(F16) for x in near], onward))
    for m in range(1, radix):
        mine = mine + swap(near[m - 1], masks[m], n).astype(F32)
    return reduce_over_chips(
        jnp.concatenate([mine[None], onward]), more, rest, bit + radix.bit_length() - 1, n
    )


def per_device(n, chol_vectors, mean_greens, greens, walker_order, noise_field):
    me = lax.axis_index("chol")
    own = greens.shape[0]
    chips = n // 2
    radices = stage_radices(chips)

    place = jnp.arange(n, dtype=jnp.int32)
    relative, weight, left = place // chips, 2, place % chips
    for stage, radix in enumerate(radices):
        later = 1
        for r in radices[stage + 1 :]:
            later *= r
        relative = relative + weight * (left // later)
        left, weight = left % later, weight * radix
    owners = jnp.bitwise_xor(relative, me)
    index = walker_order.reshape(n, own)[owners].reshape(-1)

    if chips <= DIRECT_CHIPS:
        rows, ended = collect_walkers(greens, chips, n)
        mean_greens = after(mean_greens, ended)
        source = jnp.bitwise_xor(index // own, me)
        index = ((source % 2) * chips + source // 2) * own + index % own
    else:
        rows = lax.all_to_all(greens, "chol", split_axis=1, concat_axis=0, tiled=True)
    mean, chol = mean_part(chol_vectors, mean_greens[None, :])
    mean = mean.reshape(own, -1)
    mean = mean + swap(mean, 1, n)
    keep, send = partial_bias(index[:, None], after(rows, mean), chol, 512)
    held = keep + swap(send, 1, n).astype(F32)
    raw_bias, mean = reduce_over_chips(held.reshape(chips, own, -1), mean, radices, 1, n)
    return noise_field - (jnp.tanh(raw_bias) - mean.reshape(1, -1))


def solution(mesh):
    placed = (
        P(None, "chol"),
        P("chol"),
        P(("grp", "chol"), None),
        P("grp"),
        P(("grp", "chol"), None),
    )
    return jax.shard_map(
        functools.partial(per_device, mesh.shape["chol"]),
        mesh=mesh,
        in_specs=placed,
        out_specs=P(("grp", "chol"), None),
        check_vma=False,
    )
```

time: 99.8 us -> 58 us (0.58)
  Pallas kernels: 36.4 us -> 9.43 us
  waiting for transfers between devices: 26.3 us -> 13.2 us
  matrix products: 5.64 us -> 0 us
  local copies, waits for them, and re-layouts: 5.04 us -> 6.91 us
  starting transfers between devices: 24.7 us -> 26.5 us
    pallas_call x1 -> x2, Pallas kernels: 33 us -> 5.99 us  [the longest x1 5.92 us: mean_part(): pl.pallas_call(functools.partial(mean_kernel, parts), in_specs=[pl.BlockS...]
    ppermute x21 -> x18, waiting for transfers between devices: 26.3 us -> 13.2 us  [swap(): return lax.ppermute(x, 'chol', [(i, i ^ mask) for i in range(n)])]
    dot_general x1 -> x0, matrix products: 5.64 us -> none  [per_device(): mean_field = jnp.dot(chol_vectors, mean_greens, preferred_element_type=F32)]
    ppermute x21 -> x18, starting transfers between devices: 24.7 us -> 26.5 us  [swap(): return lax.ppermute(x, 'chol', [(i, i ^ mask) for i in range(n)])]
    unnamed x16 -> x7, local copies, waits for them, and re-layouts: 4.11 us -> 4.63 us
  transfers between devices with their start and end apart: 21 -> 18, of which waited for: 10 -> 8; matrix products, arithmetic and copies ran while one was open for 8% -> 4% of each run, Pallas kernels for 0% -> 10%
where the time goes in v3:
time: 58 us; the launch traced here: 57.7 us
  starting transfers between devices  26.5 us (46%)
  waiting for transfers between devices  13.2 us (23%)
  Pallas kernels  9.43 us (16%)
  local copies, waits for them, and re-layouts  6.91 us (12%)
  other arithmetic  1.4 us (2%)
    ppermute x18, starting transfers between devices, swap(): return lax.ppermute(x, 'chol', [(i, i ^ mask) for i in range(n)])  26.5 us
    ppermute x18, waiting for transfers between devices, swap(): return lax.ppermute(x, 'chol', [(i, i ^ mask) for i in range(n)])  13.2 us
    pallas_call x1, Pallas kernels, mean_part(): pl.pallas_call(functools.partial(mean_kernel, parts), in_specs=[pl.BlockS...  5.92 us
    unnamed x7, local copies, waits for them, and re-layouts  4.63 us
    pallas_call x1, Pallas kernels, partial_bias(): pl.pallas_call(functools.partial(bias_kernel, tile), in_specs=[pl.BlockSp...  3.44 us
  transfers between devices with their start and end apart: 18, of which 8 were waited for; matrix products, arithmetic and copies ran while one was open for 4% of the time, Pallas kernels for 10%

profile of v3, /device:TPU:0, one launch (start us, length us, event | category | flops | bytes accessed | tf_op | source)
XLA Modules:
  0.0 57.7 jit_solution(9859346117091997251)
XLA Ops:
  0.0 0.0 copy-start.1
  0.0 1.2 %copy-done.1 = bf16[16,32768]{1,0:T(8,128)(2,1)S(1)} copy-done((bf16[16,32768]{1,0:T(8,128)(2,1)S(1)}, bf16[16,32768]{1,0:T(8,128)(2,1)}, u32[]{:S(2)}) %copy-start.1) | copy-done | bytes 1048600
  1.2 0.1 shard_map.55
  1.3 3.0 %collective-permute-start = (bf16[32,2048]{1,0:T(8,128)(2,1)S(1)}, bf16[32,2048]{1,0:T(8,128)(2,1)S(1)}, u32[]{:S(2)}, u32[]{:S(2)}) collective-permute-start(bf16[32,2048]{1,0:T(8,128)(2,1)S(1)} %get-tuple-element.26), channel_id=1, source_target_pairs={{0,2},{1,3},{2,0},{3,1},{4,6},{5,7},{6,4},{7,5},{8,10},{9,11},{10,... | collective-permute-start | bytes 393224 | tf_op jit(solution)/shard_map/ppermute | solution.py:24
  4.3 1.6 %collective-permute-start.1 = (bf16[32,2048]{1,0:T(8,128)(2,1)S(1)}, bf16[32,2048]{1,0:T(8,128)(2,1)S(1)}, u32[]{:S(2)}, u32[]{:S(2)}) collective-permute-start(bf16[32,2048]{1,0:T(8,128)(2,1)S(1)} %get-tuple-element.27), channel_id=1, source_target_pairs={{0,4},{1,5},{2,6},{3,7},{4,0},{5,1},{6,2},{7,3},{8,12},{9,13},{10,... | collective-permute-start | bytes 393224 | tf_op jit(solution)/shard_map/ppermute | solution.py:24
  5.9 0.0 collective-permute-start.2
  5.9 3.0 %collective-permute-start.3 = (bf16[32,2048]{1,0:T(8,128)(2,1)S(1)}, bf16[32,2048]{1,0:T(8,128)(2,1)S(1)}, u32[]{:S(2)}, u32[]{:S(2)}) collective-permute-start(bf16[32,2048]{1,0:T(8,128)(2,1)S(1)} %get-tuple-element.29), channel_id=1, source_target_pairs={{0,8},{1,9},{2,10},{3,11},{4,12},{5,13},{6,14},{7,15},{8,0},{9,1},... | collective-permute-start | bytes 393224 | tf_op jit(solution)/shard_map/ppermute | solution.py:24
  8.9 1.3 %collective-permute-start.4 = (bf16[32,2048]{1,0:T(8,128)(2,1)S(1)}, bf16[32,2048]{1,0:T(8,128)(2,1)S(1)}, u32[]{:S(2)}, u32[]{:S(2)}) collective-permute-start(bf16[32,2048]{1,0:T(8,128)(2,1)S(1)} %get-tuple-element.30), channel_id=1, source_target_pairs={{0,10},{1,11},{2,8},{3,9},{4,14},{5,15},{6,12},{7,13},{8,2},{9,3},... | collective-permute-start | bytes 393224 | tf_op jit(solution)/shard_map/ppermute | solution.py:24
  10.2 0.8 %reshape.335 = s32[16,16]{1,0:T(8,128)S(1)} reshape(s32[256]{0:T(256)} %param.8) | data formatting | bytes 2048 | tf_op jit(solution)/shard_map/reshape | solution.py:188
  11.0 0.6 gather_fusion
  11.5 0.1 reshape.346
  11.7 0.2 fusion.4.index_ref
  11.9 0.0 collective-permute-done
  11.9 3.7 %collective-permute-start.5 = (bf16[32,2048]{1,0:T(8,128)(2,1)S(1)}, bf16[32,2048]{1,0:T(8,128)(2,1)S(1)}, u32[]{:S(2)}, u32[]{:S(2)}) collective-permute-start(bf16[32,2048]{1,0:T(8,128)(2,1)S(1)} %get-tuple-element.32), channel_id=1, source_target_pairs={{0,12},{1,13},{2,14},{3,15},{4,8},{5,9},{6,10},{7,11},{8,4},{9,5},... | collective-permute-start | bytes 393224 | tf_op jit(solution)/shard_map/ppermute | solution.py:24
  15.6 0.0 collective-permute-done.1
  15.6 0.1 collective-permute-start.6
  15.7 0.0 collective-permute-done.2
  15.7 0.7 %broadcast_in_dim.2.mean_ref = bf16[1,2048]{1,0:T(2,128)(2,1)S(1)} reshape(bf16[2048]{0:T(1024)(128)(2,1)} %param.6) | data formatting | bytes 8192 | tf_op jit(solution)/shard_map/broadcast_in_dim | solution.py:197
  16.5 0.1 collective-permute-start.7
  16.6 0.0 copy-start
  16.6 3.4 %copy-done = bf16[2048,2048]{1,0:T(8,128)(2,1)S(1)} copy-done((bf16[2048,2048]{1,0:T(8,128)(2,1)S(1)}, bf16[2048,2048]{1,0:T(8,128)(2,1)}, u32[]{:S(2)}) %copy-start) | copy-done | bytes 8388632
  20.0 5.9 %shard_map.56 = (f32[1,2048]{1,0:T(1,128)S(1)}, bf16[2048,2048]{1,0:T(8,128)(2,1)S(1)}) custom-call(bf16[2048,2048]{1,0:T(8,128)(2,1)S(1)} %copy-done, bf16[1,2048]{1,0:T(2,128)(2,1)S(1)} %broadcast_in_dim.2.mean_ref), custom_call_target="tpu_custom_call" | custom-call | flops 67108864 | bytes 8388608 | tf_op jit(solution)/shard_map/pallas_call | solution.py:85
  25.9 0.0 collective-permute-done.3
  25.9 0.6 collective-permute-start.9
  26.5 1.9 %collective-permute-done.4 = bf16[32,2048]{1,0:T(8,128)(2,1)S(1)} collective-permute-done((bf16[32,2048]{1,0:T(8,128)(2,1)S(1)}, bf16[32,2048]{1,0:T(8,128)(2,1)S(1)}, u32[]{:S(2)}, u32[]{:S(2)}) %collective-permute-start.4) | collective-permute-done | bytes 131104 | tf_op jit(solution)/shard_map/ppermute | solution.py:24
  28.4 0.0 collective-permute-done.5
  28.4 0.0 collective-permute-done.6
  28.4 0.1 collective-permute-start.8
  28.5 0.0 collective-permute-done.9
  28.5 0.0 collective-permute-done.7
  28.6 1.5 %collective-permute-done.8 = bf16[64,2048]{1,0:T(8,128)(2,1)S(1)} collective-permute-done((bf16[64,2048]{1,0:T(8,128)(2,1)S(1)}, bf16[64,2048]{1,0:T(8,128)(2,1)S(1)}, u32[]{:S(2)}, u32[]{:S(2)}) %collective-permute-start.8) | collective-permute-done | bytes 262176 | tf_op jit(solution)/shard_map/ppermute | solution.py:24
  30.1 0.0 copy-start.2
  30.1 3.4 %shard_map.57 = (f32[128,2048]{1,0:T(8,128)S(1)}, bf16[128,2048]{1,0:T(8,128)(2,1)S(1)}) custom-call(s32[256,1]{1,0:T(8,128)S(1)} %fusion.4.index_ref, bf16[256,2048]{1,0:T(8,128)(2,1)S(1)} %constant_dynamic-update-slice_fusion.rows_ref, bf16[2048,2048]{1,0:T(8,128)(2,1)S(1)} %get-tuple-element.38.chol_ref), custom_call_target="tpu_custom_call" | custom-call | flops 2415919104 | bytes 11010048 | tf_op jit(solution)/shard_map/pallas_call | solution.py:122
  33.5 0.2 collective-permute-start.10
  33.7 1.8 %collective-permute-done.10 = bf16[128,2048]{1,0:T(8,128)(2,1)S(1)} collective-permute-done((bf16[128,2048]{1,0:T(8,128)(2,1)S(1)}, bf16[128,2048]{1,0:T(8,128)(2,1)S(1)}, u32[]{:S(2)}, u32[]{:S(2)}) %collective-permute-start.10) | collective-permute-done | bytes 524320 | tf_op jit(solution)/shard_map/ppermute | solution.py:24
  35.5 0.1 convert_add_fusion
  35.6 0.1 convert.26
  35.7 0.1 slice_bitcast_fusion.5
  35.8 0.1 pad_maximum_fusion.4
  35.8 1.4 %collective-permute-start.11 = (f16[16,2176]{1,0:T(8,128)(2,1)S(1)}, f16[16,2176]{1,0:T(8,128)(2,1)S(1)}, u32[]{:S(2)}, u32[]{:S(2)}) collective-permute-start(f16[16,2176]{1,0:T(8,128)(2,1)S(1)} %get-tuple-element.71), channel_id=1, source_target_pairs={{0,2},{1,3},{2,0},{3,1},{4,6},{5,7},{6,4},{7,5},{8,10},{9,11},{10,... | collective-permute-start | bytes 208904 | tf_op jit(solution)/shard_map/ppermute | solution.py:24
  37.2 4.0 %collective-permute-start.12 = (f16[16,2176]{1,0:T(8,128)(2,1)S(1)}, f16[16,2176]{1,0:T(8,128)(2,1)S(1)}, u32[]{:S(2)}, u32[]{:S(2)}) collective-permute-start(f16[16,2176]{1,0:T(8,128)(2,1)S(1)} %get-tuple-element.72), channel_id=1, source_target_pairs={{0,4},{1,5},{2,6},{3,7},{4,0},{5,1},{6,2},{7,3},{8,12},{9,13},{10,... | collective-permute-start | bytes 208904 | tf_op jit(solution)/shard_map/ppermute | solution.py:24
  41.2 1.1 %collective-permute-start.13 = (f16[16,2176]{1,0:T(8,128)(2,1)S(1)}, f16[16,2176]{1,0:T(8,128)(2,1)S(1)}, u32[]{:S(2)}, u32[]{:S(2)}) collective-permute-start(f16[16,2176]{1,0:T(8,128)(2,1)S(1)} %get-tuple-element.73), channel_id=1, source_target_pairs={{0,6},{1,7},{2,4},{3,5},{4,2},{5,3},{6,0},{7,1},{8,14},{9,15},{10,... | collective-permute-start | bytes 208904 | tf_op jit(solution)/shard_map/ppermute | solution.py:24
  42.3 0.0 collective-permute-done.11
  42.4 1.4 %collective-permute-done.12 = f16[16,2176]{1,0:T(8,128)(2,1)S(1)} collective-permute-done((f16[16,2176]{1,0:T(8,128)(2,1)S(1)}, f16[16,2176]{1,0:T(8,128)(2,1)S(1)}, u32[]{:S(2)}, u32[]{:S(2)}) %collective-permute-start.12) | collective-permute-done | bytes 69664 | tf_op jit(solution)/shard_map/ppermute | solution.py:24
  43.8 2.6 %collective-permute-done.13 = f16[16,2176]{1,0:T(8,128)(2,1)S(1)} collective-permute-done((f16[16,2176]{1,0:T(8,128)(2,1)S(1)}, f16[16,2176]{1,0:T(8,128)(2,1)S(1)}, u32[]{:S(2)}, u32[]{:S(2)}) %collective-permute-start.13) | collective-permute-done | bytes 69664 | tf_op jit(solution)/shard_map/ppermute | solution.py:24
  46.6 2.9 %collective-permute-start.17 = (f16[16,2176]{1,0:T(8,128)(2,1)S(1)}, f16[16,2176]{1,0:T(8,128)(2,1)S(1)}, u32[]{:S(2)}, u32[]{:S(2)}) collective-permute-start(f16[16,2176]{1,0:T(8,128)(2,1)S(1)} %pad_maximum_fusion.5), channel_id=1, source_target_pairs={{0,8},{1,9},{2,10},{3,11},{4,12},{5,13},{6,14},{7,15},{8,0},{9,1},... | collective-permute-start | bytes 208904 | tf_op jit(solution)/shard_map/ppermute | solution.py:24
  49.5 0.7 %collective-permute-start.14 = (f16[16,2048]{1,0:T(8,128)(2,1)S(1)}, f16[16,2048]{1,0:T(8,128)(2,1)S(1)}, u32[]{:S(2)}, u32[]{:S(2)}) collective-permute-start(f16[16,2048]{1,0:T(8,128)(2,1)S(1)} %get-tuple-element.41), channel_id=1, source_target_pairs={{0,2},{1,3},{2,0},{3,1},{4,6},{5,7},{6,4},{7,5},{8,10},{9,11},{10,... | collective-permute-start | bytes 196616 | tf_op jit(solution)/shard_map/ppermute | solution.py:24
  50.2 1.6 %collective-permute-start.15 = (f16[16,2048]{1,0:T(8,128)(2,1)S(1)}, f16[16,2048]{1,0:T(8,128)(2,1)S(1)}, u32[]{:S(2)}, u32[]{:S(2)}) collective-permute-start(f16[16,2048]{1,0:T(8,128)(2,1)S(1)} %get-tuple-element.42), channel_id=1, source_target_pairs={{0,4},{1,5},{2,6},{3,7},{4,0},{5,1},{6,2},{7,3},{8,12},{9,13},{10,... | collective-permute-start | bytes 196616 | tf_op jit(solution)/shard_map/ppermute | solution.py:24
  51.8 1.1 %collective-permute-start.16 = (f16[16,2048]{1,0:T(8,128)(2,1)S(1)}, f16[16,2048]{1,0:T(8,128)(2,1)S(1)}, u32[]{:S(2)}, u32[]{:S(2)}) collective-permute-start(f16[16,2048]{1,0:T(8,128)(2,1)S(1)} %get-tuple-element.43), channel_id=1, source_target_pairs={{0,6},{1,7},{2,4},{3,5},{4,2},{5,3},{6,0},{7,1},{8,14},{9,15},{10,... | collective-permute-start | bytes 196616 | tf_op jit(solution)/shard_map/ppermute | solution.py:24
  53.0 0.0 collective-permute-done.17
  53.0 1.4 %collective-permute-done.14 = f16[16,2048]{1,0:T(8,128)(2,1)S(1)} collective-permute-done((f16[16,2048]{1,0:T(8,128)(2,1)S(1)}, f16[16,2048]{1,0:T(8,128)(2,1)S(1)}, u32[]{:S(2)}, u32[]{:S(2)}) %collective-permute-start.14) | collective-permute-done | bytes 65568 | tf_op jit(solution)/shard_map/ppermute | solution.py:24
  54.4 0.1 collective-permute-done.15
  54.5 2.5 %collective-permute-done.16 = f16[16,2048]{1,0:T(8,128)(2,1)S(1)} collective-permute-done((f16[16,2048]{1,0:T(8,128)(2,1)S(1)}, f16[16,2048]{1,0:T(8,128)(2,1)S(1)}, u32[]{:S(2)}, u32[]{:S(2)}) %collective-permute-start.16) | collective-permute-done | bytes 65568 | tf_op jit(solution)/shard_map/ppermute | solution.py:24
  57.0 0.0 copy-done.2
  57.0 0.7 %fusion.7 = f32[16,2048]{1,0:T(8,128)} fusion(f32[16,2048]{1,0:T(8,128)S(1)} %copy-done.2, f32[16,2176]{1,0:T(8,128)S(1)} %convert_element_type.50, f32[4,2,16,2048]{3,2,1,0:T(8,128)S(1)} %bitcast.40, f16[16,2048]{1,0:T(8,128)(2,1)S(1)} %collective-permute-done.16, f16[16,2048]{1,0:T(8,128)(2,1)S(1)} %collective-permute-done.15, ...), kind=kLoop, calls=%fused_computation.22 | loop fusion | flops 294912 | bytes 729088 | tf_op jit(solution)/shard_map/sub | solution.py:203
  (24 shorter events, 0.3 us)
Async XLA Ops:
  0.0 1.2 %copy-start.1 = (bf16[16,32768]{1,0:T(8,128)(2,1)S(1)}, bf16[16,32768]{1,0:T(8,128)(2,1)}, u32[]{:S(2)}) copy-start(bf16[16,32768]{1,0:T(8,128)(2,1)} %greens_ref.1) | copy-start | bytes 3145732
  1.3 10.6 %collective-permute-start = (bf16[32,2048]{1,0:T(8,128)(2,1)S(1)}, bf16[32,2048]{1,0:T(8,128)(2,1)S(1)}, u32[]{:S(2)}, u32[]{:S(2)}) collective-permute-start(bf16[32,2048]{1,0:T(8,128)(2,1)S(1)} %get-tuple-element.26), channel_id=1, source_target_pairs={{0,2},{1,3},{2,0},{3,1},{4,6},{5,7},{6,4},{7,5},{8,10},{9,11},{10,... | collective-permute-start | bytes 393224 | tf_op jit(solution)/shard_map/ppermute | solution.py:24
  4.3 11.3 %collective-permute-start.1 = (bf16[32,2048]{1,0:T(8,128)(2,1)S(1)}, bf16[32,2048]{1,0:T(8,128)(2,1)S(1)}, u32[]{:S(2)}, u32[]{:S(2)}) collective-permute-start(bf16[32,2048]{1,0:T(8,128)(2,1)S(1)} %get-tuple-element.27), channel_id=1, source_target_pairs={{0,4},{1,5},{2,6},{3,7},{4,0},{5,1},{6,2},{7,3},{8,12},{9,13},{10,... | collective-permute-start | bytes 393224 | tf_op jit(solution)/shard_map/ppermute | solution.py:24
  5.9 9.8 %collective-permute-start.2 = (bf16[32,2048]{1,0:T(8,128)(2,1)S(1)}, bf16[32,2048]{1,0:T(8,128)(2,1)S(1)}, u32[]{:S(2)}, u32[]{:S(2)}) collective-permute-start(bf16[32,2048]{1,0:T(8,128)(2,1)S(1)} %get-tuple-element.28), channel_id=1, source_target_pairs={{0,6},{1,7},{2,4},{3,5},{4,2},{5,3},{6,0},{7,1},{8,14},{9,15},{10,... | collective-permute-start | bytes 393224 | tf_op jit(solution)/shard_map/ppermute | solution.py:24
  5.9 20.0 %collective-permute-start.3 = (bf16[32,2048]{1,0:T(8,128)(2,1)S(1)}, bf16[32,2048]{1,0:T(8,128)(2,1)S(1)}, u32[]{:S(2)}, u32[]{:S(2)}) collective-permute-start(bf16[32,2048]{1,0:T(8,128)(2,1)S(1)} %get-tuple-element.29), channel_id=1, source_target_pairs={{0,8},{1,9},{2,10},{3,11},{4,12},{5,13},{6,14},{7,15},{8,0},{9,1},... | collective-permute-start | bytes 393224 | tf_op jit(solution)/shard_map/ppermute | solution.py:24
  8.9 19.4 %collective-permute-start.4 = (bf16[32,2048]{1,0:T(8,128)(2,1)S(1)}, bf16[32,2048]{1,0:T(8,128)(2,1)S(1)}, u32[]{:S(2)}, u32[]{:S(2)}) collective-permute-start(bf16[32,2048]{1,0:T(8,128)(2,1)S(1)} %get-tuple-element.30), channel_id=1, source_target_pairs={{0,10},{1,11},{2,8},{3,9},{4,14},{5,15},{6,12},{7,13},{8,2},{9,3},... | collective-permute-start | bytes 393224 | tf_op jit(solution)/shard_map/ppermute | solution.py:24
  11.9 16.4 %collective-permute-start.5 = (bf16[32,2048]{1,0:T(8,128)(2,1)S(1)}, bf16[32,2048]{1,0:T(8,128)(2,1)S(1)}, u32[]{:S(2)}, u32[]{:S(2)}) collective-permute-start(bf16[32,2048]{1,0:T(8,128)(2,1)S(1)} %get-tuple-element.32), channel_id=1, source_target_pairs={{0,12},{1,13},{2,14},{3,15},{4,8},{5,9},{6,10},{7,11},{8,4},{9,5},... | collective-permute-start | bytes 393224 | tf_op jit(solution)/shard_map/ppermute | solution.py:24
  15.6 12.8 %collective-permute-start.6 = (bf16[32,2048]{1,0:T(8,128)(2,1)S(1)}, bf16[32,2048]{1,0:T(8,128)(2,1)S(1)}, u32[]{:S(2)}, u32[]{:S(2)}) collective-permute-start(bf16[32,2048]{1,0:T(8,128)(2,1)S(1)} %get-tuple-element.34), channel_id=1, source_target_pairs={{0,14},{1,15},{2,12},{3,13},{4,10},{5,11},{6,8},{7,9},{8,6},{9,7},... | collective-permute-start | bytes 393224 | tf_op jit(solution)/shard_map/ppermute | solution.py:24
  16.5 12.0 %collective-permute-start.7 = (bf16[64,2048]{1,0:T(8,128)(2,1)S(1)}, bf16[64,2048]{1,0:T(8,128)(2,1)S(1)}, u32[]{:S(2)}, u32[]{:S(2)}) collective-permute-start(bf16[64,2048]{1,0:T(8,128)(2,1)S(1)} %pad_maximum_fusion), channel_id=1, source_target_pairs={{0,1},{1,0},{2,3},{3,2},{4,5},{5,4},{6,7},{7,6},{8,9},{9,8},{10,11... | collective-permute-start | bytes 786440 | tf_op jit(solution)/shard_map/ppermute | solution.py:24
  16.6 3.4 %copy-start = (bf16[2048,2048]{1,0:T(8,128)(2,1)S(1)}, bf16[2048,2048]{1,0:T(8,128)(2,1)}, u32[]{:S(2)}) copy-start(bf16[2048,2048]{1,0:T(8,128)(2,1)} %chol_ref.1) | copy-start | bytes 25165828
  25.9 2.6 %collective-permute-start.9 = (f32[16,128]{1,0:T(8,128)S(1)}, f32[16,128]{1,0:T(8,128)S(1)}, u32[]{:S(2)}, u32[]{:S(2)}) collective-permute-start(f32[16,128]{1,0:T(8,128)S(1)} %bitcast.36), channel_id=1, source_target_pairs={{0,1},{1,0},{2,3},{3,2},{4,5},{5,4},{6,7},{7,6},{8,9},{9,8},{10,11... | collective-permute-start | bytes 24584 | tf_op jit(solution)/shard_map/ppermute | solution.py:24
  28.4 1.6 %collective-permute-start.8 = (bf16[64,2048]{1,0:T(8,128)(2,1)S(1)}, bf16[64,2048]{1,0:T(8,128)(2,1)S(1)}, u32[]{:S(2)}, u32[]{:S(2)}) collective-permute-start(bf16[64,2048]{1,0:T(8,128)(2,1)S(1)} %pad_maximum_fusion.1), channel_id=1, source_target_pairs={{0,1},{1,0},{2,3},{3,2},{4,5},{5,4},{6,7},{7,6},{8,9},{9,8},{10,11... | collective-permute-start | bytes 786440 | tf_op jit(solution)/shard_map/ppermute | solution.py:24
  30.1 27.0 %copy-start.2 = (f32[16,2048]{1,0:T(8,128)S(1)}, f32[16,2048]{1,0:T(8,128)}, u32[]{:S(2)}) copy-start(f32[16,2048]{1,0:T(8,128)} %param.9) | copy-start | bytes 393220
  33.5 2.0 %collective-permute-start.10 = (bf16[128,2048]{1,0:T(8,128)(2,1)S(1)}, bf16[128,2048]{1,0:T(8,128)(2,1)S(1)}, u32[]{:S(2)}, u32[]{:S(2)}) collective-permute-start(bf16[128,2048]{1,0:T(8,128)(2,1)S(1)} %get-tuple-element.40), channel_id=1, source_target_pairs={{0,1},{1,0},{2,3},{3,2},{4,5},{5,4},{6,7},{7,6},{8,9},{9,8},{10,11... | collective-permute-start | bytes 1572872 | tf_op jit(solution)/shard_map/ppermute | solution.py:24
  35.8 6.5 %collective-permute-start.11 = (f16[16,2176]{1,0:T(8,128)(2,1)S(1)}, f16[16,2176]{1,0:T(8,128)(2,1)S(1)}, u32[]{:S(2)}, u32[]{:S(2)}) collective-permute-start(f16[16,2176]{1,0:T(8,128)(2,1)S(1)} %get-tuple-element.71), channel_id=1, source_target_pairs={{0,2},{1,3},{2,0},{3,1},{4,6},{5,7},{6,4},{7,5},{8,10},{9,11},{10,... | collective-permute-start | bytes 208904 | tf_op jit(solution)/shard_map/ppermute | solution.py:24
  37.2 6.6 %collective-permute-start.12 = (f16[16,2176]{1,0:T(8,128)(2,1)S(1)}, f16[16,2176]{1,0:T(8,128)(2,1)S(1)}, u32[]{:S(2)}, u32[]{:S(2)}) collective-permute-start(f16[16,2176]{1,0:T(8,128)(2,1)S(1)} %get-tuple-element.72), channel_id=1, source_target_pairs={{0,4},{1,5},{2,6},{3,7},{4,0},{5,1},{6,2},{7,3},{8,12},{9,13},{10,... | collective-permute-start | bytes 208904 | tf_op jit(solution)/shard_map/ppermute | solution.py:24
  41.2 5.2 %collective-permute-start.13 = (f16[16,2176]{1,0:T(8,128)(2,1)S(1)}, f16[16,2176]{1,0:T(8,128)(2,1)S(1)}, u32[]{:S(2)}, u32[]{:S(2)}) collective-permute-start(f16[16,2176]{1,0:T(8,128)(2,1)S(1)} %get-tuple-element.73), channel_id=1, source_target_pairs={{0,6},{1,7},{2,4},{3,5},{4,2},{5,3},{6,0},{7,1},{8,14},{9,15},{10,... | collective-permute-start | bytes 208904 | tf_op jit(solution)/shard_map/ppermute | solution.py:24
  46.6 6.4 %collective-permute-start.17 = (f16[16,2176]{1,0:T(8,128)(2,1)S(1)}, f16[16,2176]{1,0:T(8,128)(2,1)S(1)}, u32[]{:S(2)}, u32[]{:S(2)}) collective-permute-start(f16[16,2176]{1,0:T(8,128)(2,1)S(1)} %pad_maximum_fusion.5), channel_id=1, source_target_pairs={{0,8},{1,9},{2,10},{3,11},{4,12},{5,13},{6,14},{7,15},{8,0},{9,1},... | collective-permute-start | bytes 208904 | tf_op jit(solution)/shard_map/ppermute | solution.py:24
  49.5 4.9 %collective-permute-start.14 = (f16[16,2048]{1,0:T(8,128)(2,1)S(1)}, f16[16,2048]{1,0:T(8,128)(2,1)S(1)}, u32[]{:S(2)}, u32[]{:S(2)}) collective-permute-start(f16[16,2048]{1,0:T(8,128)(2,1)S(1)} %get-tuple-element.41), channel_id=1, source_target_pairs={{0,2},{1,3},{2,0},{3,1},{4,6},{5,7},{6,4},{7,5},{8,10},{9,11},{10,... | collective-permute-start | bytes 196616 | tf_op jit(solution)/shard_map/ppermute | solution.py:24
  50.2 4.3 %collective-permute-start.15 = (f16[16,2048]{1,0:T(8,128)(2,1)S(1)}, f16[16,2048]{1,0:T(8,128)(2,1)S(1)}, u32[]{:S(2)}, u32[]{:S(2)}) collective-permute-start(f16[16,2048]{1,0:T(8,128)(2,1)S(1)} %get-tuple-element.42), channel_id=1, source_target_pairs={{0,4},{1,5},{2,6},{3,7},{4,0},{5,1},{6,2},{7,3},{8,12},{9,13},{10,... | collective-permute-start | bytes 196616 | tf_op jit(solution)/shard_map/ppermute | solution.py:24
  51.8 5.2 %collective-permute-start.16 = (f16[16,2048]{1,0:T(8,128)(2,1)S(1)}, f16[16,2048]{1,0:T(8,128)(2,1)S(1)}, u32[]{:S(2)}, u32[]{:S(2)}) collective-permute-start(f16[16,2048]{1,0:T(8,128)(2,1)S(1)} %get-tuple-element.43), channel_id=1, source_target_pairs={{0,6},{1,7},{2,4},{3,5},{4,2},{5,3},{6,0},{7,1},{8,14},{9,15},{10,... | collective-permute-start | bytes 196616 | tf_op jit(solution)/shard_map/ppermute | solution.py:24

commit v4 on v3

--- a/solution.py
+++ b/solution.py
@@ -53,15 +53,14 @@
 def collect_walkers(greens, chips, n):
     own = greens.shape[0]
     sent = split_by_chip(greens, chips)
+    waits = {3: 1, 5: 2, 7: 3} if chips == 8 else {}
     got = [sent[0]]
-    free = 2
     for m in range(1, chips):
-        ended = m - chips // 2 - free + 1
-        message = sent[m] if ended < 1 else after(sent[m], got[ended])
+        message = after(sent[m], got[waits[m]]) if m in waits else sent[m]
         got.append(swap(message, 2 * m, n))
     near, far = got[: chips // 2], got[chips // 2 :]
     passed = [swap(jnp.concatenate([x[own:] for x in part]), 1, n) for part in (near, far)]
-    return jnp.concatenate([x[:own] for x in got] + passed), near[-1]
+    return jnp.concatenate([x[:own] for x in got] + passed), got[chips // 4]
 
 
 def mean_kernel(parts, chol_ref, mean_ref, part_ref, staged_ref, sems):
@@ -91,7 +90,7 @@
             jax.ShapeDtypeStruct(chol.shape, chol.dtype),
         ],
         scratch_shapes=[pltpu.SemaphoreType.DMA((parts,))],
-        compiler_params=pltpu.CompilerParams(vmem_limit_bytes=20 * 2**20),
+        compiler_params=pltpu.CompilerParams(vmem_limit_bytes=40 * 2**20),
         cost_estimate=pl.CostEstimate(
             flops=16 * chol.size, bytes_accessed=2 * chol.size, transcendentals=0
         ),
@@ -138,36 +137,29 @@
 
 
 def swap_both(x, extra, mask, n):
-    got = swap(jnp.concatenate([x, extra], axis=-1).astype(F16), mask, n).astype(F32)
-    return got[..., : x.shape[-1]], got[..., x.shape[-1] :]
-
-
-def reduce_over_chips(held, mean, radices, bit, n):
-    radix, rest = radices[0], radices[1:]
-    later = held.shape[0] // radix
-    held = held.reshape((radix, later) + held.shape[1:])
-    masks = [m << bit for m in range(radix)]
-    mine, near = held[0, 0], [held[m, 0] for m in range(1, radix)]
-    if later == 1:
-        for m in range(1, radix):
-            got, got_mean = swap_both(near[m - 1], mean, masks[m], n)
-            mine, mean = mine + got, mean + got_mean
-        return mine, mean
-    onward, more = held[0, 1:], mean
-    for m in range(1, radix):
-        if later == 2:
-            got, got_mean = swap_both(held[m, 1], mean, masks[m], n)
-            got = got[None]
-        else:
-            got = swap(held[m, 1:].astype(F16), masks[m], n).astype(F32)
-            got_mean = swap(mean, masks[m], n)
-        onward, more = onward + got, more + got_mean
-    near, onward = lax.optimization_barrier(([x.astype(F16) for x in near], onward))
-    for m in range(1, radix):
-        mine = mine + swap(near[m - 1], masks[m], n).astype(F32)
-    return reduce_over_chips(
-        jnp.concatenate([mine[None], onward]), more, rest, bit + radix.bit_length() - 1, n
-    )
+    blocks, rows, g = x.shape
+    extra = jnp.pad(extra[None], ((0, blocks - 1), (0, 0), (0, 0)))
+    sent = jnp.concatenate([x, extra], axis=-1).astype(F16).reshape(blocks * rows, -1)
+    got = swap(sent, mask, n).astype(F32).reshape(blocks, rows, -1)
+    return got[..., :g], got[0, :, g:]
+
+
+def reduce_over_chips(held, mean, radices, n):
+    bit, mine = 1, []
+    for i, radix in enumerate(radices):
+        held = held.reshape((radix, held.shape[0] // radix) + held.shape[1:])
+        total, mean_total = held[0], mean
+        split = radix == 4 and i < len(radices) - 1
+        for m in (3, 1, 2) if radix == 4 else (1,):
+            skip = 1 if split and m == 3 else 0
+            got, got_mean = swap_both(held[m, skip:], mean, m << bit, n)
+            got = jnp.pad(got, ((skip, 0), (0, 0), (0, 0)))
+            total, mean_total = total + got, mean_total + got_mean
+        if split:
+            mine.append(swap(held[3, 0].astype(F16), 3 << bit, n).astype(F32))
+        held, mean = total, mean_total
+        bit += radix.bit_length() - 1
+    return held[0] + sum(mine), mean
 
 
 def per_device(n, chol_vectors, mean_greens, greens, walker_order, noise_field):
@@ -199,7 +191,7 @@
     mean = mean + swap(mean, 1, n)
     keep, send = partial_bias(index[:, None], after(rows, mean), chol, 512)
     held = keep + swap(send, 1, n).astype(F32)
-    raw_bias, mean = reduce_over_chips(held.reshape(chips, own, -1), mean, radices, 1, n)
+    raw_bias, mean = reduce_over_chips(held.reshape(chips, own, -1), mean, radices, n)
     return noise_field - (jnp.tanh(raw_bias) - mean.reshape(1, -1))
 
 

time: 58 us -> 55.2 us (0.952)
  starting transfers between devices: 26.5 us -> 19.9 us
  waiting for transfers between devices: 13.2 us -> 19.7 us
  local copies, waits for them, and re-layouts: 6.91 us -> 3.57 us
  Pallas kernels: 9.43 us -> 10.1 us
    ppermute x18 -> x16, starting transfers between devices: 26.5 us -> 19.9 us  [swap(): return lax.ppermute(x, 'chol', [(i, i ^ mask) for i in range(n)])]
    ppermute x18 -> x16, waiting for transfers between devices: 13.2 us -> 19.7 us  [swap(): return lax.ppermute(x, 'chol', [(i, i ^ mask) for i in range(n)])]
    unnamed x7 -> x5, local copies, waits for them, and re-layouts: 4.63 us -> 1.25 us
    pallas_call x1, Pallas kernels: 5.92 us -> 6.57 us  [mean_part(): pl.pallas_call(functools.partial(mean_kernel, parts), in_specs=[pl.BlockS...]
  transfers between devices with their start and end apart: 18 -> 16, of which waited for: 8 -> 8; matrix products, arithmetic and copies ran while one was open for 4% -> 5% of each run, Pallas kernels for 10% -> 12%
where the time goes in v4:
time: 55.2 us; the launch traced here: 55 us
  starting transfers between devices  19.9 us (36%)
  waiting for transfers between devices  19.7 us (36%)
  Pallas kernels  10.1 us (18%)
  local copies, waits for them, and re-layouts  3.57 us (6%)
  other arithmetic  1.43 us (3%)
    ppermute x16, starting transfers between devices, swap(): return lax.ppermute(x, 'chol', [(i, i ^ mask) for i in range(n)])  19.9 us
    ppermute x16, waiting for transfers between devices, swap(): return lax.ppermute(x, 'chol', [(i, i ^ mask) for i in range(n)])  19.7 us
    pallas_call x1, Pallas kernels, mean_part(): pl.pallas_call(functools.partial(mean_kernel, parts), in_specs=[pl.BlockS...  6.57 us
    pallas_call x1, Pallas kernels, partial_bias(): pl.pallas_call(functools.partial(bias_kernel, tile), in_specs=[pl.BlockSp...  3.44 us
    unnamed x5, local copies, waits for them, and re-layouts  1.25 us
  transfers between devices with their start and end apart: 16, of which 8 were waited for; matrix products, arithmetic and copies ran while one was open for 5% of the time, Pallas kernels for 12%

profile of v4, /device:TPU:0, one launch (start us, length us, event | category | flops | bytes accessed | tf_op | source)
XLA Modules:
  0.0 55.0 jit_solution(13139709210145957710)
XLA Ops:
  0.0 0.0 copy-start
  0.0 1.2 %copy-done = bf16[16,32768]{1,0:T(8,128)(2,1)S(1)} copy-done((bf16[16,32768]{1,0:T(8,128)(2,1)S(1)}, bf16[16,32768]{1,0:T(8,128)(2,1)}, u32[]{:S(2)}) %copy-start) | copy-done | bytes 1048600
  1.2 0.1 shard_map.55
  1.3 3.0 %collective-permute-start = (bf16[32,2048]{1,0:T(8,128)(2,1)S(1)}, bf16[32,2048]{1,0:T(8,128)(2,1)S(1)}, u32[]{:S(2)}, u32[]{:S(2)}) collective-permute-start(bf16[32,2048]{1,0:T(8,128)(2,1)S(1)} %get-tuple-element.23), channel_id=1, source_target_pairs={{0,2},{1,3},{2,0},{3,1},{4,6},{5,7},{6,4},{7,5},{8,10},{9,11},{10,... | collective-permute-start | bytes 393224 | tf_op jit(solution)/shard_map/ppermute | solution.py:24
  4.3 1.6 %collective-permute-start.1 = (bf16[32,2048]{1,0:T(8,128)(2,1)S(1)}, bf16[32,2048]{1,0:T(8,128)(2,1)S(1)}, u32[]{:S(2)}, u32[]{:S(2)}) collective-permute-start(bf16[32,2048]{1,0:T(8,128)(2,1)S(1)} %get-tuple-element.24), channel_id=1, source_target_pairs={{0,4},{1,5},{2,6},{3,7},{4,0},{5,1},{6,2},{7,3},{8,12},{9,13},{10,... | collective-permute-start | bytes 393224 | tf_op jit(solution)/shard_map/ppermute | solution.py:24
  5.9 2.6 %collective-permute-start.3 = (bf16[32,2048]{1,0:T(8,128)(2,1)S(1)}, bf16[32,2048]{1,0:T(8,128)(2,1)S(1)}, u32[]{:S(2)}, u32[]{:S(2)}) collective-permute-start(bf16[32,2048]{1,0:T(8,128)(2,1)S(1)} %get-tuple-element.27), channel_id=1, source_target_pairs={{0,8},{1,9},{2,10},{3,11},{4,12},{5,13},{6,14},{7,15},{8,0},{9,1},... | collective-permute-start | bytes 393224 | tf_op jit(solution)/shard_map/ppermute | solution.py:24
  8.5 0.2 collective-permute-start.5
  8.7 0.8 %reshape.395 = s32[16,16]{1,0:T(8,128)S(1)} reshape(s32[256]{0:T(256)} %param.8) | data formatting | bytes 2048 | tf_op jit(solution)/shard_map/reshape | solution.py:180
  9.5 0.6 %gather_fusion = s32[16,16]{1,0:T(8,128)S(1)} fusion(s32[16,16]{1,0:T(8,128)S(1)} %reshape.395, s32[1024]{0:T(1024)S(1)} %pad_clamp_fusion), kind=kCustom, calls=%fused_computation | custom fusion | bytes 2112 | tf_op jit(solution)/shard_map/gather | solution.py:180
  10.1 0.1 reshape.424
  10.2 0.2 fusion.4.index_ref
  10.4 0.0 collective-permute-done
  10.5 0.7 %collective-permute-start.2 = (bf16[32,2048]{1,0:T(8,128)(2,1)S(1)}, bf16[32,2048]{1,0:T(8,128)(2,1)S(1)}, u32[]{:S(2)}, u32[]{:S(2)}) collective-permute-start(bf16[32,2048]{1,0:T(8,128)(2,1)S(1)} %get-tuple-element.26), channel_id=1, source_target_pairs={{0,6},{1,7},{2,4},{3,5},{4,2},{5,3},{6,0},{7,1},{8,14},{9,15},{10,... | collective-permute-start | bytes 393224 | tf_op jit(solution)/shard_map/ppermute | solution.py:24
  11.1 0.0 collective-permute-done.1
  11.1 0.7 %broadcast_in_dim.4.mean_ref = bf16[1,2048]{1,0:T(2,128)(2,1)S(1)} reshape(bf16[2048]{0:T(1024)(128)(2,1)} %param.6) | data formatting | bytes 8192 | tf_op jit(solution)/shard_map/broadcast_in_dim | solution.py:189
  11.8 4.4 %collective-permute-start.4 = (bf16[32,2048]{1,0:T(8,128)(2,1)S(1)}, bf16[32,2048]{1,0:T(8,128)(2,1)S(1)}, u32[]{:S(2)}, u32[]{:S(2)}) collective-permute-start(bf16[32,2048]{1,0:T(8,128)(2,1)S(1)} %get-tuple-element.29), channel_id=1, source_target_pairs={{0,10},{1,11},{2,8},{3,9},{4,14},{5,15},{6,12},{7,13},{8,2},{9,3},... | collective-permute-start | bytes 393224 | tf_op jit(solution)/shard_map/ppermute | solution.py:24
  16.3 6.6 %shard_map.56 = (f32[1,2048]{1,0:T(1,128)S(1)}, bf16[2048,2048]{1,0:T(8,128)(2,1)S(1)}) custom-call(bf16[2048,2048]{1,0:T(8,128)(2,1)} %chol_ref.1, bf16[1,2048]{1,0:T(2,128)(2,1)S(1)} %broadcast_in_dim.4.mean_ref), custom_call_target="tpu_custom_call" | custom-call | flops 67108864 | bytes 8388608 | tf_op jit(solution)/shard_map/pallas_call | solution.py:84
  22.9 0.1 collective-permute-start.9
  23.0 0.0 collective-permute-done.2
  23.0 0.1 collective-permute-start.6
  23.1 0.0 collective-permute-done.3
  23.1 0.6 %collective-permute-start.7 = (bf16[64,2048]{1,0:T(8,128)(2,1)S(1)}, bf16[64,2048]{1,0:T(8,128)(2,1)S(1)}, u32[]{:S(2)}, u32[]{:S(2)}) collective-permute-start(bf16[64,2048]{1,0:T(8,128)(2,1)S(1)} %pad_maximum_fusion), channel_id=1, source_target_pairs={{0,1},{1,0},{2,3},{3,2},{4,5},{5,4},{6,7},{7,6},{8,9},{9,8},{10,11... | collective-permute-start | bytes 786440 | tf_op jit(solution)/shard_map/ppermute | solution.py:24
  23.7 1.8 %collective-permute-done.4 = bf16[32,2048]{1,0:T(8,128)(2,1)S(1)} collective-permute-done((bf16[32,2048]{1,0:T(8,128)(2,1)S(1)}, bf16[32,2048]{1,0:T(8,128)(2,1)S(1)}, u32[]{:S(2)}, u32[]{:S(2)}) %collective-permute-start.4) | collective-permute-done | bytes 131104 | tf_op jit(solution)/shard_map/ppermute | solution.py:24
  25.5 0.0 collective-permute-done.5
  25.6 6.1 %collective-permute-done.6 = bf16[32,2048]{1,0:T(8,128)(2,1)S(1)} collective-permute-done((bf16[32,2048]{1,0:T(8,128)(2,1)S(1)}, bf16[32,2048]{1,0:T(8,128)(2,1)S(1)}, u32[]{:S(2)}, u32[]{:S(2)}) %collective-permute-start.6) | collective-permute-done | bytes 131104 | tf_op jit(solution)/shard_map/ppermute | solution.py:24
  31.7 0.1 collective-permute-start.8
  31.8 0.0 collective-permute-done.9
  31.8 0.0 collective-permute-done.7
  31.8 1.5 %collective-permute-done.8 = bf16[64,2048]{1,0:T(8,128)(2,1)S(1)} collective-permute-done((bf16[64,2048]{1,0:T(8,128)(2,1)S(1)}, bf16[64,2048]{1,0:T(8,128)(2,1)S(1)}, u32[]{:S(2)}, u32[]{:S(2)}) %collective-permute-start.8) | collective-permute-done | bytes 262176 | tf_op jit(solution)/shard_map/ppermute | solution.py:24
  33.3 0.0 copy-start.1
  33.3 3.4 %shard_map.57 = (f32[128,2048]{1,0:T(8,128)S(1)}, bf16[128,2048]{1,0:T(8,128)(2,1)S(1)}) custom-call(s32[256,1]{1,0:T(8,128)S(1)} %fusion.4.index_ref, bf16[256,2048]{1,0:T(8,128)(2,1)S(1)} %constant_dynamic-update-slice_fusion.rows_ref, bf16[2048,2048]{1,0:T(8,128)(2,1)S(1)} %get-tuple-element.36.chol_ref), custom_call_target="tpu_custom_call" | custom-call | flops 2415919104 | bytes 11010048 | tf_op jit(solution)/shard_map/pallas_call | solution.py:121
  36.8 0.2 collective-permute-start.10
  37.0 1.8 %collective-permute-done.10 = bf16[128,2048]{1,0:T(8,128)(2,1)S(1)} collective-permute-done((bf16[128,2048]{1,0:T(8,128)(2,1)S(1)}, bf16[128,2048]{1,0:T(8,128)(2,1)S(1)}, u32[]{:S(2)}, u32[]{:S(2)}) %collective-permute-start.10) | collective-permute-done | bytes 524320 | tf_op jit(solution)/shard_map/ppermute | solution.py:24
  38.8 0.2 fusion.29
  39.0 1.4 %collective-permute-start.11 = (f16[16,2176]{1,0:T(8,128)(2,1)S(1)}, f16[16,2176]{1,0:T(8,128)(2,1)S(1)}, u32[]{:S(2)}, u32[]{:S(2)}) collective-permute-start(f16[16,2176]{1,0:T(8,128)(2,1)S(1)} %pad_maximum_fusion.4), channel_id=1, source_target_pairs={{0,6},{1,7},{2,4},{3,5},{4,2},{5,3},{6,0},{7,1},{8,14},{9,15},{10,... | collective-permute-start | bytes 208904 | tf_op jit(solution)/shard_map/ppermute | solution.py:24
  40.4 0.1 pad_maximum_fusion.3
  40.5 0.1 collective-permute-start.12
  40.6 2.1 %collective-permute-start.13 = (f16[32,2176]{1,0:T(8,128)(2,1)S(1)}, f16[32,2176]{1,0:T(8,128)(2,1)S(1)}, u32[]{:S(2)}, u32[]{:S(2)}) collective-permute-start(f16[32,2176]{1,0:T(8,128)(2,1)S(1)} %get-tuple-element.66), channel_id=1, source_target_pairs={{0,4},{1,5},{2,6},{3,7},{4,0},{5,1},{6,2},{7,3},{8,12},{9,13},{10,... | collective-permute-start | bytes 417800 | tf_op jit(solution)/shard_map/ppermute | solution.py:24
  42.8 1.7 %collective-permute-done.11 = f16[16,2176]{1,0:T(8,128)(2,1)S(1)} collective-permute-done((f16[16,2176]{1,0:T(8,128)(2,1)S(1)}, f16[16,2176]{1,0:T(8,128)(2,1)S(1)}, u32[]{:S(2)}, u32[]{:S(2)}) %collective-permute-start.11) | collective-permute-done | bytes 69664 | tf_op jit(solution)/shard_map/ppermute | solution.py:24
  44.5 2.7 %collective-permute-done.12 = f16[32,2176]{1,0:T(8,128)(2,1)S(1)} collective-permute-done((f16[32,2176]{1,0:T(8,128)(2,1)S(1)}, f16[32,2176]{1,0:T(8,128)(2,1)S(1)}, u32[]{:S(2)}, u32[]{:S(2)}) %collective-permute-start.12) | collective-permute-done | bytes 139296 | tf_op jit(solution)/shard_map/ppermute | solution.py:24
  47.2 0.0 collective-permute-done.13
  47.4 1.1 %collective-permute-start.14 = (f16[16,2176]{1,0:T(8,128)(2,1)S(1)}, f16[16,2176]{1,0:T(8,128)(2,1)S(1)}, u32[]{:S(2)}, u32[]{:S(2)}) collective-permute-start(f16[16,2176]{1,0:T(8,128)(2,1)S(1)} %pad_maximum_fusion.5), channel_id=1, source_target_pairs={{0,8},{1,9},{2,10},{3,11},{4,12},{5,13},{6,14},{7,15},{8,0},{9,1},... | collective-permute-start | bytes 208904 | tf_op jit(solution)/shard_map/ppermute | solution.py:24
  48.5 1.6 %collective-permute-start.15 = (f16[16,2048]{1,0:T(8,128)(2,1)S(1)}, f16[16,2048]{1,0:T(8,128)(2,1)S(1)}, u32[]{:S(2)}, u32[]{:S(2)}) collective-permute-start(f16[16,2048]{1,0:T(8,128)(2,1)S(1)} %get-tuple-element.45), channel_id=1, source_target_pairs={{0,6},{1,7},{2,4},{3,5},{4,2},{5,3},{6,0},{7,1},{8,14},{9,15},{10,... | collective-permute-start | bytes 196616 | tf_op jit(solution)/shard_map/ppermute | solution.py:24
  50.1 3.3 %collective-permute-done.14 = f16[16,2176]{1,0:T(8,128)(2,1)S(1)} collective-permute-done((f16[16,2176]{1,0:T(8,128)(2,1)S(1)}, f16[16,2176]{1,0:T(8,128)(2,1)S(1)}, u32[]{:S(2)}, u32[]{:S(2)}) %collective-permute-start.14) | collective-permute-done | bytes 69664 | tf_op jit(solution)/shard_map/ppermute | solution.py:24
  53.4 0.8 %collective-permute-done.15 = f16[16,2048]{1,0:T(8,128)(2,1)S(1)} collective-permute-done((f16[16,2048]{1,0:T(8,128)(2,1)S(1)}, f16[16,2048]{1,0:T(8,128)(2,1)S(1)}, u32[]{:S(2)}, u32[]{:S(2)}) %collective-permute-start.15) | collective-permute-done | bytes 65568 | tf_op jit(solution)/shard_map/ppermute | solution.py:24
  54.3 0.0 copy-done.1
  54.3 0.7 %fusion.9 = f32[16,2048]{1,0:T(8,128)} fusion(f32[16,2048]{1,0:T(8,128)S(1)} %copy-done.1, f32[1,16,2176]{2,1,0:T(8,128)S(1)} %bitcast_convert_fusion, f32[2,16,2048]{2,1,0:T(8,128)S(1)} %slice_add_fusion, f16[16,2048]{1,0:T(8,128)(2,1)S(1)} %collective-permute-done.15, f32[2048]{0:T(1024)S(1)} %fusion.18), kind=kLoop, calls=%fused_computation.28 | loop fusion | flops 163840 | bytes 598016 | tf_op jit(solution)/shard_map/sub | solution.py:195
  (30 shorter events, 0.5 us)
Async XLA Ops:
  0.0 1.2 %copy-start = (bf16[16,32768]{1,0:T(8,128)(2,1)S(1)}, bf16[16,32768]{1,0:T(8,128)(2,1)}, u32[]{:S(2)}) copy-start(bf16[16,32768]{1,0:T(8,128)(2,1)} %greens_ref.1) | copy-start | bytes 3145732
  1.3 9.2 %collective-permute-start = (bf16[32,2048]{1,0:T(8,128)(2,1)S(1)}, bf16[32,2048]{1,0:T(8,128)(2,1)S(1)}, u32[]{:S(2)}, u32[]{:S(2)}) collective-permute-start(bf16[32,2048]{1,0:T(8,128)(2,1)S(1)} %get-tuple-element.23), channel_id=1, source_target_pairs={{0,2},{1,3},{2,0},{3,1},{4,6},{5,7},{6,4},{7,5},{8,10},{9,11},{10,... | collective-permute-start | bytes 393224 | tf_op jit(solution)/shard_map/ppermute | solution.py:24
  4.3 6.8 %collective-permute-start.1 = (bf16[32,2048]{1,0:T(8,128)(2,1)S(1)}, bf16[32,2048]{1,0:T(8,128)(2,1)S(1)}, u32[]{:S(2)}, u32[]{:S(2)}) collective-permute-start(bf16[32,2048]{1,0:T(8,128)(2,1)S(1)} %get-tuple-element.24), channel_id=1, source_target_pairs={{0,4},{1,5},{2,6},{3,7},{4,0},{5,1},{6,2},{7,3},{8,12},{9,13},{10,... | collective-permute-start | bytes 393224 | tf_op jit(solution)/shard_map/ppermute | solution.py:24
  5.9 17.2 %collective-permute-start.3 = (bf16[32,2048]{1,0:T(8,128)(2,1)S(1)}, bf16[32,2048]{1,0:T(8,128)(2,1)S(1)}, u32[]{:S(2)}, u32[]{:S(2)}) collective-permute-start(bf16[32,2048]{1,0:T(8,128)(2,1)S(1)} %get-tuple-element.27), channel_id=1, source_target_pairs={{0,8},{1,9},{2,10},{3,11},{4,12},{5,13},{6,14},{7,15},{8,0},{9,1},... | collective-permute-start | bytes 393224 | tf_op jit(solution)/shard_map/ppermute | solution.py:24
  8.5 17.0 %collective-permute-start.5 = (bf16[32,2048]{1,0:T(8,128)(2,1)S(1)}, bf16[32,2048]{1,0:T(8,128)(2,1)S(1)}, u32[]{:S(2)}, u32[]{:S(2)}) collective-permute-start(bf16[32,2048]{1,0:T(8,128)(2,1)S(1)} %get-tuple-element.30), channel_id=1, source_target_pairs={{0,12},{1,13},{2,14},{3,15},{4,8},{5,9},{6,10},{7,11},{8,4},{9,5},... | collective-permute-start | bytes 393224 | tf_op jit(solution)/shard_map/ppermute | solution.py:24
  10.5 12.5 %collective-permute-start.2 = (bf16[32,2048]{1,0:T(8,128)(2,1)S(1)}, bf16[32,2048]{1,0:T(8,128)(2,1)S(1)}, u32[]{:S(2)}, u32[]{:S(2)}) collective-permute-start(bf16[32,2048]{1,0:T(8,128)(2,1)S(1)} %get-tuple-element.26), channel_id=1, source_target_pairs={{0,6},{1,7},{2,4},{3,5},{4,2},{5,3},{6,0},{7,1},{8,14},{9,15},{10,... | collective-permute-start | bytes 393224 | tf_op jit(solution)/shard_map/ppermute | solution.py:24
  11.8 13.7 %collective-permute-start.4 = (bf16[32,2048]{1,0:T(8,128)(2,1)S(1)}, bf16[32,2048]{1,0:T(8,128)(2,1)S(1)}, u32[]{:S(2)}, u32[]{:S(2)}) collective-permute-start(bf16[32,2048]{1,0:T(8,128)(2,1)S(1)} %get-tuple-element.29), channel_id=1, source_target_pairs={{0,10},{1,11},{2,8},{3,9},{4,14},{5,15},{6,12},{7,13},{8,2},{9,3},... | collective-permute-start | bytes 393224 | tf_op jit(solution)/shard_map/ppermute | solution.py:24
  22.9 8.9 %collective-permute-start.9 = (f32[16,128]{1,0:T(8,128)S(1)}, f32[16,128]{1,0:T(8,128)S(1)}, u32[]{:S(2)}, u32[]{:S(2)}) collective-permute-start(f32[16,128]{1,0:T(8,128)S(1)} %bitcast.60), channel_id=1, source_target_pairs={{0,1},{1,0},{2,3},{3,2},{4,5},{5,4},{6,7},{7,6},{8,9},{9,8},{10,11... | collective-permute-start | bytes 24584 | tf_op jit(solution)/shard_map/ppermute | solution.py:24
  23.0 8.7 %collective-permute-start.6 = (bf16[32,2048]{1,0:T(8,128)(2,1)S(1)}, bf16[32,2048]{1,0:T(8,128)(2,1)S(1)}, u32[]{:S(2)}, u32[]{:S(2)}) collective-permute-start(bf16[32,2048]{1,0:T(8,128)(2,1)S(1)} %get-tuple-element.32), channel_id=1, source_target_pairs={{0,14},{1,15},{2,12},{3,13},{4,10},{5,11},{6,8},{7,9},{8,6},{9,7},... | collective-permute-start | bytes 393224 | tf_op jit(solution)/shard_map/ppermute | solution.py:24
  23.1 8.7 %collective-permute-start.7 = (bf16[64,2048]{1,0:T(8,128)(2,1)S(1)}, bf16[64,2048]{1,0:T(8,128)(2,1)S(1)}, u32[]{:S(2)}, u32[]{:S(2)}) collective-permute-start(bf16[64,2048]{1,0:T(8,128)(2,1)S(1)} %pad_maximum_fusion), channel_id=1, source_target_pairs={{0,1},{1,0},{2,3},{3,2},{4,5},{5,4},{6,7},{7,6},{8,9},{9,8},{10,11... | collective-permute-start | bytes 786440 | tf_op jit(solution)/shard_map/ppermute | solution.py:24
  31.7 1.6 %collective-permute-start.8 = (bf16[64,2048]{1,0:T(8,128)(2,1)S(1)}, bf16[64,2048]{1,0:T(8,128)(2,1)S(1)}, u32[]{:S(2)}, u32[]{:S(2)}) collective-permute-start(bf16[64,2048]{1,0:T(8,128)(2,1)S(1)} %pad_maximum_fusion.1), channel_id=1, source_target_pairs={{0,1},{1,0},{2,3},{3,2},{4,5},{5,4},{6,7},{7,6},{8,9},{9,8},{10,11... | collective-permute-start | bytes 786440 | tf_op jit(solution)/shard_map/ppermute | solution.py:24
  33.3 20.9 %copy-start.1 = (f32[16,2048]{1,0:T(8,128)S(1)}, f32[16,2048]{1,0:T(8,128)}, u32[]{:S(2)}) copy-start(f32[16,2048]{1,0:T(8,128)} %param.9) | copy-start | bytes 393220
  36.8 2.0 %collective-permute-start.10 = (bf16[128,2048]{1,0:T(8,128)(2,1)S(1)}, bf16[128,2048]{1,0:T(8,128)(2,1)S(1)}, u32[]{:S(2)}, u32[]{:S(2)}) collective-permute-start(bf16[128,2048]{1,0:T(8,128)(2,1)S(1)} %get-tuple-element.38), channel_id=1, source_target_pairs={{0,1},{1,0},{2,3},{3,2},{4,5},{5,4},{6,7},{7,6},{8,9},{9,8},{10,11... | collective-permute-start | bytes 1572872 | tf_op jit(solution)/shard_map/ppermute | solution.py:24
  39.0 5.4 %collective-permute-start.11 = (f16[16,2176]{1,0:T(8,128)(2,1)S(1)}, f16[16,2176]{1,0:T(8,128)(2,1)S(1)}, u32[]{:S(2)}, u32[]{:S(2)}) collective-permute-start(f16[16,2176]{1,0:T(8,128)(2,1)S(1)} %pad_maximum_fusion.4), channel_id=1, source_target_pairs={{0,6},{1,7},{2,4},{3,5},{4,2},{5,3},{6,0},{7,1},{8,14},{9,15},{10,... | collective-permute-start | bytes 208904 | tf_op jit(solution)/shard_map/ppermute | solution.py:24
  40.5 6.7 %collective-permute-start.12 = (f16[32,2176]{1,0:T(8,128)(2,1)S(1)}, f16[32,2176]{1,0:T(8,128)(2,1)S(1)}, u32[]{:S(2)}, u32[]{:S(2)}) collective-permute-start(f16[32,2176]{1,0:T(8,128)(2,1)S(1)} %get-tuple-element.65), channel_id=1, source_target_pairs={{0,2},{1,3},{2,0},{3,1},{4,6},{5,7},{6,4},{7,5},{8,10},{9,11},{10,... | collective-permute-start | bytes 417800 | tf_op jit(solution)/shard_map/ppermute | solution.py:24
  40.6 6.6 %collective-permute-start.13 = (f16[32,2176]{1,0:T(8,128)(2,1)S(1)}, f16[32,2176]{1,0:T(8,128)(2,1)S(1)}, u32[]{:S(2)}, u32[]{:S(2)}) collective-permute-start(f16[32,2176]{1,0:T(8,128)(2,1)S(1)} %get-tuple-element.66), channel_id=1, source_target_pairs={{0,4},{1,5},{2,6},{3,7},{4,0},{5,1},{6,2},{7,3},{8,12},{9,13},{10,... | collective-permute-start | bytes 417800 | tf_op jit(solution)/shard_map/ppermute | solution.py:24
  47.4 6.0 %collective-permute-start.14 = (f16[16,2176]{1,0:T(8,128)(2,1)S(1)}, f16[16,2176]{1,0:T(8,128)(2,1)S(1)}, u32[]{:S(2)}, u32[]{:S(2)}) collective-permute-start(f16[16,2176]{1,0:T(8,128)(2,1)S(1)} %pad_maximum_fusion.5), channel_id=1, source_target_pairs={{0,8},{1,9},{2,10},{3,11},{4,12},{5,13},{6,14},{7,15},{8,0},{9,1},... | collective-permute-start | bytes 208904 | tf_op jit(solution)/shard_map/ppermute | solution.py:24
  48.5 5.7 %collective-permute-start.15 = (f16[16,2048]{1,0:T(8,128)(2,1)S(1)}, f16[16,2048]{1,0:T(8,128)(2,1)S(1)}, u32[]{:S(2)}, u32[]{:S(2)}) collective-permute-start(f16[16,2048]{1,0:T(8,128)(2,1)S(1)} %get-tuple-element.45), channel_id=1, source_target_pairs={{0,6},{1,7},{2,4},{3,5},{4,2},{5,3},{6,0},{7,1},{8,14},{9,15},{10,... | collective-permute-start | bytes 196616 | tf_op jit(solution)/shard_map/ppermute | solution.py:24

commit v5 on v4

--- a/solution.py
+++ b/solution.py
@@ -26,41 +26,53 @@
 
 def split_kernel(greens_ref, *outs):
     me = lax.axis_index("chol")
-    own, pairs = greens_ref.shape[0], outs[0].shape[1]
-    for m, out in enumerate(outs):
+    own = greens_ref.shape[0]
+    pairs = outs[0].shape[1]
+    far = len(outs) - 2
+    for m in range(2 * far):
         for j in range(2):
             there = pl.multiple_of(jnp.bitwise_xor(me, 2 * m + j) * pairs, pairs)
-            out[pl.ds(j * own, own), :] = greens_ref[:, pl.ds(there, pairs)]
-
-
-def split_by_chip(greens, chips):
+            out, at = (outs[j], m) if m < far else (outs[2 + m - far], j)
+            out[pl.ds(at * own, own), :] = greens_ref[:, pl.ds(there, pairs)]
+
+
+def split_by_device(greens, n):
     own, total = greens.shape
-    shape = (2 * own, total // (2 * chips))
-    return pl.pallas_call(
+    pairs = total // n
+    shapes = [(n // 4 * own, pairs)] * 2 + [(2 * own, pairs)] * (n // 4)
+    outs = pl.pallas_call(
         split_kernel,
         in_specs=[pl.BlockSpec(memory_space=pltpu.VMEM)],
-        out_specs=[pl.BlockSpec(memory_space=pltpu.VMEM)] * chips,
-        out_shape=[jax.ShapeDtypeStruct(shape, greens.dtype)] * chips,
+        out_specs=[pl.BlockSpec(memory_space=pltpu.VMEM)] * len(shapes),
+        out_shape=[jax.ShapeDtypeStruct(shape, greens.dtype) for shape in shapes],
         compiler_params=pltpu.CompilerParams(vmem_limit_bytes=8 * 2**20),
         cost_estimate=pl.CostEstimate(flops=0, bytes_accessed=4 * greens.size, transcendentals=0),
     )(greens)
+    return outs[0], outs[1], outs[2:]
 
 
 def after(x, *others):
     return lax.optimization_barrier((x,) + others)[0]
 
 
-def collect_walkers(greens, chips, n):
-    own = greens.shape[0]
-    sent = split_by_chip(greens, chips)
-    waits = {3: 1, 5: 2, 7: 3} if chips == 8 else {}
+def collect_walkers(greens, n):
+    own, half = greens.shape[0], n // 4
+    near, other, far = split_by_device(greens, n)
+    other = swap(other, 1, n)
+    block = lambda x, i: x[i * own : (i + 1) * own]
+    sent = [jnp.concatenate([block(near, i), block(other, i)]) for i in range(half)] + list(far)
+    waits = {5: 1, 7: 2} if half == 4 else {}
     got = [sent[0]]
-    for m in range(1, chips):
+    for m in range(1, 2 * half):
         message = after(sent[m], got[waits[m]]) if m in waits else sent[m]
         got.append(swap(message, 2 * m, n))
-    near, far = got[: chips // 2], got[chips // 2 :]
-    passed = [swap(jnp.concatenate([x[own:] for x in part]), 1, n) for part in (near, far)]
-    return jnp.concatenate([x[:own] for x in got] + passed), got[chips // 4]
+    passed = swap(jnp.concatenate([x[own:] for x in got[half:]]), 1, n)
+    return jnp.concatenate(got[:half] + [x[:own] for x in got[half:]] + [passed]), got[1]
+
+
+def place_of_source(source, n):
+    far = n // 2 + (source % 2) * (n // 4) + (source - n // 2) // 2
+    return jnp.where(source < n // 2, source, far)
 
 
 def mean_kernel(parts, chol_ref, mean_ref, part_ref, staged_ref, sems):
@@ -69,10 +81,13 @@
     for t in range(parts):
         at = pl.ds(t * step, step)
         copies.append(pltpu.make_async_copy(chol_ref.at[at], staged_ref.at[at], sems.at[t]))
-        copies[-1].start()
+    for copy in copies[:2]:
+        copy.start()
     mean = jnp.broadcast_to(mean_ref[...], (8, mean_ref.shape[1]))
     for t, copy in enumerate(copies):
         copy.wait()
+        if t + 2 < parts:
+            copies[t + 2].start()
         at = pl.ds(t * step, step)
         part = lax.dot_general(
             mean, staged_ref[at, :], (((1,), (1,)), ((), ())), preferred_element_type=F32
@@ -80,7 +95,7 @@
         part_ref[:, at] = part[:1]
 
 
-def mean_part(chol, mean, parts=8):
+def mean_part(chol, mean, parts=4):
     return pl.pallas_call(
         functools.partial(mean_kernel, parts),
         in_specs=[pl.BlockSpec(memory_space=pl.ANY), pl.BlockSpec(memory_space=pltpu.VMEM)],
@@ -179,14 +194,15 @@
     owners = jnp.bitwise_xor(relative, me)
     index = walker_order.reshape(n, own)[owners].reshape(-1)
 
+    mean_row = mean_greens[None, :]
     if chips <= DIRECT_CHIPS:
-        rows, ended = collect_walkers(greens, chips, n)
-        mean_greens = after(mean_greens, ended)
+        rows, ended = collect_walkers(greens, n)
+        mean_row = after(mean_row, ended)
         source = jnp.bitwise_xor(index // own, me)
-        index = ((source % 2) * chips + source // 2) * own + index % own
+        index = place_of_source(source, n) * own + index % own
     else:
         rows = lax.all_to_all(greens, "chol", split_axis=1, concat_axis=0, tiled=True)
-    mean, chol = mean_part(chol_vectors, mean_greens[None, :])
+    mean, chol = mean_part(chol_vectors, mean_row)
     mean = mean.reshape(own, -1)
     mean = mean + swap(mean, 1, n)
     keep, send = partial_bias(index[:, None], after(rows, mean), chol, 512)

time: 55.2 us -> 53.8 us (0.975)
  starting transfers between devices: 19.9 us -> 24.6 us
  waiting for transfers between devices: 19.7 us -> 15.5 us
  Pallas kernels: 10.1 us -> 8.2 us
    ppermute x16, starting transfers between devices: 19.9 us -> 24.6 us  [swap(): return lax.ppermute(x, 'chol', [(i, i ^ mask) for i in range(n)])]
    ppermute x16, waiting for transfers between devices: 19.7 us -> 15.5 us  [swap(): return lax.ppermute(x, 'chol', [(i, i ^ mask) for i in range(n)])]
    pallas_call x1, Pallas kernels: 6.57 us -> 4.7 us  [mean_part(): pl.pallas_call(functools.partial(mean_kernel, parts), in_specs=[pl.BlockS...]
    unnamed x5 -> x7, local copies, waits for them, and re-layouts: 1.25 us -> 1.26 us
  transfers between devices with their start and end apart: 16 -> 16, of which waited for: 8 -> 9; matrix products, arithmetic and copies ran while one was open for 5% -> 5% of each run, Pallas kernels for 12% -> 9%
where the time goes in v5:
time: 53.8 us; the launch traced here: 53.6 us
  starting transfers between devices  24.6 us (46%)
  waiting for transfers between devices  15.5 us (29%)
  Pallas kernels  8.2 us (15%)
  local copies, waits for them, and re-layouts  3.58 us (7%)
  other arithmetic  1.47 us (3%)
    ppermute x16, starting transfers between devices, swap(): return lax.ppermute(x, 'chol', [(i, i ^ mask) for i in range(n)])  24.6 us
    ppermute x16, waiting for transfers between devices, swap(): return lax.ppermute(x, 'chol', [(i, i ^ mask) for i in range(n)])  15.5 us
    pallas_call x1, Pallas kernels, mean_part(): pl.pallas_call(functools.partial(mean_kernel, parts), in_specs=[pl.BlockS...  4.7 us
    pallas_call x1, Pallas kernels, partial_bias(): pl.pallas_call(functools.partial(bias_kernel, tile), in_specs=[pl.BlockSp...  3.44 us
    unnamed x7, local copies, waits for them, and re-layouts  1.26 us
  transfers between devices with their start and end apart: 16, of which 9 were waited for; matrix products, arithmetic and copies ran while one was open for 5% of the time, Pallas kernels for 9%

profile of v5, /device:TPU:0, one launch (start us, length us, event | category | flops | bytes accessed | tf_op | source)
XLA Modules:
  0.0 53.6 jit_solution(6956716008537896764)
XLA Ops:
  0.0 0.0 copy-start
  0.0 1.2 %copy-done = bf16[16,32768]{1,0:T(8,128)(2,1)S(1)} copy-done((bf16[16,32768]{1,0:T(8,128)(2,1)S(1)}, bf16[16,32768]{1,0:T(8,128)(2,1)}, u32[]{:S(2)}) %copy-start) | copy-done | bytes 1048600
  1.2 0.1 shard_map.55
  1.3 4.1 %collective-permute-start.4 = (bf16[32,2048]{1,0:T(8,128)(2,1)S(1)}, bf16[32,2048]{1,0:T(8,128)(2,1)S(1)}, u32[]{:S(2)}, u32[]{:S(2)}) collective-permute-start(bf16[32,2048]{1,0:T(8,128)(2,1)S(1)} %get-tuple-element.21), channel_id=1, source_target_pairs={{0,8},{1,9},{2,10},{3,11},{4,12},{5,13},{6,14},{7,15},{8,0},{9,1},... | collective-permute-start | bytes 393224 | tf_op jit(solution)/shard_map/ppermute | solution.py:24
  5.4 1.3 %collective-permute-start.6 = (bf16[32,2048]{1,0:T(8,128)(2,1)S(1)}, bf16[32,2048]{1,0:T(8,128)(2,1)S(1)}, u32[]{:S(2)}, u32[]{:S(2)}) collective-permute-start(bf16[32,2048]{1,0:T(8,128)(2,1)S(1)} %get-tuple-element.24), channel_id=1, source_target_pairs={{0,12},{1,13},{2,14},{3,15},{4,8},{5,9},{6,10},{7,11},{8,4},{9,5},... | collective-permute-start | bytes 393224 | tf_op jit(solution)/shard_map/ppermute | solution.py:24
  6.7 0.0 collective-permute-start
  6.8 0.7 %broadcast_in_dim.4.mean_ref = bf16[1,2048]{1,0:T(2,128)(2,1)S(1)} reshape(bf16[2048]{0:T(1024)(128)(2,1)} %param.6) | data formatting | bytes 8192 | tf_op jit(solution)/shard_map/broadcast_in_dim | solution.py:197
  7.5 0.8 %reshape.421 = s32[16,16]{1,0:T(8,128)S(1)} reshape(s32[256]{0:T(256)} %param.8) | data formatting | bytes 2048 | tf_op jit(solution)/shard_map/reshape | solution.py:195
  8.2 0.6 %gather_fusion = s32[16,16]{1,0:T(8,128)S(1)} fusion(s32[16,16]{1,0:T(8,128)S(1)} %reshape.421, s32[1024]{0:T(1024)S(1)} %pad_clamp_fusion), kind=kCustom, calls=%fused_computation | custom fusion | bytes 2112 | tf_op jit(solution)/shard_map/gather | solution.py:195
  8.8 0.1 reshape.450
  8.9 0.0 collective-permute-done
  9.0 1.6 %collective-permute-start.1 = (bf16[32,2048]{1,0:T(8,128)(2,1)S(1)}, bf16[32,2048]{1,0:T(8,128)(2,1)S(1)}, u32[]{:S(2)}, u32[]{:S(2)}) collective-permute-start(bf16[32,2048]{1,0:T(8,128)(2,1)S(1)} %pad_maximum_fusion.3), channel_id=1, source_target_pairs={{0,2},{1,3},{2,0},{3,1},{4,6},{5,7},{6,4},{7,5},{8,10},{9,11},{10,... | collective-permute-start | bytes 393224 | tf_op jit(solution)/shard_map/ppermute | solution.py:24
  10.6 0.3 collective-permute-start.2
  10.9 1.8 %collective-permute-start.3 = (bf16[32,2048]{1,0:T(8,128)(2,1)S(1)}, bf16[32,2048]{1,0:T(8,128)(2,1)S(1)}, u32[]{:S(2)}, u32[]{:S(2)}) collective-permute-start(bf16[32,2048]{1,0:T(8,128)(2,1)S(1)} %pad_maximum_fusion.5), channel_id=1, source_target_pairs={{0,6},{1,7},{2,4},{3,5},{4,2},{5,3},{6,0},{7,1},{8,14},{9,15},{10,... | collective-permute-start | bytes 393224 | tf_op jit(solution)/shard_map/ppermute | solution.py:24
  12.7 2.3 %collective-permute-done.1 = bf16[32,2048]{1,0:T(8,128)(2,1)S(1)} collective-permute-done((bf16[32,2048]{1,0:T(8,128)(2,1)S(1)}, bf16[32,2048]{1,0:T(8,128)(2,1)S(1)}, u32[]{:S(2)}, u32[]{:S(2)}) %collective-permute-start.1) | collective-permute-done | bytes 131104 | tf_op jit(solution)/shard_map/ppermute | solution.py:24
  15.0 2.6 %collective-permute-start.5 = (bf16[32,2048]{1,0:T(8,128)(2,1)S(1)}, bf16[32,2048]{1,0:T(8,128)(2,1)S(1)}, u32[]{:S(2)}, u32[]{:S(2)}) collective-permute-start(bf16[32,2048]{1,0:T(8,128)(2,1)S(1)} %get-tuple-element.23), channel_id=1, source_target_pairs={{0,10},{1,11},{2,8},{3,9},{4,14},{5,15},{6,12},{7,13},{8,2},{9,3},... | collective-permute-start | bytes 393224 | tf_op jit(solution)/shard_map/ppermute | solution.py:24
  17.6 0.0 collective-permute-done.2
  17.6 4.3 %collective-permute-start.7 = (bf16[32,2048]{1,0:T(8,128)(2,1)S(1)}, bf16[32,2048]{1,0:T(8,128)(2,1)S(1)}, u32[]{:S(2)}, u32[]{:S(2)}) collective-permute-start(bf16[32,2048]{1,0:T(8,128)(2,1)S(1)} %get-tuple-element.26), channel_id=1, source_target_pairs={{0,14},{1,15},{2,12},{3,13},{4,10},{5,11},{6,8},{7,9},{8,6},{9,7},... | collective-permute-start | bytes 393224 | tf_op jit(solution)/shard_map/ppermute | solution.py:24
  21.9 4.7 %shard_map.56 = (f32[1,2048]{1,0:T(1,128)S(1)}, bf16[2048,2048]{1,0:T(8,128)(2,1)S(1)}) custom-call(bf16[2048,2048]{1,0:T(8,128)(2,1)} %chol_ref.1, bf16[1,2048]{1,0:T(2,128)(2,1)S(1)} %broadcast_in_dim.4.mean_ref), custom_call_target="tpu_custom_call" | custom-call | flops 67108864 | bytes 8388608 | tf_op jit(solution)/shard_map/pallas_call | solution.py:99
  26.7 0.0 collective-permute-done.3
  26.7 0.1 collective-permute-start.9
  26.8 0.0 collective-permute-done.4
  26.8 1.6 %collective-permute-done.5 = bf16[32,2048]{1,0:T(8,128)(2,1)S(1)} collective-permute-done((bf16[32,2048]{1,0:T(8,128)(2,1)S(1)}, bf16[32,2048]{1,0:T(8,128)(2,1)S(1)}, u32[]{:S(2)}, u32[]{:S(2)}) %collective-permute-start.5) | collective-permute-done | bytes 131104 | tf_op jit(solution)/shard_map/ppermute | solution.py:24
  28.4 0.0 collective-permute-done.6
  28.4 0.0 collective-permute-done.7
  28.5 0.1 collective-permute-start.8
  28.5 0.3 fusion.6.index_ref
  28.8 0.0 collective-permute-done.9
  28.9 1.2 %collective-permute-done.8 = bf16[64,2048]{1,0:T(8,128)(2,1)S(1)} collective-permute-done((bf16[64,2048]{1,0:T(8,128)(2,1)S(1)}, bf16[64,2048]{1,0:T(8,128)(2,1)S(1)}, u32[]{:S(2)}, u32[]{:S(2)}) %collective-permute-start.8) | collective-permute-done | bytes 262176 | tf_op jit(solution)/shard_map/ppermute | solution.py:24
  30.1 0.0 copy-start.1
  30.1 3.4 %shard_map.57 = (f32[128,2048]{1,0:T(8,128)S(1)}, bf16[128,2048]{1,0:T(8,128)(2,1)S(1)}) custom-call(s32[256,1]{1,0:T(8,128)S(1)} %fusion.6.index_ref, bf16[256,2048]{1,0:T(8,128)(2,1)S(1)} %constant_dynamic-update-slice_fusion.rows_ref, bf16[2048,2048]{1,0:T(8,128)(2,1)S(1)} %get-tuple-element.30.chol_ref), custom_call_target="tpu_custom_call" | custom-call | flops 2415919104 | bytes 11010048 | tf_op jit(solution)/shard_map/pallas_call | solution.py:136
  33.6 0.2 collective-permute-start.10
  33.8 1.8 %collective-permute-done.10 = bf16[128,2048]{1,0:T(8,128)(2,1)S(1)} collective-permute-done((bf16[128,2048]{1,0:T(8,128)(2,1)S(1)}, bf16[128,2048]{1,0:T(8,128)(2,1)S(1)}, u32[]{:S(2)}, u32[]{:S(2)}) %collective-permute-start.10) | collective-permute-done | bytes 524320 | tf_op jit(solution)/shard_map/ppermute | solution.py:24
  35.5 0.2 fusion.29
  35.8 3.5 %collective-permute-start.11 = (f16[16,2176]{1,0:T(8,128)(2,1)S(1)}, f16[16,2176]{1,0:T(8,128)(2,1)S(1)}, u32[]{:S(2)}, u32[]{:S(2)}) collective-permute-start(f16[16,2176]{1,0:T(8,128)(2,1)S(1)} %pad_maximum_fusion.6), channel_id=1, source_target_pairs={{0,6},{1,7},{2,4},{3,5},{4,2},{5,3},{6,0},{7,1},{8,14},{9,15},{10,... | collective-permute-start | bytes 208904 | tf_op jit(solution)/shard_map/ppermute | solution.py:24
  39.3 0.1 pad_maximum_fusion.2
  39.4 0.6 %collective-permute-start.12 = (f16[32,2176]{1,0:T(8,128)(2,1)S(1)}, f16[32,2176]{1,0:T(8,128)(2,1)S(1)}, u32[]{:S(2)}, u32[]{:S(2)}) collective-permute-start(f16[32,2176]{1,0:T(8,128)(2,1)S(1)} %get-tuple-element.59), channel_id=1, source_target_pairs={{0,2},{1,3},{2,0},{3,1},{4,6},{5,7},{6,4},{7,5},{8,10},{9,11},{10,... | collective-permute-start | bytes 417800 | tf_op jit(solution)/shard_map/ppermute | solution.py:24
  40.0 0.1 collective-permute-start.13
  40.0 1.8 %collective-permute-done.11 = f16[16,2176]{1,0:T(8,128)(2,1)S(1)} collective-permute-done((f16[16,2176]{1,0:T(8,128)(2,1)S(1)}, f16[16,2176]{1,0:T(8,128)(2,1)S(1)}, u32[]{:S(2)}, u32[]{:S(2)}) %collective-permute-start.11) | collective-permute-done | bytes 69664 | tf_op jit(solution)/shard_map/ppermute | solution.py:24
  41.9 3.0 %collective-permute-done.12 = f16[32,2176]{1,0:T(8,128)(2,1)S(1)} collective-permute-done((f16[32,2176]{1,0:T(8,128)(2,1)S(1)}, f16[32,2176]{1,0:T(8,128)(2,1)S(1)}, u32[]{:S(2)}, u32[]{:S(2)}) %collective-permute-start.12) | collective-permute-done | bytes 139296 | tf_op jit(solution)/shard_map/ppermute | solution.py:24
  44.9 0.2 collective-permute-done.13
  45.3 2.5 %collective-permute-start.14 = (f16[16,2176]{1,0:T(8,128)(2,1)S(1)}, f16[16,2176]{1,0:T(8,128)(2,1)S(1)}, u32[]{:S(2)}, u32[]{:S(2)}) collective-permute-start(f16[16,2176]{1,0:T(8,128)(2,1)S(1)} %pad_maximum_fusion.7), channel_id=1, source_target_pairs={{0,8},{1,9},{2,10},{3,11},{4,12},{5,13},{6,14},{7,15},{8,0},{9,1},... | collective-permute-start | bytes 208904 | tf_op jit(solution)/shard_map/ppermute | solution.py:24
  47.7 1.6 %collective-permute-start.15 = (f16[16,2048]{1,0:T(8,128)(2,1)S(1)}, f16[16,2048]{1,0:T(8,128)(2,1)S(1)}, u32[]{:S(2)}, u32[]{:S(2)}) collective-permute-start(f16[16,2048]{1,0:T(8,128)(2,1)S(1)} %get-tuple-element.39), channel_id=1, source_target_pairs={{0,6},{1,7},{2,4},{3,5},{4,2},{5,3},{6,0},{7,1},{8,14},{9,15},{10,... | collective-permute-start | bytes 196616 | tf_op jit(solution)/shard_map/ppermute | solution.py:24
  49.3 1.3 %collective-permute-done.14 = f16[16,2176]{1,0:T(8,128)(2,1)S(1)} collective-permute-done((f16[16,2176]{1,0:T(8,128)(2,1)S(1)}, f16[16,2176]{1,0:T(8,128)(2,1)S(1)}, u32[]{:S(2)}, u32[]{:S(2)}) %collective-permute-start.14) | collective-permute-done | bytes 69664 | tf_op jit(solution)/shard_map/ppermute | solution.py:24
  50.6 2.3 %collective-permute-done.15 = f16[16,2048]{1,0:T(8,128)(2,1)S(1)} collective-permute-done((f16[16,2048]{1,0:T(8,128)(2,1)S(1)}, f16[16,2048]{1,0:T(8,128)(2,1)S(1)}, u32[]{:S(2)}, u32[]{:S(2)}) %collective-permute-start.15) | collective-permute-done | bytes 65568 | tf_op jit(solution)/shard_map/ppermute | solution.py:24
  52.9 0.0 copy-done.1
  52.9 0.7 %fusion.12 = f32[16,2048]{1,0:T(8,128)} fusion(f32[16,2048]{1,0:T(8,128)S(1)} %copy-done.1, f32[1,16,2176]{2,1,0:T(8,128)S(1)} %bitcast_convert_fusion, f32[2,16,2048]{2,1,0:T(8,128)S(1)} %slice_add_fusion, f16[16,2048]{1,0:T(8,128)(2,1)S(1)} %collective-permute-done.15, f32[2048]{0:T(1024)S(1)} %fusion.18), kind=kLoop, calls=%fused_computation.33 | loop fusion | flops 163840 | bytes 598016 | tf_op jit(solution)/shard_map/sub | solution.py:211
  (32 shorter events, 0.5 us)
Async XLA Ops:
  0.0 1.2 %copy-start = (bf16[16,32768]{1,0:T(8,128)(2,1)S(1)}, bf16[16,32768]{1,0:T(8,128)(2,1)}, u32[]{:S(2)}) copy-start(bf16[16,32768]{1,0:T(8,128)(2,1)} %greens_ref.1) | copy-start | bytes 3145732
  1.3 25.5 %collective-permute-start.4 = (bf16[32,2048]{1,0:T(8,128)(2,1)S(1)}, bf16[32,2048]{1,0:T(8,128)(2,1)S(1)}, u32[]{:S(2)}, u32[]{:S(2)}) collective-permute-start(bf16[32,2048]{1,0:T(8,128)(2,1)S(1)} %get-tuple-element.21), channel_id=1, source_target_pairs={{0,8},{1,9},{2,10},{3,11},{4,12},{5,13},{6,14},{7,15},{8,0},{9,1},... | collective-permute-start | bytes 393224 | tf_op jit(solution)/shard_map/ppermute | solution.py:24
  5.4 23.0 %collective-permute-start.6 = (bf16[32,2048]{1,0:T(8,128)(2,1)S(1)}, bf16[32,2048]{1,0:T(8,128)(2,1)S(1)}, u32[]{:S(2)}, u32[]{:S(2)}) collective-permute-start(bf16[32,2048]{1,0:T(8,128)(2,1)S(1)} %get-tuple-element.24), channel_id=1, source_target_pairs={{0,12},{1,13},{2,14},{3,15},{4,8},{5,9},{6,10},{7,11},{8,4},{9,5},... | collective-permute-start | bytes 393224 | tf_op jit(solution)/shard_map/ppermute | solution.py:24
  6.7 2.2 %collective-permute-start = (bf16[64,2048]{1,0:T(8,128)(2,1)S(1)}, bf16[64,2048]{1,0:T(8,128)(2,1)S(1)}, u32[]{:S(2)}, u32[]{:S(2)}) collective-permute-start(bf16[64,2048]{1,0:T(8,128)(2,1)S(1)} %get-tuple-element.20), channel_id=1, source_target_pairs={{0,1},{1,0},{2,3},{3,2},{4,5},{5,4},{6,7},{7,6},{8,9},{9,8},{10,11... | collective-permute-start | bytes 786440 | tf_op jit(solution)/shard_map/ppermute | solution.py:24
  9.0 6.0 %collective-permute-start.1 = (bf16[32,2048]{1,0:T(8,128)(2,1)S(1)}, bf16[32,2048]{1,0:T(8,128)(2,1)S(1)}, u32[]{:S(2)}, u32[]{:S(2)}) collective-permute-start(bf16[32,2048]{1,0:T(8,128)(2,1)S(1)} %pad_maximum_fusion.3), channel_id=1, source_target_pairs={{0,2},{1,3},{2,0},{3,1},{4,6},{5,7},{6,4},{7,5},{8,10},{9,11},{10,... | collective-permute-start | bytes 393224 | tf_op jit(solution)/shard_map/ppermute | solution.py:24
  10.6 7.0 %collective-permute-start.2 = (bf16[32,2048]{1,0:T(8,128)(2,1)S(1)}, bf16[32,2048]{1,0:T(8,128)(2,1)S(1)}, u32[]{:S(2)}, u32[]{:S(2)}) collective-permute-start(bf16[32,2048]{1,0:T(8,128)(2,1)S(1)} %pad_maximum_fusion.4), channel_id=1, source_target_pairs={{0,4},{1,5},{2,6},{3,7},{4,0},{5,1},{6,2},{7,3},{8,12},{9,13},{10,... | collective-permute-start | bytes 393224 | tf_op jit(solution)/shard_map/ppermute | solution.py:24
  10.9 15.8 %collective-permute-start.3 = (bf16[32,2048]{1,0:T(8,128)(2,1)S(1)}, bf16[32,2048]{1,0:T(8,128)(2,1)S(1)}, u32[]{:S(2)}, u32[]{:S(2)}) collective-permute-start(bf16[32,2048]{1,0:T(8,128)(2,1)S(1)} %pad_maximum_fusion.5), channel_id=1, source_target_pairs={{0,6},{1,7},{2,4},{3,5},{4,2},{5,3},{6,0},{7,1},{8,14},{9,15},{10,... | collective-permute-start | bytes 393224 | tf_op jit(solution)/shard_map/ppermute | solution.py:24
  15.0 13.4 %collective-permute-start.5 = (bf16[32,2048]{1,0:T(8,128)(2,1)S(1)}, bf16[32,2048]{1,0:T(8,128)(2,1)S(1)}, u32[]{:S(2)}, u32[]{:S(2)}) collective-permute-start(bf16[32,2048]{1,0:T(8,128)(2,1)S(1)} %get-tuple-element.23), channel_id=1, source_target_pairs={{0,10},{1,11},{2,8},{3,9},{4,14},{5,15},{6,12},{7,13},{8,2},{9,3},... | collective-permute-start | bytes 393224 | tf_op jit(solution)/shard_map/ppermute | solution.py:24
  17.6 10.8 %collective-permute-start.7 = (bf16[32,2048]{1,0:T(8,128)(2,1)S(1)}, bf16[32,2048]{1,0:T(8,128)(2,1)S(1)}, u32[]{:S(2)}, u32[]{:S(2)}) collective-permute-start(bf16[32,2048]{1,0:T(8,128)(2,1)S(1)} %get-tuple-element.26), channel_id=1, source_target_pairs={{0,14},{1,15},{2,12},{3,13},{4,10},{5,11},{6,8},{7,9},{8,6},{9,7},... | collective-permute-start | bytes 393224 | tf_op jit(solution)/shard_map/ppermute | solution.py:24
  26.7 2.2 %collective-permute-start.9 = (f32[16,128]{1,0:T(8,128)S(1)}, f32[16,128]{1,0:T(8,128)S(1)}, u32[]{:S(2)}, u32[]{:S(2)}) collective-permute-start(f32[16,128]{1,0:T(8,128)S(1)} %bitcast.60), channel_id=1, source_target_pairs={{0,1},{1,0},{2,3},{3,2},{4,5},{5,4},{6,7},{7,6},{8,9},{9,8},{10,11... | collective-permute-start | bytes 24584 | tf_op jit(solution)/shard_map/ppermute | solution.py:24
  28.5 1.6 %collective-permute-start.8 = (bf16[64,2048]{1,0:T(8,128)(2,1)S(1)}, bf16[64,2048]{1,0:T(8,128)(2,1)S(1)}, u32[]{:S(2)}, u32[]{:S(2)}) collective-permute-start(bf16[64,2048]{1,0:T(8,128)(2,1)S(1)} %pad_maximum_fusion), channel_id=1, source_target_pairs={{0,1},{1,0},{2,3},{3,2},{4,5},{5,4},{6,7},{7,6},{8,9},{9,8},{10,11... | collective-permute-start | bytes 786440 | tf_op jit(solution)/shard_map/ppermute | solution.py:24
  30.1 22.8 %copy-start.1 = (f32[16,2048]{1,0:T(8,128)S(1)}, f32[16,2048]{1,0:T(8,128)}, u32[]{:S(2)}) copy-start(f32[16,2048]{1,0:T(8,128)} %param.9) | copy-start | bytes 393220
  33.6 2.0 %collective-permute-start.10 = (bf16[128,2048]{1,0:T(8,128)(2,1)S(1)}, bf16[128,2048]{1,0:T(8,128)(2,1)S(1)}, u32[]{:S(2)}, u32[]{:S(2)}) collective-permute-start(bf16[128,2048]{1,0:T(8,128)(2,1)S(1)} %get-tuple-element.32), channel_id=1, source_target_pairs={{0,1},{1,0},{2,3},{3,2},{4,5},{5,4},{6,7},{7,6},{8,9},{9,8},{10,11... | collective-permute-start | bytes 1572872 | tf_op jit(solution)/shard_map/ppermute | solution.py:24
  35.8 6.0 %collective-permute-start.11 = (f16[16,2176]{1,0:T(8,128)(2,1)S(1)}, f16[16,2176]{1,0:T(8,128)(2,1)S(1)}, u32[]{:S(2)}, u32[]{:S(2)}) collective-permute-start(f16[16,2176]{1,0:T(8,128)(2,1)S(1)} %pad_maximum_fusion.6), channel_id=1, source_target_pairs={{0,6},{1,7},{2,4},{3,5},{4,2},{5,3},{6,0},{7,1},{8,14},{9,15},{10,... | collective-permute-start | bytes 208904 | tf_op jit(solution)/shard_map/ppermute | solution.py:24
  39.4 5.5 %collective-permute-start.12 = (f16[32,2176]{1,0:T(8,128)(2,1)S(1)}, f16[32,2176]{1,0:T(8,128)(2,1)S(1)}, u32[]{:S(2)}, u32[]{:S(2)}) collective-permute-start(f16[32,2176]{1,0:T(8,128)(2,1)S(1)} %get-tuple-element.59), channel_id=1, source_target_pairs={{0,2},{1,3},{2,0},{3,1},{4,6},{5,7},{6,4},{7,5},{8,10},{9,11},{10,... | collective-permute-start | bytes 417800 | tf_op jit(solution)/shard_map/ppermute | solution.py:24
  40.0 5.2 %collective-permute-start.13 = (f16[32,2176]{1,0:T(8,128)(2,1)S(1)}, f16[32,2176]{1,0:T(8,128)(2,1)S(1)}, u32[]{:S(2)}, u32[]{:S(2)}) collective-permute-start(f16[32,2176]{1,0:T(8,128)(2,1)S(1)} %get-tuple-element.60), channel_id=1, source_target_pairs={{0,4},{1,5},{2,6},{3,7},{4,0},{5,1},{6,2},{7,3},{8,12},{9,13},{10,... | collective-permute-start | bytes 417800 | tf_op jit(solution)/shard_map/ppermute | solution.py:24
  45.3 5.3 %collective-permute-start.14 = (f16[16,2176]{1,0:T(8,128)(2,1)S(1)}, f16[16,2176]{1,0:T(8,128)(2,1)S(1)}, u32[]{:S(2)}, u32[]{:S(2)}) collective-permute-start(f16[16,2176]{1,0:T(8,128)(2,1)S(1)} %pad_maximum_fusion.7), channel_id=1, source_target_pairs={{0,8},{1,9},{2,10},{3,11},{4,12},{5,13},{6,14},{7,15},{8,0},{9,1},... | collective-permute-start | bytes 208904 | tf_op jit(solution)/shard_map/ppermute | solution.py:24
  47.7 5.2 %collective-permute-start.15 = (f16[16,2048]{1,0:T(8,128)(2,1)S(1)}, f16[16,2048]{1,0:T(8,128)(2,1)S(1)}, u32[]{:S(2)}, u32[]{:S(2)}) collective-permute-start(f16[16,2048]{1,0:T(8,128)(2,1)S(1)} %get-tuple-element.39), channel_id=1, source_target_pairs={{0,6},{1,7},{2,4},{3,5},{4,2},{5,3},{6,0},{7,1},{8,14},{9,15},{10,... | collective-permute-start | bytes 196616 | tf_op jit(solution)/shard_map/ppermute | solution.py:24

commit v6 on v5

--- a/solution.py
+++ b/solution.py
@@ -66,8 +66,8 @@
     for m in range(1, 2 * half):
         message = after(sent[m], got[waits[m]]) if m in waits else sent[m]
         got.append(swap(message, 2 * m, n))
-    passed = swap(jnp.concatenate([x[own:] for x in got[half:]]), 1, n)
-    return jnp.concatenate(got[:half] + [x[:own] for x in got[half:]] + [passed]), got[1]
+    passed = [swap(jnp.concatenate([x[own:] for x in part]), 1, n) for part in (got[half:-1], got[-1:])]
+    return jnp.concatenate(got[:half] + [x[:own] for x in got[half:]] + passed), got[1]
 
 
 def place_of_source(source, n):
@@ -120,9 +120,8 @@
         chosen.astype(BF16), rows_ref[...], preferred_element_type=F32
     ).astype(BF16)
 
-    @pl.loop(0, nchol // tile)
-    def _(t):
-        at = pl.ds(pl.multiple_of(t * tile, tile), tile)
+    for t in range(nchol // tile):
+        at = pl.ds(t * tile, tile)
         part = lax.dot_general(
             picked[...], chol_ref[at, :], (((1,), (1,)), ((), ())), preferred_element_type=F32
         )

time: 53.8 us -> 53 us (0.985)
  Pallas kernels: 8.2 us -> 7.4 us
    pallas_call x1, Pallas kernels: 3.44 us -> 2.63 us  [partial_bias(): pl.pallas_call(functools.partial(bias_kernel, tile), in_specs=[pl.BlockSp...]
    ppermute x16 -> x17, waiting for transfers between devices: 15.5 us -> 15.3 us  [swap(): return lax.ppermute(x, 'chol', [(i, i ^ mask) for i in range(n)])]
    ppermute x16 -> x17, starting transfers between devices: 24.6 us -> 24.8 us  [swap(): return lax.ppermute(x, 'chol', [(i, i ^ mask) for i in range(n)])]
    unnamed x7 -> x8, local copies, waits for them, and re-layouts: 1.26 us -> 1.27 us
  transfers between devices with their start and end apart: 16 -> 17, of which waited for: 9 -> 11; matrix products, arithmetic and copies ran while one was open for 5% -> 5% of each run, Pallas kernels for 9% -> 9%
where the time goes in v6:
time: 53 us; the launch traced here: 52.8 us
  starting transfers between devices  24.8 us (47%)
  waiting for transfers between devices  15.3 us (29%)
  Pallas kernels  7.4 us (14%)
  local copies, waits for them, and re-layouts  3.58 us (7%)
  other arithmetic  1.46 us (3%)
    ppermute x17, starting transfers between devices, swap(): return lax.ppermute(x, 'chol', [(i, i ^ mask) for i in range(n)])  24.8 us
    ppermute x17, waiting for transfers between devices, swap(): return lax.ppermute(x, 'chol', [(i, i ^ mask) for i in range(n)])  15.3 us
    pallas_call x1, Pallas kernels, mean_part(): pl.pallas_call(functools.partial(mean_kernel, parts), in_specs=[pl.BlockS...  4.7 us
    pallas_call x1, Pallas kernels, partial_bias(): pl.pallas_call(functools.partial(bias_kernel, tile), in_specs=[pl.BlockSp...  2.63 us
    unnamed x8, local copies, waits for them, and re-layouts  1.27 us
  transfers between devices with their start and end apart: 17, of which 11 were waited for; matrix products, arithmetic and copies ran while one was open for 5% of the time, Pallas kernels for 9%

profile of v6, /device:TPU:0, one launch (start us, length us, event | category | flops | bytes accessed | tf_op | source)
XLA Modules:
  0.0 52.8 jit_solution(8471525164254238203)
XLA Ops:
  0.0 0.0 copy-start
  0.0 1.2 %copy-done = bf16[16,32768]{1,0:T(8,128)(2,1)S(1)} copy-done((bf16[16,32768]{1,0:T(8,128)(2,1)S(1)}, bf16[16,32768]{1,0:T(8,128)(2,1)}, u32[]{:S(2)}) %copy-start) | copy-done | bytes 1048600
  1.2 0.1 shard_map.55
  1.3 4.1 %collective-permute-start.4 = (bf16[32,2048]{1,0:T(8,128)(2,1)S(1)}, bf16[32,2048]{1,0:T(8,128)(2,1)S(1)}, u32[]{:S(2)}, u32[]{:S(2)}) collective-permute-start(bf16[32,2048]{1,0:T(8,128)(2,1)S(1)} %get-tuple-element.21), channel_id=1, source_target_pairs={{0,8},{1,9},{2,10},{3,11},{4,12},{5,13},{6,14},{7,15},{8,0},{9,1},... | collective-permute-start | bytes 393224 | tf_op jit(solution)/shard_map/ppermute | solution.py:24
  5.4 1.3 %collective-permute-start.6 = (bf16[32,2048]{1,0:T(8,128)(2,1)S(1)}, bf16[32,2048]{1,0:T(8,128)(2,1)S(1)}, u32[]{:S(2)}, u32[]{:S(2)}) collective-permute-start(bf16[32,2048]{1,0:T(8,128)(2,1)S(1)} %get-tuple-element.24), channel_id=1, source_target_pairs={{0,12},{1,13},{2,14},{3,15},{4,8},{5,9},{6,10},{7,11},{8,4},{9,5},... | collective-permute-start | bytes 393224 | tf_op jit(solution)/shard_map/ppermute | solution.py:24
  6.7 0.0 collective-permute-start
  6.8 0.7 %broadcast_in_dim.4.mean_ref = bf16[1,2048]{1,0:T(2,128)(2,1)S(1)} reshape(bf16[2048]{0:T(1024)(128)(2,1)} %param.6) | data formatting | bytes 8192 | tf_op jit(solution)/shard_map/broadcast_in_dim | solution.py:196
  7.5 0.8 %reshape.421 = s32[16,16]{1,0:T(8,128)S(1)} reshape(s32[256]{0:T(256)} %param.8) | data formatting | bytes 2048 | tf_op jit(solution)/shard_map/reshape | solution.py:194
  8.3 0.6 %gather_fusion = s32[16,16]{1,0:T(8,128)S(1)} fusion(s32[16,16]{1,0:T(8,128)S(1)} %reshape.421, s32[1024]{0:T(1024)S(1)} %pad_clamp_fusion), kind=kCustom, calls=%fused_computation | custom fusion | bytes 2112 | tf_op jit(solution)/shard_map/gather | solution.py:194
  8.8 0.1 reshape.450
  8.9 0.3 fusion.6.index_ref
  9.2 0.0 collective-permute-done
  9.3 1.6 %collective-permute-start.1 = (bf16[32,2048]{1,0:T(8,128)(2,1)S(1)}, bf16[32,2048]{1,0:T(8,128)(2,1)S(1)}, u32[]{:S(2)}, u32[]{:S(2)}) collective-permute-start(bf16[32,2048]{1,0:T(8,128)(2,1)S(1)} %pad_maximum_fusion.3), channel_id=1, source_target_pairs={{0,2},{1,3},{2,0},{3,1},{4,6},{5,7},{6,4},{7,5},{8,10},{9,11},{10,... | collective-permute-start | bytes 393224 | tf_op jit(solution)/shard_map/ppermute | solution.py:24
  10.9 0.3 collective-permute-start.2
  11.2 1.8 %collective-permute-start.3 = (bf16[32,2048]{1,0:T(8,128)(2,1)S(1)}, bf16[32,2048]{1,0:T(8,128)(2,1)S(1)}, u32[]{:S(2)}, u32[]{:S(2)}) collective-permute-start(bf16[32,2048]{1,0:T(8,128)(2,1)S(1)} %pad_maximum_fusion.5), channel_id=1, source_target_pairs={{0,6},{1,7},{2,4},{3,5},{4,2},{5,3},{6,0},{7,1},{8,14},{9,15},{10,... | collective-permute-start | bytes 393224 | tf_op jit(solution)/shard_map/ppermute | solution.py:24
  13.0 2.3 %collective-permute-done.1 = bf16[32,2048]{1,0:T(8,128)(2,1)S(1)} collective-permute-done((bf16[32,2048]{1,0:T(8,128)(2,1)S(1)}, bf16[32,2048]{1,0:T(8,128)(2,1)S(1)}, u32[]{:S(2)}, u32[]{:S(2)}) %collective-permute-start.1) | collective-permute-done | bytes 131104 | tf_op jit(solution)/shard_map/ppermute | solution.py:24
  15.2 2.6 %collective-permute-start.5 = (bf16[32,2048]{1,0:T(8,128)(2,1)S(1)}, bf16[32,2048]{1,0:T(8,128)(2,1)S(1)}, u32[]{:S(2)}, u32[]{:S(2)}) collective-permute-start(bf16[32,2048]{1,0:T(8,128)(2,1)S(1)} %get-tuple-element.23), channel_id=1, source_target_pairs={{0,10},{1,11},{2,8},{3,9},{4,14},{5,15},{6,12},{7,13},{8,2},{9,3},... | collective-permute-start | bytes 393224 | tf_op jit(solution)/shard_map/ppermute | solution.py:24
  17.9 0.0 collective-permute-done.2
  17.9 4.0 %collective-permute-start.7 = (bf16[32,2048]{1,0:T(8,128)(2,1)S(1)}, bf16[32,2048]{1,0:T(8,128)(2,1)S(1)}, u32[]{:S(2)}, u32[]{:S(2)}) collective-permute-start(bf16[32,2048]{1,0:T(8,128)(2,1)S(1)} %get-tuple-element.26), channel_id=1, source_target_pairs={{0,14},{1,15},{2,12},{3,13},{4,10},{5,11},{6,8},{7,9},{8,6},{9,7},... | collective-permute-start | bytes 393224 | tf_op jit(solution)/shard_map/ppermute | solution.py:24
  21.9 4.7 %shard_map.56 = (f32[1,2048]{1,0:T(1,128)S(1)}, bf16[2048,2048]{1,0:T(8,128)(2,1)S(1)}) custom-call(bf16[2048,2048]{1,0:T(8,128)(2,1)} %chol_ref.1, bf16[1,2048]{1,0:T(2,128)(2,1)S(1)} %broadcast_in_dim.4.mean_ref), custom_call_target="tpu_custom_call" | custom-call | flops 67108864 | bytes 8388608 | tf_op jit(solution)/shard_map/pallas_call | solution.py:99
  26.6 0.0 collective-permute-done.3
  26.6 0.1 collective-permute-start.10
  26.7 0.0 collective-permute-done.4
  26.8 1.1 %collective-permute-done.10 = f32[16,128]{1,0:T(8,128)S(1)} collective-permute-done((f32[16,128]{1,0:T(8,128)S(1)}, f32[16,128]{1,0:T(8,128)S(1)}, u32[]{:S(2)}, u32[]{:S(2)}) %collective-permute-start.10) | collective-permute-done | bytes 8224 | tf_op jit(solution)/shard_map/ppermute | solution.py:24
  27.9 0.8 %collective-permute-done.5 = bf16[32,2048]{1,0:T(8,128)(2,1)S(1)} collective-permute-done((bf16[32,2048]{1,0:T(8,128)(2,1)S(1)}, bf16[32,2048]{1,0:T(8,128)(2,1)S(1)}, u32[]{:S(2)}, u32[]{:S(2)}) %collective-permute-start.5) | collective-permute-done | bytes 131104 | tf_op jit(solution)/shard_map/ppermute | solution.py:24
  28.7 0.0 collective-permute-done.6
  28.7 0.1 collective-permute-start.8
  28.8 0.0 collective-permute-done.7
  28.8 0.5 %collective-permute-start.9 = (bf16[16,2048]{1,0:T(8,128)(2,1)S(1)}, bf16[16,2048]{1,0:T(8,128)(2,1)S(1)}, u32[]{:S(2)}, u32[]{:S(2)}) collective-permute-start(bf16[16,2048]{1,0:T(8,128)(2,1)S(1)} %get-tuple-element.51), channel_id=1, source_target_pairs={{0,1},{1,0},{2,3},{3,2},{4,5},{5,4},{6,7},{7,6},{8,9},{9,8},{10,11... | collective-permute-start | bytes 196616 | tf_op jit(solution)/shard_map/ppermute | solution.py:24
  29.4 0.8 %collective-permute-done.8 = bf16[48,2048]{1,0:T(8,128)(2,1)S(1)} collective-permute-done((bf16[48,2048]{1,0:T(8,128)(2,1)S(1)}, bf16[48,2048]{1,0:T(8,128)(2,1)S(1)}, u32[]{:S(2)}, u32[]{:S(2)}) %collective-permute-start.8) | collective-permute-done | bytes 196640 | tf_op jit(solution)/shard_map/ppermute | solution.py:24
  30.2 0.1 collective-permute-done.9
  30.3 0.0 copy-start.1
  30.3 2.6 %shard_map.57 = (f32[128,2048]{1,0:T(8,128)S(1)}, bf16[128,2048]{1,0:T(8,128)(2,1)S(1)}) custom-call(s32[256,1]{1,0:T(8,128)S(1)} %fusion.6.index_ref, bf16[256,2048]{1,0:T(8,128)(2,1)S(1)} %constant_dynamic-update-slice_fusion.rows_ref, bf16[2048,2048]{1,0:T(8,128)(2,1)S(1)} %get-tuple-element.30.chol_ref), custom_call_target="tpu_custom_call" | custom-call | flops 2415919104 | bytes 11010048 | tf_op jit(solution)/shard_map/pallas_call | solution.py:135
  33.0 0.4 collective-permute-start.11
  33.4 1.6 %collective-permute-done.11 = bf16[128,2048]{1,0:T(8,128)(2,1)S(1)} collective-permute-done((bf16[128,2048]{1,0:T(8,128)(2,1)S(1)}, bf16[128,2048]{1,0:T(8,128)(2,1)S(1)}, u32[]{:S(2)}, u32[]{:S(2)}) %collective-permute-start.11) | collective-permute-done | bytes 524320 | tf_op jit(solution)/shard_map/ppermute | solution.py:24
  34.9 0.2 fusion.29
  35.2 3.2 %collective-permute-start.12 = (f16[16,2176]{1,0:T(8,128)(2,1)S(1)}, f16[16,2176]{1,0:T(8,128)(2,1)S(1)}, u32[]{:S(2)}, u32[]{:S(2)}) collective-permute-start(f16[16,2176]{1,0:T(8,128)(2,1)S(1)} %pad_maximum_fusion.6), channel_id=1, source_target_pairs={{0,6},{1,7},{2,4},{3,5},{4,2},{5,3},{6,0},{7,1},{8,14},{9,15},{10,... | collective-permute-start | bytes 208904 | tf_op jit(solution)/shard_map/ppermute | solution.py:24
  38.4 0.1 pad_maximum_fusion.2
  38.5 0.6 %collective-permute-start.13 = (f16[32,2176]{1,0:T(8,128)(2,1)S(1)}, f16[32,2176]{1,0:T(8,128)(2,1)S(1)}, u32[]{:S(2)}, u32[]{:S(2)}) collective-permute-start(f16[32,2176]{1,0:T(8,128)(2,1)S(1)} %get-tuple-element.59), channel_id=1, source_target_pairs={{0,2},{1,3},{2,0},{3,1},{4,6},{5,7},{6,4},{7,5},{8,10},{9,11},{10,... | collective-permute-start | bytes 417800 | tf_op jit(solution)/shard_map/ppermute | solution.py:24
  39.1 0.1 collective-permute-start.14
  39.2 1.8 %collective-permute-done.12 = f16[16,2176]{1,0:T(8,128)(2,1)S(1)} collective-permute-done((f16[16,2176]{1,0:T(8,128)(2,1)S(1)}, f16[16,2176]{1,0:T(8,128)(2,1)S(1)}, u32[]{:S(2)}, u32[]{:S(2)}) %collective-permute-start.12) | collective-permute-done | bytes 69664 | tf_op jit(solution)/shard_map/ppermute | solution.py:24
  41.0 3.0 %collective-permute-done.13 = f16[32,2176]{1,0:T(8,128)(2,1)S(1)} collective-permute-done((f16[32,2176]{1,0:T(8,128)(2,1)S(1)}, f16[32,2176]{1,0:T(8,128)(2,1)S(1)}, u32[]{:S(2)}, u32[]{:S(2)}) %collective-permute-start.13) | collective-permute-done | bytes 139296 | tf_op jit(solution)/shard_map/ppermute | solution.py:24
  44.1 0.2 collective-permute-done.14
  44.4 2.5 %collective-permute-start.15 = (f16[16,2176]{1,0:T(8,128)(2,1)S(1)}, f16[16,2176]{1,0:T(8,128)(2,1)S(1)}, u32[]{:S(2)}, u32[]{:S(2)}) collective-permute-start(f16[16,2176]{1,0:T(8,128)(2,1)S(1)} %pad_maximum_fusion.7), channel_id=1, source_target_pairs={{0,8},{1,9},{2,10},{3,11},{4,12},{5,13},{6,14},{7,15},{8,0},{9,1},... | collective-permute-start | bytes 208904 | tf_op jit(solution)/shard_map/ppermute | solution.py:24
  46.9 1.6 %collective-permute-start.16 = (f16[16,2048]{1,0:T(8,128)(2,1)S(1)}, f16[16,2048]{1,0:T(8,128)(2,1)S(1)}, u32[]{:S(2)}, u32[]{:S(2)}) collective-permute-start(f16[16,2048]{1,0:T(8,128)(2,1)S(1)} %get-tuple-element.39), channel_id=1, source_target_pairs={{0,6},{1,7},{2,4},{3,5},{4,2},{5,3},{6,0},{7,1},{8,14},{9,15},{10,... | collective-permute-start | bytes 196616 | tf_op jit(solution)/shard_map/ppermute | solution.py:24
  48.5 2.5 %collective-permute-done.15 = f16[16,2176]{1,0:T(8,128)(2,1)S(1)} collective-permute-done((f16[16,2176]{1,0:T(8,128)(2,1)S(1)}, f16[16,2176]{1,0:T(8,128)(2,1)S(1)}, u32[]{:S(2)}, u32[]{:S(2)}) %collective-permute-start.15) | collective-permute-done | bytes 69664 | tf_op jit(solution)/shard_map/ppermute | solution.py:24
  51.0 1.1 %collective-permute-done.16 = f16[16,2048]{1,0:T(8,128)(2,1)S(1)} collective-permute-done((f16[16,2048]{1,0:T(8,128)(2,1)S(1)}, f16[16,2048]{1,0:T(8,128)(2,1)S(1)}, u32[]{:S(2)}, u32[]{:S(2)}) %collective-permute-start.16) | collective-permute-done | bytes 65568 | tf_op jit(solution)/shard_map/ppermute | solution.py:24
  52.1 0.0 copy-done.1
  52.1 0.7 %fusion.12 = f32[16,2048]{1,0:T(8,128)} fusion(f32[16,2048]{1,0:T(8,128)S(1)} %copy-done.1, f32[1,16,2176]{2,1,0:T(8,128)S(1)} %bitcast_convert_fusion, f32[2,16,2048]{2,1,0:T(8,128)S(1)} %slice_add_fusion, f16[16,2048]{1,0:T(8,128)(2,1)S(1)} %collective-permute-done.16, f32[2048]{0:T(1024)S(1)} %fusion.18), kind=kLoop, calls=%fused_computation.33 | loop fusion | flops 163840 | bytes 598016 | tf_op jit(solution)/shard_map/sub | solution.py:210
  (33 shorter events, 0.5 us)
Async XLA Ops:
  0.0 1.2 %copy-start = (bf16[16,32768]{1,0:T(8,128)(2,1)S(1)}, bf16[16,32768]{1,0:T(8,128)(2,1)}, u32[]{:S(2)}) copy-start(bf16[16,32768]{1,0:T(8,128)(2,1)} %greens_ref.1) | copy-start | bytes 3145732
  1.3 25.4 %collective-permute-start.4 = (bf16[32,2048]{1,0:T(8,128)(2,1)S(1)}, bf16[32,2048]{1,0:T(8,128)(2,1)S(1)}, u32[]{:S(2)}, u32[]{:S(2)}) collective-permute-start(bf16[32,2048]{1,0:T(8,128)(2,1)S(1)} %get-tuple-element.21), channel_id=1, source_target_pairs={{0,8},{1,9},{2,10},{3,11},{4,12},{5,13},{6,14},{7,15},{8,0},{9,1},... | collective-permute-start | bytes 393224 | tf_op jit(solution)/shard_map/ppermute | solution.py:24
  5.4 23.3 %collective-permute-start.6 = (bf16[32,2048]{1,0:T(8,128)(2,1)S(1)}, bf16[32,2048]{1,0:T(8,128)(2,1)S(1)}, u32[]{:S(2)}, u32[]{:S(2)}) collective-permute-start(bf16[32,2048]{1,0:T(8,128)(2,1)S(1)} %get-tuple-element.24), channel_id=1, source_target_pairs={{0,12},{1,13},{2,14},{3,15},{4,8},{5,9},{6,10},{7,11},{8,4},{9,5},... | collective-permute-start | bytes 393224 | tf_op jit(solution)/shard_map/ppermute | solution.py:24
  6.7 2.5 %collective-permute-start = (bf16[64,2048]{1,0:T(8,128)(2,1)S(1)}, bf16[64,2048]{1,0:T(8,128)(2,1)S(1)}, u32[]{:S(2)}, u32[]{:S(2)}) collective-permute-start(bf16[64,2048]{1,0:T(8,128)(2,1)S(1)} %get-tuple-element.20), channel_id=1, source_target_pairs={{0,1},{1,0},{2,3},{3,2},{4,5},{5,4},{6,7},{7,6},{8,9},{9,8},{10,11... | collective-permute-start | bytes 786440 | tf_op jit(solution)/shard_map/ppermute | solution.py:24
  9.3 6.0 %collective-permute-start.1 = (bf16[32,2048]{1,0:T(8,128)(2,1)S(1)}, bf16[32,2048]{1,0:T(8,128)(2,1)S(1)}, u32[]{:S(2)}, u32[]{:S(2)}) collective-permute-start(bf16[32,2048]{1,0:T(8,128)(2,1)S(1)} %pad_maximum_fusion.3), channel_id=1, source_target_pairs={{0,2},{1,3},{2,0},{3,1},{4,6},{5,7},{6,4},{7,5},{8,10},{9,11},{10,... | collective-permute-start | bytes 393224 | tf_op jit(solution)/shard_map/ppermute | solution.py:24
  10.9 7.0 %collective-permute-start.2 = (bf16[32,2048]{1,0:T(8,128)(2,1)S(1)}, bf16[32,2048]{1,0:T(8,128)(2,1)S(1)}, u32[]{:S(2)}, u32[]{:S(2)}) collective-permute-start(bf16[32,2048]{1,0:T(8,128)(2,1)S(1)} %pad_maximum_fusion.4), channel_id=1, source_target_pairs={{0,4},{1,5},{2,6},{3,7},{4,0},{5,1},{6,2},{7,3},{8,12},{9,13},{10,... | collective-permute-start | bytes 393224 | tf_op jit(solution)/shard_map/ppermute | solution.py:24
  11.2 15.5 %collective-permute-start.3 = (bf16[32,2048]{1,0:T(8,128)(2,1)S(1)}, bf16[32,2048]{1,0:T(8,128)(2,1)S(1)}, u32[]{:S(2)}, u32[]{:S(2)}) collective-permute-start(bf16[32,2048]{1,0:T(8,128)(2,1)S(1)} %pad_maximum_fusion.5), channel_id=1, source_target_pairs={{0,6},{1,7},{2,4},{3,5},{4,2},{5,3},{6,0},{7,1},{8,14},{9,15},{10,... | collective-permute-start | bytes 393224 | tf_op jit(solution)/shard_map/ppermute | solution.py:24
  15.2 13.4 %collective-permute-start.5 = (bf16[32,2048]{1,0:T(8,128)(2,1)S(1)}, bf16[32,2048]{1,0:T(8,128)(2,1)S(1)}, u32[]{:S(2)}, u32[]{:S(2)}) collective-permute-start(bf16[32,2048]{1,0:T(8,128)(2,1)S(1)} %get-tuple-element.23), channel_id=1, source_target_pairs={{0,10},{1,11},{2,8},{3,9},{4,14},{5,15},{6,12},{7,13},{8,2},{9,3},... | collective-permute-start | bytes 393224 | tf_op jit(solution)/shard_map/ppermute | solution.py:24
  17.9 10.9 %collective-permute-start.7 = (bf16[32,2048]{1,0:T(8,128)(2,1)S(1)}, bf16[32,2048]{1,0:T(8,128)(2,1)S(1)}, u32[]{:S(2)}, u32[]{:S(2)}) collective-permute-start(bf16[32,2048]{1,0:T(8,128)(2,1)S(1)} %get-tuple-element.26), channel_id=1, source_target_pairs={{0,14},{1,15},{2,12},{3,13},{4,10},{5,11},{6,8},{7,9},{8,6},{9,7},... | collective-permute-start | bytes 393224 | tf_op jit(solution)/shard_map/ppermute | solution.py:24
  26.6 1.2 %collective-permute-start.10 = (f32[16,128]{1,0:T(8,128)S(1)}, f32[16,128]{1,0:T(8,128)S(1)}, u32[]{:S(2)}, u32[]{:S(2)}) collective-permute-start(f32[16,128]{1,0:T(8,128)S(1)} %bitcast.60), channel_id=1, source_target_pairs={{0,1},{1,0},{2,3},{3,2},{4,5},{5,4},{6,7},{7,6},{8,9},{9,8},{10,11... | collective-permute-start | bytes 24584 | tf_op jit(solution)/shard_map/ppermute | solution.py:24
  28.7 1.5 %collective-permute-start.8 = (bf16[48,2048]{1,0:T(8,128)(2,1)S(1)}, bf16[48,2048]{1,0:T(8,128)(2,1)S(1)}, u32[]{:S(2)}, u32[]{:S(2)}) collective-permute-start(bf16[48,2048]{1,0:T(8,128)(2,1)S(1)} %pad_maximum_fusion), channel_id=1, source_target_pairs={{0,1},{1,0},{2,3},{3,2},{4,5},{5,4},{6,7},{7,6},{8,9},{9,8},{10,11... | collective-permute-start | bytes 589832 | tf_op jit(solution)/shard_map/ppermute | solution.py:24
  28.8 1.5 %collective-permute-start.9 = (bf16[16,2048]{1,0:T(8,128)(2,1)S(1)}, bf16[16,2048]{1,0:T(8,128)(2,1)S(1)}, u32[]{:S(2)}, u32[]{:S(2)}) collective-permute-start(bf16[16,2048]{1,0:T(8,128)(2,1)S(1)} %get-tuple-element.51), channel_id=1, source_target_pairs={{0,1},{1,0},{2,3},{3,2},{4,5},{5,4},{6,7},{7,6},{8,9},{9,8},{10,11... | collective-permute-start | bytes 196616 | tf_op jit(solution)/shard_map/ppermute | solution.py:24
  30.3 21.8 %copy-start.1 = (f32[16,2048]{1,0:T(8,128)S(1)}, f32[16,2048]{1,0:T(8,128)}, u32[]{:S(2)}) copy-start(f32[16,2048]{1,0:T(8,128)} %param.9) | copy-start | bytes 393220
  33.0 2.0 %collective-permute-start.11 = (bf16[128,2048]{1,0:T(8,128)(2,1)S(1)}, bf16[128,2048]{1,0:T(8,128)(2,1)S(1)}, u32[]{:S(2)}, u32[]{:S(2)}) collective-permute-start(bf16[128,2048]{1,0:T(8,128)(2,1)S(1)} %get-tuple-element.32), channel_id=1, source_target_pairs={{0,1},{1,0},{2,3},{3,2},{4,5},{5,4},{6,7},{7,6},{8,9},{9,8},{10,11... | collective-permute-start | bytes 1572872 | tf_op jit(solution)/shard_map/ppermute | solution.py:24
  35.2 5.7 %collective-permute-start.12 = (f16[16,2176]{1,0:T(8,128)(2,1)S(1)}, f16[16,2176]{1,0:T(8,128)(2,1)S(1)}, u32[]{:S(2)}, u32[]{:S(2)}) collective-permute-start(f16[16,2176]{1,0:T(8,128)(2,1)S(1)} %pad_maximum_fusion.6), channel_id=1, source_target_pairs={{0,6},{1,7},{2,4},{3,5},{4,2},{5,3},{6,0},{7,1},{8,14},{9,15},{10,... | collective-permute-start | bytes 208904 | tf_op jit(solution)/shard_map/ppermute | solution.py:24
  38.5 5.5 %collective-permute-start.13 = (f16[32,2176]{1,0:T(8,128)(2,1)S(1)}, f16[32,2176]{1,0:T(8,128)(2,1)S(1)}, u32[]{:S(2)}, u32[]{:S(2)}) collective-permute-start(f16[32,2176]{1,0:T(8,128)(2,1)S(1)} %get-tuple-element.59), channel_id=1, source_target_pairs={{0,2},{1,3},{2,0},{3,1},{4,6},{5,7},{6,4},{7,5},{8,10},{9,11},{10,... | collective-permute-start | bytes 417800 | tf_op jit(solution)/shard_map/ppermute | solution.py:24
  39.1 5.2 %collective-permute-start.14 = (f16[32,2176]{1,0:T(8,128)(2,1)S(1)}, f16[32,2176]{1,0:T(8,128)(2,1)S(1)}, u32[]{:S(2)}, u32[]{:S(2)}) collective-permute-start(f16[32,2176]{1,0:T(8,128)(2,1)S(1)} %get-tuple-element.60), channel_id=1, source_target_pairs={{0,4},{1,5},{2,6},{3,7},{4,0},{5,1},{6,2},{7,3},{8,12},{9,13},{10,... | collective-permute-start | bytes 417800 | tf_op jit(solution)/shard_map/ppermute | solution.py:24
  44.4 6.6 %collective-permute-start.15 = (f16[16,2176]{1,0:T(8,128)(2,1)S(1)}, f16[16,2176]{1,0:T(8,128)(2,1)S(1)}, u32[]{:S(2)}, u32[]{:S(2)}) collective-permute-start(f16[16,2176]{1,0:T(8,128)(2,1)S(1)} %pad_maximum_fusion.7), channel_id=1, source_target_pairs={{0,8},{1,9},{2,10},{3,11},{4,12},{5,13},{6,14},{7,15},{8,0},{9,1},... | collective-permute-start | bytes 208904 | tf_op jit(solution)/shard_map/ppermute | solution.py:24
  46.9 5.2 %collective-permute-start.16 = (f16[16,2048]{1,0:T(8,128)(2,1)S(1)}, f16[16,2048]{1,0:T(8,128)(2,1)S(1)}, u32[]{:S(2)}, u32[]{:S(2)}) collective-permute-start(f16[16,2048]{1,0:T(8,128)(2,1)S(1)} %get-tuple-element.39), channel_id=1, source_target_pairs={{0,6},{1,7},{2,4},{3,5},{4,2},{5,3},{6,0},{7,1},{8,14},{9,15},{10,... | collective-permute-start | bytes 196616 | tf_op jit(solution)/shard_map/ppermute | solution.py:24

commit v7 on v6

--- a/solution.py
+++ b/solution.py
@@ -28,27 +28,33 @@
     me = lax.axis_index("chol")
     own = greens_ref.shape[0]
     pairs = outs[0].shape[1]
-    far = len(outs) - 2
-    for m in range(2 * far):
+    half = outs[0].shape[0] // own
+    for m in range(2 * half):
         for j in range(2):
             there = pl.multiple_of(jnp.bitwise_xor(me, 2 * m + j) * pairs, pairs)
-            out, at = (outs[j], m) if m < far else (outs[2 + m - far], j)
+            if m < half:
+                out, at = outs[j], m
+            elif m < 2 * half - 1:
+                out, at = outs[2 + m - half], j
+            else:
+                out, at = outs[1 + half + j], 0
             out[pl.ds(at * own, own), :] = greens_ref[:, pl.ds(there, pairs)]
 
 
 def split_by_device(greens, n):
     own, total = greens.shape
     pairs = total // n
-    shapes = [(n // 4 * own, pairs)] * 2 + [(2 * own, pairs)] * (n // 4)
+    half = n // 4
+    rows = [half * own] * 2 + [2 * own] * (half - 1) + [own] * 2
     outs = pl.pallas_call(
         split_kernel,
         in_specs=[pl.BlockSpec(memory_space=pltpu.VMEM)],
-        out_specs=[pl.BlockSpec(memory_space=pltpu.VMEM)] * len(shapes),
-        out_shape=[jax.ShapeDtypeStruct(shape, greens.dtype) for shape in shapes],
+        out_specs=[pl.BlockSpec(memory_space=pltpu.VMEM)] * len(rows),
+        out_shape=[jax.ShapeDtypeStruct((r, pairs), greens.dtype) for r in rows],
         compiler_params=pltpu.CompilerParams(vmem_limit_bytes=8 * 2**20),
         cost_estimate=pl.CostEstimate(flops=0, bytes_accessed=4 * greens.size, transcendentals=0),
     )(greens)
-    return outs[0], outs[1], outs[2:]
+    return outs[0], outs[1], outs[2 : half + 1], outs[half + 1 :]
 
 
 def after(x, *others):
@@ -57,22 +63,27 @@
 
 def collect_walkers(greens, n):
     own, half = greens.shape[0], n // 4
-    near, other, far = split_by_device(greens, n)
+    near, other, far, last = split_by_device(greens, n)
     other = swap(other, 1, n)
     block = lambda x, i: x[i * own : (i + 1) * own]
     sent = [jnp.concatenate([block(near, i), block(other, i)]) for i in range(half)] + list(far)
-    waits = {5: 1, 7: 2} if half == 4 else {}
-    got = [sent[0]]
-    for m in range(1, 2 * half):
+    waits = {5: 1} if half == 4 else {}
+    got = {0: sent[0]}
+    for m in range(1, 2 * half - 1):
         message = after(sent[m], got[waits[m]]) if m in waits else sent[m]
-        got.append(swap(message, 2 * m, n))
-    passed = [swap(jnp.concatenate([x[own:] for x in part]), 1, n) for part in (got[half:-1], got[-1:])]
-    return jnp.concatenate(got[:half] + [x[:own] for x in got[half:]] + passed), got[1]
+        got[m] = swap(message, 2 * m, n)
+    last = [after(x, got[w]) for x, w in zip(last, (2, 3))]
+    last = [swap(x, n - 2 + j, n) for j, x in enumerate(last)]
+    far = [got[m] for m in range(half, 2 * half - 1)]
+    passed = swap(jnp.concatenate([x[own:] for x in far]), 1, n)
+    rows = [got[m] for m in range(half)] + [x[:own] for x in far] + [passed] + last
+    return jnp.concatenate(rows), got[1]
 
 
 def place_of_source(source, n):
-    far = n // 2 + (source % 2) * (n // 4) + (source - n // 2) // 2
-    return jnp.where(source < n // 2, source, far)
+    half = n // 4
+    far = n // 2 + (source % 2) * (half - 1) + source // 2 - half
+    return jnp.where((source < n // 2) | (source >= n - 2), source, far)
 
 
 def mean_kernel(parts, chol_ref, mean_ref, part_ref, staged_ref, sems):

time: 53 us -> 51.9 us (0.979)
  waiting for transfers between devices: 15.3 us -> 13.4 us
  starting transfers between devices: 24.8 us -> 25.5 us
    ppermute x17, waiting for transfers between devices: 15.3 us -> 13.4 us  [swap(): return lax.ppermute(x, 'chol', [(i, i ^ mask) for i in range(n)])]
    ppermute x17, starting transfers between devices: 24.8 us -> 25.5 us  [swap(): return lax.ppermute(x, 'chol', [(i, i ^ mask) for i in range(n)])]
    unnamed x8 -> x9, local copies, waits for them, and re-layouts: 1.27 us -> 1.28 us
  transfers between devices with their start and end apart: 17 -> 17, of which waited for: 11 -> 10; matrix products, arithmetic and copies ran while one was open for 5% -> 5% of each run, Pallas kernels for 9% -> 9%
where the time goes in v7:
time: 51.9 us; the launch traced here: 51.6 us
  starting transfers between devices  25.5 us (49%)
  waiting for transfers between devices  13.4 us (26%)
  Pallas kernels  7.4 us (14%)
  local copies, waits for them, and re-layouts  3.58 us (7%)
  other arithmetic  1.46 us (3%)
    ppermute x17, starting transfers between devices, swap(): return lax.ppermute(x, 'chol', [(i, i ^ mask) for i in range(n)])  25.5 us
    ppermute x17, waiting for transfers between devices, swap(): return lax.ppermute(x, 'chol', [(i, i ^ mask) for i in range(n)])  13.4 us
    pallas_call x1, Pallas kernels, mean_part(): pl.pallas_call(functools.partial(mean_kernel, parts), in_specs=[pl.BlockS...  4.7 us
    pallas_call x1, Pallas kernels, partial_bias(): pl.pallas_call(functools.partial(bias_kernel, tile), in_specs=[pl.BlockSp...  2.63 us
    unnamed x9, local copies, waits for them, and re-layouts  1.28 us
  transfers between devices with their start and end apart: 17, of which 10 were waited for; matrix products, arithmetic and copies ran while one was open for 5% of the time, Pallas kernels for 9%

profile of v7, /device:TPU:0, one launch (start us, length us, event | category | flops | bytes accessed | tf_op | source)
XLA Modules:
  0.0 51.6 jit_solution(6037738650591364132)
XLA Ops:
  0.0 0.0 copy-start
  0.0 1.2 %copy-done = bf16[16,32768]{1,0:T(8,128)(2,1)S(1)} copy-done((bf16[16,32768]{1,0:T(8,128)(2,1)S(1)}, bf16[16,32768]{1,0:T(8,128)(2,1)}, u32[]{:S(2)}) %copy-start) | copy-done | bytes 1048600
  1.2 0.1 shard_map.55
  1.3 4.1 %collective-permute-start.4 = (bf16[32,2048]{1,0:T(8,128)(2,1)S(1)}, bf16[32,2048]{1,0:T(8,128)(2,1)S(1)}, u32[]{:S(2)}, u32[]{:S(2)}) collective-permute-start(bf16[32,2048]{1,0:T(8,128)(2,1)S(1)} %get-tuple-element.23), channel_id=1, source_target_pairs={{0,8},{1,9},{2,10},{3,11},{4,12},{5,13},{6,14},{7,15},{8,0},{9,1},... | collective-permute-start | bytes 393224 | tf_op jit(solution)/shard_map/ppermute | solution.py:24
  5.4 1.3 %collective-permute-start.6 = (bf16[32,2048]{1,0:T(8,128)(2,1)S(1)}, bf16[32,2048]{1,0:T(8,128)(2,1)S(1)}, u32[]{:S(2)}, u32[]{:S(2)}) collective-permute-start(bf16[32,2048]{1,0:T(8,128)(2,1)S(1)} %get-tuple-element.26), channel_id=1, source_target_pairs={{0,12},{1,13},{2,14},{3,15},{4,8},{5,9},{6,10},{7,11},{8,4},{9,5},... | collective-permute-start | bytes 393224 | tf_op jit(solution)/shard_map/ppermute | solution.py:24
  6.7 0.0 collective-permute-start
  6.8 0.7 %broadcast_in_dim.4.mean_ref = bf16[1,2048]{1,0:T(2,128)(2,1)S(1)} reshape(bf16[2048]{0:T(1024)(128)(2,1)} %param.6) | data formatting | bytes 8192 | tf_op jit(solution)/shard_map/broadcast_in_dim | solution.py:207
  7.5 0.8 %reshape.413 = s32[16,16]{1,0:T(8,128)S(1)} reshape(s32[256]{0:T(256)} %param.8) | data formatting | bytes 2048 | tf_op jit(solution)/shard_map/reshape | solution.py:205
  8.2 0.6 %gather_fusion = s32[16,16]{1,0:T(8,128)S(1)} fusion(s32[16,16]{1,0:T(8,128)S(1)} %reshape.413, s32[1024]{0:T(1024)S(1)} %pad_clamp_fusion), kind=kCustom, calls=%fused_computation | custom fusion | bytes 2112 | tf_op jit(solution)/shard_map/gather | solution.py:205
  8.8 0.1 reshape.442
  8.9 0.0 collective-permute-done
  9.0 1.6 %collective-permute-start.1 = (bf16[32,2048]{1,0:T(8,128)(2,1)S(1)}, bf16[32,2048]{1,0:T(8,128)(2,1)S(1)}, u32[]{:S(2)}, u32[]{:S(2)}) collective-permute-start(bf16[32,2048]{1,0:T(8,128)(2,1)S(1)} %pad_maximum_fusion.3), channel_id=1, source_target_pairs={{0,2},{1,3},{2,0},{3,1},{4,6},{5,7},{6,4},{7,5},{8,10},{9,11},{10,... | collective-permute-start | bytes 393224 | tf_op jit(solution)/shard_map/ppermute | solution.py:24
  10.6 0.3 collective-permute-start.2
  10.9 1.8 %collective-permute-start.3 = (bf16[32,2048]{1,0:T(8,128)(2,1)S(1)}, bf16[32,2048]{1,0:T(8,128)(2,1)S(1)}, u32[]{:S(2)}, u32[]{:S(2)}) collective-permute-start(bf16[32,2048]{1,0:T(8,128)(2,1)S(1)} %pad_maximum_fusion.5), channel_id=1, source_target_pairs={{0,6},{1,7},{2,4},{3,5},{4,2},{5,3},{6,0},{7,1},{8,14},{9,15},{10,... | collective-permute-start | bytes 393224 | tf_op jit(solution)/shard_map/ppermute | solution.py:24
  12.7 0.3 fusion.7.index_ref
  13.0 2.0 %collective-permute-done.1 = bf16[32,2048]{1,0:T(8,128)(2,1)S(1)} collective-permute-done((bf16[32,2048]{1,0:T(8,128)(2,1)S(1)}, bf16[32,2048]{1,0:T(8,128)(2,1)S(1)}, u32[]{:S(2)}, u32[]{:S(2)}) %collective-permute-start.1) | collective-permute-done | bytes 131104 | tf_op jit(solution)/shard_map/ppermute | solution.py:24
  15.0 2.6 %collective-permute-start.5 = (bf16[32,2048]{1,0:T(8,128)(2,1)S(1)}, bf16[32,2048]{1,0:T(8,128)(2,1)S(1)}, u32[]{:S(2)}, u32[]{:S(2)}) collective-permute-start(bf16[32,2048]{1,0:T(8,128)(2,1)S(1)} %get-tuple-element.25), channel_id=1, source_target_pairs={{0,10},{1,11},{2,8},{3,9},{4,14},{5,15},{6,12},{7,13},{8,2},{9,3},... | collective-permute-start | bytes 393224 | tf_op jit(solution)/shard_map/ppermute | solution.py:24
  17.6 0.0 collective-permute-done.2
  17.6 4.3 %collective-permute-start.8 = (bf16[16,2048]{1,0:T(8,128)(2,1)S(1)}, bf16[16,2048]{1,0:T(8,128)(2,1)S(1)}, u32[]{:S(2)}, u32[]{:S(2)}) collective-permute-start(bf16[16,2048]{1,0:T(8,128)(2,1)S(1)} %get-tuple-element.28), channel_id=1, source_target_pairs={{0,14},{1,15},{2,12},{3,13},{4,10},{5,11},{6,8},{7,9},{8,6},{9,7},... | collective-permute-start | bytes 196616 | tf_op jit(solution)/shard_map/ppermute | solution.py:24
  21.9 0.4 collective-permute-done.3
  22.3 2.3 %collective-permute-start.9 = (bf16[16,2048]{1,0:T(8,128)(2,1)S(1)}, bf16[16,2048]{1,0:T(8,128)(2,1)S(1)}, u32[]{:S(2)}, u32[]{:S(2)}) collective-permute-start(bf16[16,2048]{1,0:T(8,128)(2,1)S(1)} %get-tuple-element.30), channel_id=1, source_target_pairs={{0,15},{1,14},{2,13},{3,12},{4,11},{5,10},{6,9},{7,8},{8,7},{9,6},... | collective-permute-start | bytes 196616 | tf_op jit(solution)/shard_map/ppermute | solution.py:24
  24.7 4.7 %shard_map.56 = (f32[1,2048]{1,0:T(1,128)S(1)}, bf16[2048,2048]{1,0:T(8,128)(2,1)S(1)}) custom-call(bf16[2048,2048]{1,0:T(8,128)(2,1)} %chol_ref.1, bf16[1,2048]{1,0:T(2,128)(2,1)S(1)} %broadcast_in_dim.4.mean_ref), custom_call_target="tpu_custom_call" | custom-call | flops 67108864 | bytes 8388608 | tf_op jit(solution)/shard_map/pallas_call | solution.py:110
  29.4 0.0 collective-permute-done.4
  29.4 0.5 %collective-permute-start.10 = (f32[16,128]{1,0:T(8,128)S(1)}, f32[16,128]{1,0:T(8,128)S(1)}, u32[]{:S(2)}, u32[]{:S(2)}) collective-permute-start(f32[16,128]{1,0:T(8,128)S(1)} %bitcast.60), channel_id=1, source_target_pairs={{0,1},{1,0},{2,3},{3,2},{4,5},{5,4},{6,7},{7,6},{8,9},{9,8},{10,11... | collective-permute-start | bytes 24584 | tf_op jit(solution)/shard_map/ppermute | solution.py:24
  30.0 0.0 collective-permute-done.5
  30.0 0.0 collective-permute-done.6
  30.0 0.1 collective-permute-start.7
  30.2 0.6 %collective-permute-done.10 = f32[16,128]{1,0:T(8,128)S(1)} collective-permute-done((f32[16,128]{1,0:T(8,128)S(1)}, f32[16,128]{1,0:T(8,128)S(1)}, u32[]{:S(2)}, u32[]{:S(2)}) %collective-permute-start.10) | collective-permute-done | bytes 8224 | tf_op jit(solution)/shard_map/ppermute | solution.py:24
  30.8 0.8 %collective-permute-done.7 = bf16[48,2048]{1,0:T(8,128)(2,1)S(1)} collective-permute-done((bf16[48,2048]{1,0:T(8,128)(2,1)S(1)}, bf16[48,2048]{1,0:T(8,128)(2,1)S(1)}, u32[]{:S(2)}, u32[]{:S(2)}) %collective-permute-start.7) | collective-permute-done | bytes 196640 | tf_op jit(solution)/shard_map/ppermute | solution.py:24
  31.6 0.0 collective-permute-done.8
  31.6 0.0 collective-permute-done.9
  31.6 0.0 copy-start.1
  31.6 2.6 %shard_map.57 = (f32[128,2048]{1,0:T(8,128)S(1)}, bf16[128,2048]{1,0:T(8,128)(2,1)S(1)}) custom-call(s32[256,1]{1,0:T(8,128)S(1)} %fusion.7.index_ref, bf16[256,2048]{1,0:T(8,128)(2,1)S(1)} %constant_dynamic-update-slice_fusion.rows_ref, bf16[2048,2048]{1,0:T(8,128)(2,1)S(1)} %get-tuple-element.34.chol_ref), custom_call_target="tpu_custom_call" | custom-call | flops 2415919104 | bytes 11010048 | tf_op jit(solution)/shard_map/pallas_call | solution.py:146
  34.3 0.2 collective-permute-start.11
  34.5 1.8 %collective-permute-done.11 = bf16[128,2048]{1,0:T(8,128)(2,1)S(1)} collective-permute-done((bf16[128,2048]{1,0:T(8,128)(2,1)S(1)}, bf16[128,2048]{1,0:T(8,128)(2,1)S(1)}, u32[]{:S(2)}, u32[]{:S(2)}) %collective-permute-start.11) | collective-permute-done | bytes 524320 | tf_op jit(solution)/shard_map/ppermute | solution.py:24
  36.3 0.2 fusion.30
  36.5 0.1 collective-permute-start.12
  36.6 0.1 pad_maximum_fusion.2
  36.7 1.3 %collective-permute-start.13 = (f16[32,2176]{1,0:T(8,128)(2,1)S(1)}, f16[32,2176]{1,0:T(8,128)(2,1)S(1)}, u32[]{:S(2)}, u32[]{:S(2)}) collective-permute-start(f16[32,2176]{1,0:T(8,128)(2,1)S(1)} %get-tuple-element.61), channel_id=1, source_target_pairs={{0,2},{1,3},{2,0},{3,1},{4,6},{5,7},{6,4},{7,5},{8,10},{9,11},{10,... | collective-permute-start | bytes 417800 | tf_op jit(solution)/shard_map/ppermute | solution.py:24
  38.0 2.2 %collective-permute-start.14 = (f16[32,2176]{1,0:T(8,128)(2,1)S(1)}, f16[32,2176]{1,0:T(8,128)(2,1)S(1)}, u32[]{:S(2)}, u32[]{:S(2)}) collective-permute-start(f16[32,2176]{1,0:T(8,128)(2,1)S(1)} %get-tuple-element.62), channel_id=1, source_target_pairs={{0,4},{1,5},{2,6},{3,7},{4,0},{5,1},{6,2},{7,3},{8,12},{9,13},{10,... | collective-permute-start | bytes 417800 | tf_op jit(solution)/shard_map/ppermute | solution.py:24
  40.3 2.0 %collective-permute-done.12 = f16[16,2176]{1,0:T(8,128)(2,1)S(1)} collective-permute-done((f16[16,2176]{1,0:T(8,128)(2,1)S(1)}, f16[16,2176]{1,0:T(8,128)(2,1)S(1)}, u32[]{:S(2)}, u32[]{:S(2)}) %collective-permute-start.12) | collective-permute-done | bytes 69664 | tf_op jit(solution)/shard_map/ppermute | solution.py:24
  42.3 1.7 %collective-permute-done.13 = f16[32,2176]{1,0:T(8,128)(2,1)S(1)} collective-permute-done((f16[32,2176]{1,0:T(8,128)(2,1)S(1)}, f16[32,2176]{1,0:T(8,128)(2,1)S(1)}, u32[]{:S(2)}, u32[]{:S(2)}) %collective-permute-start.13) | collective-permute-done | bytes 139296 | tf_op jit(solution)/shard_map/ppermute | solution.py:24
  44.0 0.5 collective-permute-done.14
  44.6 0.8 %collective-permute-start.15 = (f16[16,2176]{1,0:T(8,128)(2,1)S(1)}, f16[16,2176]{1,0:T(8,128)(2,1)S(1)}, u32[]{:S(2)}, u32[]{:S(2)}) collective-permute-start(f16[16,2176]{1,0:T(8,128)(2,1)S(1)} %pad_maximum_fusion.7), channel_id=1, source_target_pairs={{0,8},{1,9},{2,10},{3,11},{4,12},{5,13},{6,14},{7,15},{8,0},{9,1},... | collective-permute-start | bytes 208904 | tf_op jit(solution)/shard_map/ppermute | solution.py:24
  45.5 1.8 %collective-permute-start.16 = (f16[16,2048]{1,0:T(8,128)(2,1)S(1)}, f16[16,2048]{1,0:T(8,128)(2,1)S(1)}, u32[]{:S(2)}, u32[]{:S(2)}) collective-permute-start(f16[16,2048]{1,0:T(8,128)(2,1)S(1)} %get-tuple-element.43), channel_id=1, source_target_pairs={{0,6},{1,7},{2,4},{3,5},{4,2},{5,3},{6,0},{7,1},{8,14},{9,15},{10,... | collective-permute-start | bytes 196616 | tf_op jit(solution)/shard_map/ppermute | solution.py:24
  47.3 3.4 %collective-permute-done.15 = f16[16,2176]{1,0:T(8,128)(2,1)S(1)} collective-permute-done((f16[16,2176]{1,0:T(8,128)(2,1)S(1)}, f16[16,2176]{1,0:T(8,128)(2,1)S(1)}, u32[]{:S(2)}, u32[]{:S(2)}) %collective-permute-start.15) | collective-permute-done | bytes 69664 | tf_op jit(solution)/shard_map/ppermute | solution.py:24
  50.7 0.3 collective-permute-done.16
  50.9 0.0 copy-done.1
  50.9 0.7 %fusion.12 = f32[16,2048]{1,0:T(8,128)} fusion(f32[16,2048]{1,0:T(8,128)S(1)} %copy-done.1, f32[1,16,2176]{2,1,0:T(8,128)S(1)} %bitcast_convert_fusion, f32[2,16,2048]{2,1,0:T(8,128)S(1)} %slice_add_fusion, f16[16,2048]{1,0:T(8,128)(2,1)S(1)} %collective-permute-done.16, f32[2048]{0:T(1024)S(1)} %fusion.19), kind=kLoop, calls=%fused_computation.30 | loop fusion | flops 163840 | bytes 598016 | tf_op jit(solution)/shard_map/sub | solution.py:221
  (33 shorter events, 0.5 us)
Async XLA Ops:
  0.0 1.2 %copy-start = (bf16[16,32768]{1,0:T(8,128)(2,1)S(1)}, bf16[16,32768]{1,0:T(8,128)(2,1)}, u32[]{:S(2)}) copy-start(bf16[16,32768]{1,0:T(8,128)(2,1)} %greens_ref.1) | copy-start | bytes 3145732
  1.3 28.1 %collective-permute-start.4 = (bf16[32,2048]{1,0:T(8,128)(2,1)S(1)}, bf16[32,2048]{1,0:T(8,128)(2,1)S(1)}, u32[]{:S(2)}, u32[]{:S(2)}) collective-permute-start(bf16[32,2048]{1,0:T(8,128)(2,1)S(1)} %get-tuple-element.23), channel_id=1, source_target_pairs={{0,8},{1,9},{2,10},{3,11},{4,12},{5,13},{6,14},{7,15},{8,0},{9,1},... | collective-permute-start | bytes 393224 | tf_op jit(solution)/shard_map/ppermute | solution.py:24
  5.4 24.6 %collective-permute-start.6 = (bf16[32,2048]{1,0:T(8,128)(2,1)S(1)}, bf16[32,2048]{1,0:T(8,128)(2,1)S(1)}, u32[]{:S(2)}, u32[]{:S(2)}) collective-permute-start(bf16[32,2048]{1,0:T(8,128)(2,1)S(1)} %get-tuple-element.26), channel_id=1, source_target_pairs={{0,12},{1,13},{2,14},{3,15},{4,8},{5,9},{6,10},{7,11},{8,4},{9,5},... | collective-permute-start | bytes 393224 | tf_op jit(solution)/shard_map/ppermute | solution.py:24
  6.7 2.2 %collective-permute-start = (bf16[64,2048]{1,0:T(8,128)(2,1)S(1)}, bf16[64,2048]{1,0:T(8,128)(2,1)S(1)}, u32[]{:S(2)}, u32[]{:S(2)}) collective-permute-start(bf16[64,2048]{1,0:T(8,128)(2,1)S(1)} %get-tuple-element.22), channel_id=1, source_target_pairs={{0,1},{1,0},{2,3},{3,2},{4,5},{5,4},{6,7},{7,6},{8,9},{9,8},{10,11... | collective-permute-start | bytes 786440 | tf_op jit(solution)/shard_map/ppermute | solution.py:24
  9.0 6.0 %collective-permute-start.1 = (bf16[32,2048]{1,0:T(8,128)(2,1)S(1)}, bf16[32,2048]{1,0:T(8,128)(2,1)S(1)}, u32[]{:S(2)}, u32[]{:S(2)}) collective-permute-start(bf16[32,2048]{1,0:T(8,128)(2,1)S(1)} %pad_maximum_fusion.3), channel_id=1, source_target_pairs={{0,2},{1,3},{2,0},{3,1},{4,6},{5,7},{6,4},{7,5},{8,10},{9,11},{10,... | collective-permute-start | bytes 393224 | tf_op jit(solution)/shard_map/ppermute | solution.py:24
  10.6 7.0 %collective-permute-start.2 = (bf16[32,2048]{1,0:T(8,128)(2,1)S(1)}, bf16[32,2048]{1,0:T(8,128)(2,1)S(1)}, u32[]{:S(2)}, u32[]{:S(2)}) collective-permute-start(bf16[32,2048]{1,0:T(8,128)(2,1)S(1)} %pad_maximum_fusion.4), channel_id=1, source_target_pairs={{0,4},{1,5},{2,6},{3,7},{4,0},{5,1},{6,2},{7,3},{8,12},{9,13},{10,... | collective-permute-start | bytes 393224 | tf_op jit(solution)/shard_map/ppermute | solution.py:24
  10.9 11.4 %collective-permute-start.3 = (bf16[32,2048]{1,0:T(8,128)(2,1)S(1)}, bf16[32,2048]{1,0:T(8,128)(2,1)S(1)}, u32[]{:S(2)}, u32[]{:S(2)}) collective-permute-start(bf16[32,2048]{1,0:T(8,128)(2,1)S(1)} %pad_maximum_fusion.5), channel_id=1, source_target_pairs={{0,6},{1,7},{2,4},{3,5},{4,2},{5,3},{6,0},{7,1},{8,14},{9,15},{10,... | collective-permute-start | bytes 393224 | tf_op jit(solution)/shard_map/ppermute | solution.py:24
  15.0 15.0 %collective-permute-start.5 = (bf16[32,2048]{1,0:T(8,128)(2,1)S(1)}, bf16[32,2048]{1,0:T(8,128)(2,1)S(1)}, u32[]{:S(2)}, u32[]{:S(2)}) collective-permute-start(bf16[32,2048]{1,0:T(8,128)(2,1)S(1)} %get-tuple-element.25), channel_id=1, source_target_pairs={{0,10},{1,11},{2,8},{3,9},{4,14},{5,15},{6,12},{7,13},{8,2},{9,3},... | collective-permute-start | bytes 393224 | tf_op jit(solution)/shard_map/ppermute | solution.py:24
  17.6 14.0 %collective-permute-start.8 = (bf16[16,2048]{1,0:T(8,128)(2,1)S(1)}, bf16[16,2048]{1,0:T(8,128)(2,1)S(1)}, u32[]{:S(2)}, u32[]{:S(2)}) collective-permute-start(bf16[16,2048]{1,0:T(8,128)(2,1)S(1)} %get-tuple-element.28), channel_id=1, source_target_pairs={{0,14},{1,15},{2,12},{3,13},{4,10},{5,11},{6,8},{7,9},{8,6},{9,7},... | collective-permute-start | bytes 196616 | tf_op jit(solution)/shard_map/ppermute | solution.py:24
  22.3 9.3 %collective-permute-start.9 = (bf16[16,2048]{1,0:T(8,128)(2,1)S(1)}, bf16[16,2048]{1,0:T(8,128)(2,1)S(1)}, u32[]{:S(2)}, u32[]{:S(2)}) collective-permute-start(bf16[16,2048]{1,0:T(8,128)(2,1)S(1)} %get-tuple-element.30), channel_id=1, source_target_pairs={{0,15},{1,14},{2,13},{3,12},{4,11},{5,10},{6,9},{7,8},{8,7},{9,6},... | collective-permute-start | bytes 196616 | tf_op jit(solution)/shard_map/ppermute | solution.py:24
  29.4 1.4 %collective-permute-start.10 = (f32[16,128]{1,0:T(8,128)S(1)}, f32[16,128]{1,0:T(8,128)S(1)}, u32[]{:S(2)}, u32[]{:S(2)}) collective-permute-start(f32[16,128]{1,0:T(8,128)S(1)} %bitcast.60), channel_id=1, source_target_pairs={{0,1},{1,0},{2,3},{3,2},{4,5},{5,4},{6,7},{7,6},{8,9},{9,8},{10,11... | collective-permute-start | bytes 24584 | tf_op jit(solution)/shard_map/ppermute | solution.py:24
  30.0 1.5 %collective-permute-start.7 = (bf16[48,2048]{1,0:T(8,128)(2,1)S(1)}, bf16[48,2048]{1,0:T(8,128)(2,1)S(1)}, u32[]{:S(2)}, u32[]{:S(2)}) collective-permute-start(bf16[48,2048]{1,0:T(8,128)(2,1)S(1)} %pad_maximum_fusion), channel_id=1, source_target_pairs={{0,1},{1,0},{2,3},{3,2},{4,5},{5,4},{6,7},{7,6},{8,9},{9,8},{10,11... | collective-permute-start | bytes 589832 | tf_op jit(solution)/shard_map/ppermute | solution.py:24
  31.6 19.3 %copy-start.1 = (f32[16,2048]{1,0:T(8,128)S(1)}, f32[16,2048]{1,0:T(8,128)}, u32[]{:S(2)}) copy-start(f32[16,2048]{1,0:T(8,128)} %param.9) | copy-start | bytes 393220
  34.3 2.0 %collective-permute-start.11 = (bf16[128,2048]{1,0:T(8,128)(2,1)S(1)}, bf16[128,2048]{1,0:T(8,128)(2,1)S(1)}, u32[]{:S(2)}, u32[]{:S(2)}) collective-permute-start(bf16[128,2048]{1,0:T(8,128)(2,1)S(1)} %get-tuple-element.36), channel_id=1, source_target_pairs={{0,1},{1,0},{2,3},{3,2},{4,5},{5,4},{6,7},{7,6},{8,9},{9,8},{10,11... | collective-permute-start | bytes 1572872 | tf_op jit(solution)/shard_map/ppermute | solution.py:24
  36.5 5.7 %collective-permute-start.12 = (f16[16,2176]{1,0:T(8,128)(2,1)S(1)}, f16[16,2176]{1,0:T(8,128)(2,1)S(1)}, u32[]{:S(2)}, u32[]{:S(2)}) collective-permute-start(f16[16,2176]{1,0:T(8,128)(2,1)S(1)} %pad_maximum_fusion.6), channel_id=1, source_target_pairs={{0,6},{1,7},{2,4},{3,5},{4,2},{5,3},{6,0},{7,1},{8,14},{9,15},{10,... | collective-permute-start | bytes 208904 | tf_op jit(solution)/shard_map/ppermute | solution.py:24
  36.7 7.3 %collective-permute-start.13 = (f16[32,2176]{1,0:T(8,128)(2,1)S(1)}, f16[32,2176]{1,0:T(8,128)(2,1)S(1)}, u32[]{:S(2)}, u32[]{:S(2)}) collective-permute-start(f16[32,2176]{1,0:T(8,128)(2,1)S(1)} %get-tuple-element.61), channel_id=1, source_target_pairs={{0,2},{1,3},{2,0},{3,1},{4,6},{5,7},{6,4},{7,5},{8,10},{9,11},{10,... | collective-permute-start | bytes 417800 | tf_op jit(solution)/shard_map/ppermute | solution.py:24
  38.0 6.5 %collective-permute-start.14 = (f16[32,2176]{1,0:T(8,128)(2,1)S(1)}, f16[32,2176]{1,0:T(8,128)(2,1)S(1)}, u32[]{:S(2)}, u32[]{:S(2)}) collective-permute-start(f16[32,2176]{1,0:T(8,128)(2,1)S(1)} %get-tuple-element.62), channel_id=1, source_target_pairs={{0,4},{1,5},{2,6},{3,7},{4,0},{5,1},{6,2},{7,3},{8,12},{9,13},{10,... | collective-permute-start | bytes 417800 | tf_op jit(solution)/shard_map/ppermute | solution.py:24
  44.6 6.0 %collective-permute-start.15 = (f16[16,2176]{1,0:T(8,128)(2,1)S(1)}, f16[16,2176]{1,0:T(8,128)(2,1)S(1)}, u32[]{:S(2)}, u32[]{:S(2)}) collective-permute-start(f16[16,2176]{1,0:T(8,128)(2,1)S(1)} %pad_maximum_fusion.7), channel_id=1, source_target_pairs={{0,8},{1,9},{2,10},{3,11},{4,12},{5,13},{6,14},{7,15},{8,0},{9,1},... | collective-permute-start | bytes 208904 | tf_op jit(solution)/shard_map/ppermute | solution.py:24
  45.5 5.5 %collective-permute-start.16 = (f16[16,2048]{1,0:T(8,128)(2,1)S(1)}, f16[16,2048]{1,0:T(8,128)(2,1)S(1)}, u32[]{:S(2)}, u32[]{:S(2)}) collective-permute-start(f16[16,2048]{1,0:T(8,128)(2,1)S(1)} %get-tuple-element.43), channel_id=1, source_target_pairs={{0,6},{1,7},{2,4},{3,5},{4,2},{5,3},{6,0},{7,1},{8,14},{9,15},{10,... | collective-permute-start | bytes 196616 | tf_op jit(solution)/shard_map/ppermute | solution.py:24

commit v8 on v7

--- a/solution.py
+++ b/solution.py
@@ -75,8 +75,8 @@
     last = [after(x, got[w]) for x, w in zip(last, (2, 3))]
     last = [swap(x, n - 2 + j, n) for j, x in enumerate(last)]
     far = [got[m] for m in range(half, 2 * half - 1)]
-    passed = swap(jnp.concatenate([x[own:] for x in far]), 1, n)
-    rows = [got[m] for m in range(half)] + [x[:own] for x in far] + [passed] + last
+    passed = [swap(jnp.concatenate([x[own:] for x in part]), 1, n) for part in (far[:1], far[1:])]
+    rows = [got[m] for m in range(half)] + [x[:own] for x in far] + passed + last
     return jnp.concatenate(rows), got[1]
 
 
@@ -86,79 +86,71 @@
     return jnp.where((source < n // 2) | (source >= n - 2), source, far)
 
 
-def mean_kernel(parts, chol_ref, mean_ref, part_ref, staged_ref, sems):
+def stage_kernel(parts, chol_ref, mean_ref, staged_ref, means_ref, sems):
     step = chol_ref.shape[0] // parts
     copies = []
     for t in range(parts):
         at = pl.ds(t * step, step)
         copies.append(pltpu.make_async_copy(chol_ref.at[at], staged_ref.at[at], sems.at[t]))
-    for copy in copies[:2]:
-        copy.start()
-    mean = jnp.broadcast_to(mean_ref[...], (8, mean_ref.shape[1]))
-    for t, copy in enumerate(copies):
+        copies[-1].start()
+    means_ref[...] = jnp.broadcast_to(mean_ref[...], means_ref.shape)
+    for copy in copies:
         copy.wait()
-        if t + 2 < parts:
-            copies[t + 2].start()
-        at = pl.ds(t * step, step)
-        part = lax.dot_general(
-            mean, staged_ref[at, :], (((1,), (1,)), ((), ())), preferred_element_type=F32
-        )
-        part_ref[:, at] = part[:1]
-
-
-def mean_part(chol, mean, parts=4):
+
+
+def stage_chol(chol, mean, parts=4):
     return pl.pallas_call(
-        functools.partial(mean_kernel, parts),
+        functools.partial(stage_kernel, parts),
         in_specs=[pl.BlockSpec(memory_space=pl.ANY), pl.BlockSpec(memory_space=pltpu.VMEM)],
         out_specs=[pl.BlockSpec(memory_space=pltpu.VMEM)] * 2,
         out_shape=[
-            jax.ShapeDtypeStruct((1, chol.shape[0]), F32),
             jax.ShapeDtypeStruct(chol.shape, chol.dtype),
+            jax.ShapeDtypeStruct((16, mean.shape[1]), mean.dtype),
         ],
         scratch_shapes=[pltpu.SemaphoreType.DMA((parts,))],
         compiler_params=pltpu.CompilerParams(vmem_limit_bytes=40 * 2**20),
-        cost_estimate=pl.CostEstimate(
-            flops=16 * chol.size, bytes_accessed=2 * chol.size, transcendentals=0
-        ),
+        cost_estimate=pl.CostEstimate(flops=0, bytes_accessed=2 * chol.size, transcendentals=0),
     )(chol, mean)
 
 
-def bias_kernel(tile, index_ref, rows_ref, chol_ref, keep_ref, send_ref, picked):
+def bias_kernel(tile, index_ref, rows_ref, chol_ref, mean_ref, keep_ref, send_ref, field_ref, picked):
     half, nchol = keep_ref.shape
     walkers = rows_ref.shape[0]
     chosen = index_ref[...] == lax.broadcasted_iota(jnp.int32, (2 * half, walkers), 1)
-    picked[...] = jnp.dot(
+    picked[pl.ds(0, 2 * half), :] = jnp.dot(
         chosen.astype(BF16), rows_ref[...], preferred_element_type=F32
     ).astype(BF16)
-
+    picked[pl.ds(2 * half, 16), :] = mean_ref[...]
     for t in range(nchol // tile):
         at = pl.ds(t * tile, tile)
         part = lax.dot_general(
             picked[...], chol_ref[at, :], (((1,), (1,)), ((), ())), preferred_element_type=F32
         )
         keep_ref[:, at] = part[:half]
-        send_ref[:, at] = part[half:].astype(BF16)
-
-
-def partial_bias(index, rows, chol, tile):
+        send_ref[:, at] = part[half : 2 * half].astype(BF16)
+        field_ref[:, at] = part[2 * half : 2 * half + 1]
+
+
+def partial_bias(index, rows, chol, mean, tile):
     slots, (nchol, pairs) = index.shape[0], chol.shape
     half = slots // 2
     return pl.pallas_call(
         functools.partial(bias_kernel, tile),
-        in_specs=[pl.BlockSpec(memory_space=pltpu.VMEM)] * 3,
-        out_specs=[pl.BlockSpec(memory_space=pltpu.VMEM)] * 2,
+        in_specs=[pl.BlockSpec(memory_space=pltpu.VMEM)] * 4,
+        out_specs=[pl.BlockSpec(memory_space=pltpu.VMEM)] * 3,
         out_shape=[
             jax.ShapeDtypeStruct((half, nchol), F32),
             jax.ShapeDtypeStruct((half, nchol), BF16),
+            jax.ShapeDtypeStruct((1, nchol), F32),
         ],
-        scratch_shapes=[pltpu.VMEM((slots, pairs), BF16)],
+        scratch_shapes=[pltpu.VMEM((slots + 16, pairs), BF16)],
         compiler_params=pltpu.CompilerParams(vmem_limit_bytes=28 * 2**20),
         cost_estimate=pl.CostEstimate(
             flops=2 * slots * pairs * (nchol + rows.shape[0]),
             bytes_accessed=2 * nchol * pairs + 2 * rows.size + 6 * half * nchol,
             transcendentals=0,
         ),
-    )(index, rows, chol)
+    )(index, rows, chol, mean)
 
 
 def swap_both(x, extra, mask, n):
@@ -212,10 +204,10 @@
         index = place_of_source(source, n) * own + index % own
     else:
         rows = lax.all_to_all(greens, "chol", split_axis=1, concat_axis=0, tiled=True)
-    mean, chol = mean_part(chol_vectors, mean_row)
+    chol, means = stage_chol(chol_vectors, mean_row)
+    keep, send, mean = partial_bias(index[:, None], after(rows, means), chol, means, 512)
     mean = mean.reshape(own, -1)
     mean = mean + swap(mean, 1, n)
-    keep, send = partial_bias(index[:, None], after(rows, mean), chol, 512)
     held = keep + swap(send, 1, n).astype(F32)
     raw_bias, mean = reduce_over_chips(held.reshape(chips, own, -1), mean, radices, n)
     return noise_field - (jnp.tanh(raw_bias) - mean.reshape(1, -1))

time: 51.9 us -> 51.6 us (level)
  Pallas kernels: 7.4 us -> 6.36 us
  starting transfers between devices: 25.5 us -> 26.3 us
    pallas_call x1, Pallas kernels: 4.7 us -> 3.5 us  [stage_chol(): pl.pallas_call(functools.partial(stage_kernel, parts), in_specs=[pl.Block...]
    ppermute x17 -> x18, starting transfers between devices: 25.5 us -> 26.3 us  [swap(): return lax.ppermute(x, 'chol', [(i, i ^ mask) for i in range(n)])]
    ppermute x17 -> x18, waiting for transfers between devices: 13.4 us -> 13.4 us  [swap(): return lax.ppermute(x, 'chol', [(i, i ^ mask) for i in range(n)])]
    unnamed x9 -> x10, local copies, waits for them, and re-layouts: 1.28 us -> 1.28 us
  transfers between devices with their start and end apart: 17 -> 18, of which waited for: 10 -> 8; matrix products, arithmetic and copies ran while one was open for 5% -> 5% of each run, Pallas kernels for 9% -> 7%
where the time goes in v8:
time: 51.6 us; the launch traced here: 51.4 us
  starting transfers between devices  26.3 us (51%)
  waiting for transfers between devices  13.4 us (26%)
  Pallas kernels  6.36 us (12%)
  local copies, waits for them, and re-layouts  3.58 us (7%)
  other arithmetic  1.48 us (3%)
    ppermute x18, starting transfers between devices, swap(): return lax.ppermute(x, 'chol', [(i, i ^ mask) for i in range(n)])  26.3 us
    ppermute x18, waiting for transfers between devices, swap(): return lax.ppermute(x, 'chol', [(i, i ^ mask) for i in range(n)])  13.4 us
    pallas_call x1, Pallas kernels, stage_chol(): pl.pallas_call(functools.partial(stage_kernel, parts), in_specs=[pl.Block...  3.5 us
    pallas_call x1, Pallas kernels, partial_bias(): pl.pallas_call(functools.partial(bias_kernel, tile), in_specs=[pl.BlockSp...  2.79 us
    unnamed x10, local copies, waits for them, and re-layouts  1.28 us
  transfers between devices with their start and end apart: 18, of which 8 were waited for; matrix products, arithmetic and copies ran while one was open for 5% of the time, Pallas kernels for 7%

profile of v8, /device:TPU:0, one launch (start us, length us, event | category | flops | bytes accessed | tf_op | source)
XLA Modules:
  0.0 51.4 jit_solution(10718841490855570288)
XLA Ops:
  0.0 0.0 copy-start
  0.0 1.2 %copy-done = bf16[16,32768]{1,0:T(8,128)(2,1)S(1)} copy-done((bf16[16,32768]{1,0:T(8,128)(2,1)S(1)}, bf16[16,32768]{1,0:T(8,128)(2,1)}, u32[]{:S(2)}) %copy-start) | copy-done | bytes 1048600
  1.2 0.1 shard_map.55
  1.3 4.1 %collective-permute-start.4 = (bf16[32,2048]{1,0:T(8,128)(2,1)S(1)}, bf16[32,2048]{1,0:T(8,128)(2,1)S(1)}, u32[]{:S(2)}, u32[]{:S(2)}) collective-permute-start(bf16[32,2048]{1,0:T(8,128)(2,1)S(1)} %get-tuple-element.24), channel_id=1, source_target_pairs={{0,8},{1,9},{2,10},{3,11},{4,12},{5,13},{6,14},{7,15},{8,0},{9,1},... | collective-permute-start | bytes 393224 | tf_op jit(solution)/shard_map/ppermute | solution.py:24
  5.4 1.3 %collective-permute-start.6 = (bf16[32,2048]{1,0:T(8,128)(2,1)S(1)}, bf16[32,2048]{1,0:T(8,128)(2,1)S(1)}, u32[]{:S(2)}, u32[]{:S(2)}) collective-permute-start(bf16[32,2048]{1,0:T(8,128)(2,1)S(1)} %get-tuple-element.27), channel_id=1, source_target_pairs={{0,12},{1,13},{2,14},{3,15},{4,8},{5,9},{6,10},{7,11},{8,4},{9,5},... | collective-permute-start | bytes 393224 | tf_op jit(solution)/shard_map/ppermute | solution.py:24
  6.7 0.0 collective-permute-start
  6.8 0.7 %broadcast_in_dim.4.mean_ref = bf16[1,2048]{1,0:T(2,128)(2,1)S(1)} reshape(bf16[2048]{0:T(1024)(128)(2,1)} %param.6) | data formatting | bytes 8192 | tf_op jit(solution)/shard_map/broadcast_in_dim | solution.py:199
  7.5 0.8 %reshape.413 = s32[16,16]{1,0:T(8,128)S(1)} reshape(s32[256]{0:T(256)} %param.8) | data formatting | bytes 2048 | tf_op jit(solution)/shard_map/reshape | solution.py:197
  8.2 0.6 %gather_fusion = s32[16,16]{1,0:T(8,128)S(1)} fusion(s32[16,16]{1,0:T(8,128)S(1)} %reshape.413, s32[1024]{0:T(1024)S(1)} %pad_clamp_fusion), kind=kCustom, calls=%fused_computation | custom fusion | bytes 2112 | tf_op jit(solution)/shard_map/gather | solution.py:197
  8.8 0.1 reshape.442
  8.9 0.0 collective-permute-done
  9.0 1.6 %collective-permute-start.1 = (bf16[32,2048]{1,0:T(8,128)(2,1)S(1)}, bf16[32,2048]{1,0:T(8,128)(2,1)S(1)}, u32[]{:S(2)}, u32[]{:S(2)}) collective-permute-start(bf16[32,2048]{1,0:T(8,128)(2,1)S(1)} %pad_maximum_fusion.2), channel_id=1, source_target_pairs={{0,2},{1,3},{2,0},{3,1},{4,6},{5,7},{6,4},{7,5},{8,10},{9,11},{10,... | collective-permute-start | bytes 393224 | tf_op jit(solution)/shard_map/ppermute | solution.py:24
  10.6 0.3 collective-permute-start.2
  10.9 1.8 %collective-permute-start.3 = (bf16[32,2048]{1,0:T(8,128)(2,1)S(1)}, bf16[32,2048]{1,0:T(8,128)(2,1)S(1)}, u32[]{:S(2)}, u32[]{:S(2)}) collective-permute-start(bf16[32,2048]{1,0:T(8,128)(2,1)S(1)} %pad_maximum_fusion.4), channel_id=1, source_target_pairs={{0,6},{1,7},{2,4},{3,5},{4,2},{5,3},{6,0},{7,1},{8,14},{9,15},{10,... | collective-permute-start | bytes 393224 | tf_op jit(solution)/shard_map/ppermute | solution.py:24
  12.7 0.3 fusion.7.index_ref
  13.0 2.0 %collective-permute-done.1 = bf16[32,2048]{1,0:T(8,128)(2,1)S(1)} collective-permute-done((bf16[32,2048]{1,0:T(8,128)(2,1)S(1)}, bf16[32,2048]{1,0:T(8,128)(2,1)S(1)}, u32[]{:S(2)}, u32[]{:S(2)}) %collective-permute-start.1) | collective-permute-done | bytes 131104 | tf_op jit(solution)/shard_map/ppermute | solution.py:24
  15.0 2.6 %collective-permute-start.5 = (bf16[32,2048]{1,0:T(8,128)(2,1)S(1)}, bf16[32,2048]{1,0:T(8,128)(2,1)S(1)}, u32[]{:S(2)}, u32[]{:S(2)}) collective-permute-start(bf16[32,2048]{1,0:T(8,128)(2,1)S(1)} %get-tuple-element.26), channel_id=1, source_target_pairs={{0,10},{1,11},{2,8},{3,9},{4,14},{5,15},{6,12},{7,13},{8,2},{9,3},... | collective-permute-start | bytes 393224 | tf_op jit(solution)/shard_map/ppermute | solution.py:24
  17.6 0.0 collective-permute-done.2
  17.6 4.3 %collective-permute-start.9 = (bf16[16,2048]{1,0:T(8,128)(2,1)S(1)}, bf16[16,2048]{1,0:T(8,128)(2,1)S(1)}, u32[]{:S(2)}, u32[]{:S(2)}) collective-permute-start(bf16[16,2048]{1,0:T(8,128)(2,1)S(1)} %get-tuple-element.29), channel_id=1, source_target_pairs={{0,14},{1,15},{2,12},{3,13},{4,10},{5,11},{6,8},{7,9},{8,6},{9,7},... | collective-permute-start | bytes 196616 | tf_op jit(solution)/shard_map/ppermute | solution.py:24
  21.9 0.4 collective-permute-done.3
  22.3 2.3 %collective-permute-start.10 = (bf16[16,2048]{1,0:T(8,128)(2,1)S(1)}, bf16[16,2048]{1,0:T(8,128)(2,1)S(1)}, u32[]{:S(2)}, u32[]{:S(2)}) collective-permute-start(bf16[16,2048]{1,0:T(8,128)(2,1)S(1)} %get-tuple-element.31), channel_id=1, source_target_pairs={{0,15},{1,14},{2,13},{3,12},{4,11},{5,10},{6,9},{7,8},{8,7},{9,6},... | collective-permute-start | bytes 196616 | tf_op jit(solution)/shard_map/ppermute | solution.py:24
  24.7 0.0 collective-permute-done.4
  24.7 0.5 %collective-permute-start.7 = (bf16[16,2048]{1,0:T(8,128)(2,1)S(1)}, bf16[16,2048]{1,0:T(8,128)(2,1)S(1)}, u32[]{:S(2)}, u32[]{:S(2)}) collective-permute-start(bf16[16,2048]{1,0:T(8,128)(2,1)S(1)} %get-tuple-element.61), channel_id=1, source_target_pairs={{0,1},{1,0},{2,3},{3,2},{4,5},{5,4},{6,7},{7,6},{8,9},{9,8},{10,11... | collective-permute-start | bytes 196616 | tf_op jit(solution)/shard_map/ppermute | solution.py:24
  25.3 3.5 %shard_map.56 = (bf16[2048,2048]{1,0:T(8,128)(2,1)S(1)}, bf16[16,2048]{1,0:T(8,128)(2,1)S(1)}) custom-call(bf16[2048,2048]{1,0:T(8,128)(2,1)} %chol_ref.1, bf16[1,2048]{1,0:T(2,128)(2,1)S(1)} %broadcast_in_dim.4.mean_ref), custom_call_target="tpu_custom_call" | custom-call | bytes 8388608 | tf_op jit(solution)/shard_map/pallas_call | solution.py:102
  28.8 0.0 collective-permute-done.5
  28.8 0.0 collective-permute-done.6
  28.9 0.1 collective-permute-start.8
  29.0 0.0 collective-permute-done.7
  29.0 1.3 %collective-permute-done.8 = bf16[32,2048]{1,0:T(8,128)(2,1)S(1)} collective-permute-done((bf16[32,2048]{1,0:T(8,128)(2,1)S(1)}, bf16[32,2048]{1,0:T(8,128)(2,1)S(1)}, u32[]{:S(2)}, u32[]{:S(2)}) %collective-permute-start.8) | collective-permute-done | bytes 131104 | tf_op jit(solution)/shard_map/ppermute | solution.py:24
  30.3 0.0 collective-permute-done.9
  30.3 0.0 collective-permute-done.10
  30.3 0.0 copy-start.1
  30.3 2.8 %shard_map.57 = (f32[128,2048]{1,0:T(8,128)S(1)}, bf16[128,2048]{1,0:T(8,128)(2,1)S(1)}, f32[1,2048]{1,0:T(1,128)S(1)}) custom-call(s32[256,1]{1,0:T(8,128)S(1)} %fusion.7.index_ref, bf16[256,2048]{1,0:T(8,128)(2,1)S(1)} %constant_dynamic-update-slice_fusion.rows_ref, bf16[2048,2048]{1,0:T(8,128)(2,1)S(1)} %get-tuple-element.35.chol_ref, ...), custom_call_target="tpu_custom_call" | custom-call | flops 2415919104 | bytes 11010048 | tf_op jit(solution)/shard_map/pallas_call | solution.py:137
  33.1 0.2 collective-permute-start.11
  33.4 0.4 collective-permute-start.12
  33.7 1.4 %collective-permute-done.12 = f32[16,128]{1,0:T(8,128)S(1)} collective-permute-done((f32[16,128]{1,0:T(8,128)S(1)}, f32[16,128]{1,0:T(8,128)S(1)}, u32[]{:S(2)}, u32[]{:S(2)}) %collective-permute-start.12) | collective-permute-done | bytes 8224 | tf_op jit(solution)/shard_map/ppermute | solution.py:24
  35.1 0.0 collective-permute-done.11
  35.1 0.2 fusion.30
  35.5 1.0 %collective-permute-start.13 = (f16[16,2176]{1,0:T(8,128)(2,1)S(1)}, f16[16,2176]{1,0:T(8,128)(2,1)S(1)}, u32[]{:S(2)}, u32[]{:S(2)}) collective-permute-start(f16[16,2176]{1,0:T(8,128)(2,1)S(1)} %pad_maximum_fusion.6), channel_id=1, source_target_pairs={{0,6},{1,7},{2,4},{3,5},{4,2},{5,3},{6,0},{7,1},{8,14},{9,15},{10,... | collective-permute-start | bytes 208904 | tf_op jit(solution)/shard_map/ppermute | solution.py:24
  36.5 0.1 pad_maximum_fusion.1
  36.6 0.6 %collective-permute-start.14 = (f16[32,2176]{1,0:T(8,128)(2,1)S(1)}, f16[32,2176]{1,0:T(8,128)(2,1)S(1)}, u32[]{:S(2)}, u32[]{:S(2)}) collective-permute-start(f16[32,2176]{1,0:T(8,128)(2,1)S(1)} %get-tuple-element.63), channel_id=1, source_target_pairs={{0,2},{1,3},{2,0},{3,1},{4,6},{5,7},{6,4},{7,5},{8,10},{9,11},{10,... | collective-permute-start | bytes 417800 | tf_op jit(solution)/shard_map/ppermute | solution.py:24
  37.2 2.0 %collective-permute-start.15 = (f16[32,2176]{1,0:T(8,128)(2,1)S(1)}, f16[32,2176]{1,0:T(8,128)(2,1)S(1)}, u32[]{:S(2)}, u32[]{:S(2)}) collective-permute-start(f16[32,2176]{1,0:T(8,128)(2,1)S(1)} %get-tuple-element.64), channel_id=1, source_target_pairs={{0,4},{1,5},{2,6},{3,7},{4,0},{5,1},{6,2},{7,3},{8,12},{9,13},{10,... | collective-permute-start | bytes 417800 | tf_op jit(solution)/shard_map/ppermute | solution.py:24
  39.2 1.8 %collective-permute-done.13 = f16[16,2176]{1,0:T(8,128)(2,1)S(1)} collective-permute-done((f16[16,2176]{1,0:T(8,128)(2,1)S(1)}, f16[16,2176]{1,0:T(8,128)(2,1)S(1)}, u32[]{:S(2)}, u32[]{:S(2)}) %collective-permute-start.13) | collective-permute-done | bytes 69664 | tf_op jit(solution)/shard_map/ppermute | solution.py:24
  41.1 2.6 %collective-permute-done.14 = f16[32,2176]{1,0:T(8,128)(2,1)S(1)} collective-permute-done((f16[32,2176]{1,0:T(8,128)(2,1)S(1)}, f16[32,2176]{1,0:T(8,128)(2,1)S(1)}, u32[]{:S(2)}, u32[]{:S(2)}) %collective-permute-start.14) | collective-permute-done | bytes 139296 | tf_op jit(solution)/shard_map/ppermute | solution.py:24
  43.7 0.0 collective-permute-done.15
  43.8 1.6 %collective-permute-start.16 = (f16[16,2176]{1,0:T(8,128)(2,1)S(1)}, f16[16,2176]{1,0:T(8,128)(2,1)S(1)}, u32[]{:S(2)}, u32[]{:S(2)}) collective-permute-start(f16[16,2176]{1,0:T(8,128)(2,1)S(1)} %pad_maximum_fusion.7), channel_id=1, source_target_pairs={{0,8},{1,9},{2,10},{3,11},{4,12},{5,13},{6,14},{7,15},{8,0},{9,1},... | collective-permute-start | bytes 208904 | tf_op jit(solution)/shard_map/ppermute | solution.py:24
  45.5 1.4 %collective-permute-start.17 = (f16[16,2048]{1,0:T(8,128)(2,1)S(1)}, f16[16,2048]{1,0:T(8,128)(2,1)S(1)}, u32[]{:S(2)}, u32[]{:S(2)}) collective-permute-start(f16[16,2048]{1,0:T(8,128)(2,1)S(1)} %get-tuple-element.45), channel_id=1, source_target_pairs={{0,6},{1,7},{2,4},{3,5},{4,2},{5,3},{6,0},{7,1},{8,14},{9,15},{10,... | collective-permute-start | bytes 196616 | tf_op jit(solution)/shard_map/ppermute | solution.py:24
  46.8 3.0 %collective-permute-done.16 = f16[16,2176]{1,0:T(8,128)(2,1)S(1)} collective-permute-done((f16[16,2176]{1,0:T(8,128)(2,1)S(1)}, f16[16,2176]{1,0:T(8,128)(2,1)S(1)}, u32[]{:S(2)}, u32[]{:S(2)}) %collective-permute-start.16) | collective-permute-done | bytes 69664 | tf_op jit(solution)/shard_map/ppermute | solution.py:24
  49.9 0.8 %collective-permute-done.17 = f16[16,2048]{1,0:T(8,128)(2,1)S(1)} collective-permute-done((f16[16,2048]{1,0:T(8,128)(2,1)S(1)}, f16[16,2048]{1,0:T(8,128)(2,1)S(1)}, u32[]{:S(2)}, u32[]{:S(2)}) %collective-permute-start.17) | collective-permute-done | bytes 65568 | tf_op jit(solution)/shard_map/ppermute | solution.py:24
  50.7 0.0 copy-done.1
  50.7 0.7 %fusion.12 = f32[16,2048]{1,0:T(8,128)} fusion(f32[16,2048]{1,0:T(8,128)S(1)} %copy-done.1, f32[1,16,2176]{2,1,0:T(8,128)S(1)} %bitcast_convert_fusion, f32[2,16,2048]{2,1,0:T(8,128)S(1)} %slice_add_fusion, f16[16,2048]{1,0:T(8,128)(2,1)S(1)} %collective-permute-done.17, f32[2048]{0:T(1024)S(1)} %fusion.19), kind=kLoop, calls=%fused_computation.29 | loop fusion | flops 163840 | bytes 598016 | tf_op jit(solution)/shard_map/sub | solution.py:213
  (34 shorter events, 0.5 us)
Async XLA Ops:
  0.0 1.2 %copy-start = (bf16[16,32768]{1,0:T(8,128)(2,1)S(1)}, bf16[16,32768]{1,0:T(8,128)(2,1)}, u32[]{:S(2)}) copy-start(bf16[16,32768]{1,0:T(8,128)(2,1)} %greens_ref.1) | copy-start | bytes 3145732
  1.3 23.4 %collective-permute-start.4 = (bf16[32,2048]{1,0:T(8,128)(2,1)S(1)}, bf16[32,2048]{1,0:T(8,128)(2,1)S(1)}, u32[]{:S(2)}, u32[]{:S(2)}) collective-permute-start(bf16[32,2048]{1,0:T(8,128)(2,1)S(1)} %get-tuple-element.24), channel_id=1, source_target_pairs={{0,8},{1,9},{2,10},{3,11},{4,12},{5,13},{6,14},{7,15},{8,0},{9,1},... | collective-permute-start | bytes 393224 | tf_op jit(solution)/shard_map/ppermute | solution.py:24
  5.4 23.4 %collective-permute-start.6 = (bf16[32,2048]{1,0:T(8,128)(2,1)S(1)}, bf16[32,2048]{1,0:T(8,128)(2,1)S(1)}, u32[]{:S(2)}, u32[]{:S(2)}) collective-permute-start(bf16[32,2048]{1,0:T(8,128)(2,1)S(1)} %get-tuple-element.27), channel_id=1, source_target_pairs={{0,12},{1,13},{2,14},{3,15},{4,8},{5,9},{6,10},{7,11},{8,4},{9,5},... | collective-permute-start | bytes 393224 | tf_op jit(solution)/shard_map/ppermute | solution.py:24
  6.7 2.2 %collective-permute-start = (bf16[64,2048]{1,0:T(8,128)(2,1)S(1)}, bf16[64,2048]{1,0:T(8,128)(2,1)S(1)}, u32[]{:S(2)}, u32[]{:S(2)}) collective-permute-start(bf16[64,2048]{1,0:T(8,128)(2,1)S(1)} %get-tuple-element.23), channel_id=1, source_target_pairs={{0,1},{1,0},{2,3},{3,2},{4,5},{5,4},{6,7},{7,6},{8,9},{9,8},{10,11... | collective-permute-start | bytes 786440 | tf_op jit(solution)/shard_map/ppermute | solution.py:24
  9.0 6.0 %collective-permute-start.1 = (bf16[32,2048]{1,0:T(8,128)(2,1)S(1)}, bf16[32,2048]{1,0:T(8,128)(2,1)S(1)}, u32[]{:S(2)}, u32[]{:S(2)}) collective-permute-start(bf16[32,2048]{1,0:T(8,128)(2,1)S(1)} %pad_maximum_fusion.2), channel_id=1, source_target_pairs={{0,2},{1,3},{2,0},{3,1},{4,6},{5,7},{6,4},{7,5},{8,10},{9,11},{10,... | collective-permute-start | bytes 393224 | tf_op jit(solution)/shard_map/ppermute | solution.py:24
  10.6 7.0 %collective-permute-start.2 = (bf16[32,2048]{1,0:T(8,128)(2,1)S(1)}, bf16[32,2048]{1,0:T(8,128)(2,1)S(1)}, u32[]{:S(2)}, u32[]{:S(2)}) collective-permute-start(bf16[32,2048]{1,0:T(8,128)(2,1)S(1)} %pad_maximum_fusion.3), channel_id=1, source_target_pairs={{0,4},{1,5},{2,6},{3,7},{4,0},{5,1},{6,2},{7,3},{8,12},{9,13},{10,... | collective-permute-start | bytes 393224 | tf_op jit(solution)/shard_map/ppermute | solution.py:24
  10.9 11.4 %collective-permute-start.3 = (bf16[32,2048]{1,0:T(8,128)(2,1)S(1)}, bf16[32,2048]{1,0:T(8,128)(2,1)S(1)}, u32[]{:S(2)}, u32[]{:S(2)}) collective-permute-start(bf16[32,2048]{1,0:T(8,128)(2,1)S(1)} %pad_maximum_fusion.4), channel_id=1, source_target_pairs={{0,6},{1,7},{2,4},{3,5},{4,2},{5,3},{6,0},{7,1},{8,14},{9,15},{10,... | collective-permute-start | bytes 393224 | tf_op jit(solution)/shard_map/ppermute | solution.py:24
  15.0 13.8 %collective-permute-start.5 = (bf16[32,2048]{1,0:T(8,128)(2,1)S(1)}, bf16[32,2048]{1,0:T(8,128)(2,1)S(1)}, u32[]{:S(2)}, u32[]{:S(2)}) collective-permute-start(bf16[32,2048]{1,0:T(8,128)(2,1)S(1)} %get-tuple-element.26), channel_id=1, source_target_pairs={{0,10},{1,11},{2,8},{3,9},{4,14},{5,15},{6,12},{7,13},{8,2},{9,3},... | collective-permute-start | bytes 393224 | tf_op jit(solution)/shard_map/ppermute | solution.py:24
  17.6 12.7 %collective-permute-start.9 = (bf16[16,2048]{1,0:T(8,128)(2,1)S(1)}, bf16[16,2048]{1,0:T(8,128)(2,1)S(1)}, u32[]{:S(2)}, u32[]{:S(2)}) collective-permute-start(bf16[16,2048]{1,0:T(8,128)(2,1)S(1)} %get-tuple-element.29), channel_id=1, source_target_pairs={{0,14},{1,15},{2,12},{3,13},{4,10},{5,11},{6,8},{7,9},{8,6},{9,7},... | collective-permute-start | bytes 196616 | tf_op jit(solution)/shard_map/ppermute | solution.py:24
  22.3 8.0 %collective-permute-start.10 = (bf16[16,2048]{1,0:T(8,128)(2,1)S(1)}, bf16[16,2048]{1,0:T(8,128)(2,1)S(1)}, u32[]{:S(2)}, u32[]{:S(2)}) collective-permute-start(bf16[16,2048]{1,0:T(8,128)(2,1)S(1)} %get-tuple-element.31), channel_id=1, source_target_pairs={{0,15},{1,14},{2,13},{3,12},{4,11},{5,10},{6,9},{7,8},{8,7},{9,6},... | collective-permute-start | bytes 196616 | tf_op jit(solution)/shard_map/ppermute | solution.py:24
  24.7 4.2 %collective-permute-start.7 = (bf16[16,2048]{1,0:T(8,128)(2,1)S(1)}, bf16[16,2048]{1,0:T(8,128)(2,1)S(1)}, u32[]{:S(2)}, u32[]{:S(2)}) collective-permute-start(bf16[16,2048]{1,0:T(8,128)(2,1)S(1)} %get-tuple-element.61), channel_id=1, source_target_pairs={{0,1},{1,0},{2,3},{3,2},{4,5},{5,4},{6,7},{7,6},{8,9},{9,8},{10,11... | collective-permute-start | bytes 196616 | tf_op jit(solution)/shard_map/ppermute | solution.py:24
  28.9 1.4 %collective-permute-start.8 = (bf16[32,2048]{1,0:T(8,128)(2,1)S(1)}, bf16[32,2048]{1,0:T(8,128)(2,1)S(1)}, u32[]{:S(2)}, u32[]{:S(2)}) collective-permute-start(bf16[32,2048]{1,0:T(8,128)(2,1)S(1)} %pad_maximum_fusion.5), channel_id=1, source_target_pairs={{0,1},{1,0},{2,3},{3,2},{4,5},{5,4},{6,7},{7,6},{8,9},{9,8},{10,11... | collective-permute-start | bytes 393224 | tf_op jit(solution)/shard_map/ppermute | solution.py:24
  30.3 20.3 %copy-start.1 = (f32[16,2048]{1,0:T(8,128)S(1)}, f32[16,2048]{1,0:T(8,128)}, u32[]{:S(2)}) copy-start(f32[16,2048]{1,0:T(8,128)} %param.9) | copy-start | bytes 393220
  33.1 2.0 %collective-permute-start.11 = (bf16[128,2048]{1,0:T(8,128)(2,1)S(1)}, bf16[128,2048]{1,0:T(8,128)(2,1)S(1)}, u32[]{:S(2)}, u32[]{:S(2)}) collective-permute-start(bf16[128,2048]{1,0:T(8,128)(2,1)S(1)} %get-tuple-element.37), channel_id=1, source_target_pairs={{0,1},{1,0},{2,3},{3,2},{4,5},{5,4},{6,7},{7,6},{8,9},{9,8},{10,11... | collective-permute-start | bytes 1572872 | tf_op jit(solution)/shard_map/ppermute | solution.py:24
  33.4 1.8 %collective-permute-start.12 = (f32[16,128]{1,0:T(8,128)S(1)}, f32[16,128]{1,0:T(8,128)S(1)}, u32[]{:S(2)}, u32[]{:S(2)}) collective-permute-start(f32[16,128]{1,0:T(8,128)S(1)} %bitcast.60), channel_id=1, source_target_pairs={{0,1},{1,0},{2,3},{3,2},{4,5},{5,4},{6,7},{7,6},{8,9},{9,8},{10,11... | collective-permute-start | bytes 24584 | tf_op jit(solution)/shard_map/ppermute | solution.py:24
  35.5 5.6 %collective-permute-start.13 = (f16[16,2176]{1,0:T(8,128)(2,1)S(1)}, f16[16,2176]{1,0:T(8,128)(2,1)S(1)}, u32[]{:S(2)}, u32[]{:S(2)}) collective-permute-start(f16[16,2176]{1,0:T(8,128)(2,1)S(1)} %pad_maximum_fusion.6), channel_id=1, source_target_pairs={{0,6},{1,7},{2,4},{3,5},{4,2},{5,3},{6,0},{7,1},{8,14},{9,15},{10,... | collective-permute-start | bytes 208904 | tf_op jit(solution)/shard_map/ppermute | solution.py:24
  36.6 7.1 %collective-permute-start.14 = (f16[32,2176]{1,0:T(8,128)(2,1)S(1)}, f16[32,2176]{1,0:T(8,128)(2,1)S(1)}, u32[]{:S(2)}, u32[]{:S(2)}) collective-permute-start(f16[32,2176]{1,0:T(8,128)(2,1)S(1)} %get-tuple-element.63), channel_id=1, source_target_pairs={{0,2},{1,3},{2,0},{3,1},{4,6},{5,7},{6,4},{7,5},{8,10},{9,11},{10,... | collective-permute-start | bytes 417800 | tf_op jit(solution)/shard_map/ppermute | solution.py:24
  37.2 6.5 %collective-permute-start.15 = (f16[32,2176]{1,0:T(8,128)(2,1)S(1)}, f16[32,2176]{1,0:T(8,128)(2,1)S(1)}, u32[]{:S(2)}, u32[]{:S(2)}) collective-permute-start(f16[32,2176]{1,0:T(8,128)(2,1)S(1)} %get-tuple-element.64), channel_id=1, source_target_pairs={{0,4},{1,5},{2,6},{3,7},{4,0},{5,1},{6,2},{7,3},{8,12},{9,13},{10,... | collective-permute-start | bytes 417800 | tf_op jit(solution)/shard_map/ppermute | solution.py:24
  43.8 6.0 %collective-permute-start.16 = (f16[16,2176]{1,0:T(8,128)(2,1)S(1)}, f16[16,2176]{1,0:T(8,128)(2,1)S(1)}, u32[]{:S(2)}, u32[]{:S(2)}) collective-permute-start(f16[16,2176]{1,0:T(8,128)(2,1)S(1)} %pad_maximum_fusion.7), channel_id=1, source_target_pairs={{0,8},{1,9},{2,10},{3,11},{4,12},{5,13},{6,14},{7,15},{8,0},{9,1},... | collective-permute-start | bytes 208904 | tf_op jit(solution)/shard_map/ppermute | solution.py:24
  45.5 5.2 %collective-permute-start.17 = (f16[16,2048]{1,0:T(8,128)(2,1)S(1)}, f16[16,2048]{1,0:T(8,128)(2,1)S(1)}, u32[]{:S(2)}, u32[]{:S(2)}) collective-permute-start(f16[16,2048]{1,0:T(8,128)(2,1)S(1)} %get-tuple-element.45), channel_id=1, source_target_pairs={{0,6},{1,7},{2,4},{3,5},{4,2},{5,3},{6,0},{7,1},{8,14},{9,15},{10,... | collective-permute-start | bytes 196616 | tf_op jit(solution)/shard_map/ppermute | solution.py:24

commit v9 on v8

--- a/solution.py
+++ b/solution.py
@@ -179,6 +179,34 @@
     return held[0] + sum(mine), mean
 
 
+def swap_of_four(x, q, n):
+    partner = lambda i: i ^ 2 * (q if q == 3 or i % 2 == 0 else 3 - q)
+    return lax.ppermute(x, "chol", [(i, partner(i)) for i in range(n)])
+
+
+def reduce_over_eight(held, mean, n):
+    _, own, g = held.shape
+    held = held.reshape(4, 2, own, g)
+    columns = lambda x, extra: jnp.concatenate([x, extra], axis=-1).astype(F16)
+    none = jnp.zeros_like(mean)
+    messages = (
+        jnp.concatenate(
+            [columns(held[1, 1], mean), columns(held[1, 0], none), columns(held[3, 0], none)]
+        ),
+        columns(held[2, 1], mean),
+        columns(held[3, 1], mean),
+    )
+    messages = (messages[0],) + tuple(after(x, messages[0]) for x in messages[1:])
+    first, second, third = (
+        swap_of_four(x, q, n).astype(F32) for q, x in enumerate(messages, 1)
+    )
+    far = jnp.concatenate([held[0, 1], mean], axis=-1) + second + third + first[:own]
+    across = swap(far.astype(F16), n // 2, n).astype(F32)
+    passed = swap_of_four((held[2, 0] + first[2 * own :, :g]).astype(F16), 2, n).astype(F32)
+    total = held[0, 0] + first[own : 2 * own, :g] + passed + across[:, :g]
+    return total, far[:, g:] + across[:, g:]
+
+
 def per_device(n, chol_vectors, mean_greens, greens, walker_order, noise_field):
     me = lax.axis_index("chol")
     own = greens.shape[0]
@@ -193,6 +221,11 @@
             later *= r
         relative = relative + weight * (left // later)
         left, weight = left % later, weight * radix
+    if chips == 8:
+        core = jnp.bitwise_xor(place // chips, me) % 2
+        four = relative // 2 % 4
+        other = (core == 1) & ((four == 1) | (four == 2))
+        relative = jnp.where(other, jnp.bitwise_xor(relative, 6), relative)
     owners = jnp.bitwise_xor(relative, me)
     index = walker_order.reshape(n, own)[owners].reshape(-1)
 
@@ -209,7 +242,11 @@
     mean = mean.reshape(own, -1)
     mean = mean + swap(mean, 1, n)
     held = keep + swap(send, 1, n).astype(F32)
-    raw_bias, mean = reduce_over_chips(held.reshape(chips, own, -1), mean, radices, n)
+    held = held.reshape(chips, own, -1)
+    if chips == 8:
+        raw_bias, mean = reduce_over_eight(held, mean, n)
+    else:
+        raw_bias, mean = reduce_over_chips(held, mean, radices, n)
     return noise_field - (jnp.tanh(raw_bias) - mean.reshape(1, -1))
 
 

time: 51.6 us -> 51 us (0.988)
  starting transfers between devices: 26.3 us -> 25.7 us
    ppermute x18 -> x14, starting transfers between devices: 26.3 us -> 21.3 us  [swap(): return lax.ppermute(x, 'chol', [(i, i ^ mask) for i in range(n)])]
    ppermute x0 -> x4, waiting for transfers between devices: none -> 4.67 us  [swap_of_four(): return lax.ppermute(x, 'chol', [(i, partner(i)) for i in range(n)])]
    ppermute x18 -> x14, waiting for transfers between devices: 13.4 us -> 8.76 us  [swap(): return lax.ppermute(x, 'chol', [(i, i ^ mask) for i in range(n)])]
    ppermute x0 -> x4, starting transfers between devices: none -> 4.38 us  [swap_of_four(): return lax.ppermute(x, 'chol', [(i, partner(i)) for i in range(n)])]
  transfers between devices with their start and end apart: 18 -> 18, of which waited for: 8 -> 9; matrix products, arithmetic and copies ran while one was open for 5% -> 5% of each run, Pallas kernels for 7% -> 7%
where the time goes in v9:
time: 51 us; the launch traced here: 50.8 us
  starting transfers between devices  25.7 us (50%)
  waiting for transfers between devices  13.4 us (26%)
  Pallas kernels  6.36 us (12%)
  local copies, waits for them, and re-layouts  3.54 us (7%)
  other arithmetic  1.47 us (3%)
    ppermute x14, starting transfers between devices, swap(): return lax.ppermute(x, 'chol', [(i, i ^ mask) for i in range(n)])  21.3 us
    ppermute x14, waiting for transfers between devices, swap(): return lax.ppermute(x, 'chol', [(i, i ^ mask) for i in range(n)])  8.76 us
    ppermute x4, waiting for transfers between devices, swap_of_four(): return lax.ppermute(x, 'chol', [(i, partner(i)) for i in range(n)])  4.67 us
    ppermute x4, starting transfers between devices, swap_of_four(): return lax.ppermute(x, 'chol', [(i, partner(i)) for i in range(n)])  4.38 us
    pallas_call x1, Pallas kernels, stage_chol(): pl.pallas_call(functools.partial(stage_kernel, parts), in_specs=[pl.Block...  3.5 us
    pallas_call x1, Pallas kernels, partial_bias(): pl.pallas_call(functools.partial(bias_kernel, tile), in_specs=[pl.BlockSp...  2.79 us
    unnamed x10, local copies, waits for them, and re-layouts  1.28 us
  transfers between devices with their start and end apart: 18, of which 9 were waited for; matrix products, arithmetic and copies ran while one was open for 5% of the time, Pallas kernels for 7%

profile of v9, /device:TPU:0, one launch (start us, length us, event | category | flops | bytes accessed | tf_op | source)
XLA Modules:
  0.0 50.8 jit_solution(9899730021630989639)
XLA Ops:
  0.0 0.0 copy-start
  0.0 1.2 %copy-done = bf16[16,32768]{1,0:T(8,128)(2,1)S(1)} copy-done((bf16[16,32768]{1,0:T(8,128)(2,1)S(1)}, bf16[16,32768]{1,0:T(8,128)(2,1)}, u32[]{:S(2)}) %copy-start) | copy-done | bytes 1048600
  1.2 0.1 shard_map.55
  1.3 4.1 %collective-permute-start.4 = (bf16[32,2048]{1,0:T(8,128)(2,1)S(1)}, bf16[32,2048]{1,0:T(8,128)(2,1)S(1)}, u32[]{:S(2)}, u32[]{:S(2)}) collective-permute-start(bf16[32,2048]{1,0:T(8,128)(2,1)S(1)} %get-tuple-element.26), channel_id=1, source_target_pairs={{0,8},{1,9},{2,10},{3,11},{4,12},{5,13},{6,14},{7,15},{8,0},{9,1},... | collective-permute-start | bytes 393224 | tf_op jit(solution)/shard_map/ppermute | solution.py:24
  5.4 1.3 %collective-permute-start.6 = (bf16[32,2048]{1,0:T(8,128)(2,1)S(1)}, bf16[32,2048]{1,0:T(8,128)(2,1)S(1)}, u32[]{:S(2)}, u32[]{:S(2)}) collective-permute-start(bf16[32,2048]{1,0:T(8,128)(2,1)S(1)} %get-tuple-element.29), channel_id=1, source_target_pairs={{0,12},{1,13},{2,14},{3,15},{4,8},{5,9},{6,10},{7,11},{8,4},{9,5},... | collective-permute-start | bytes 393224 | tf_op jit(solution)/shard_map/ppermute | solution.py:24
  6.7 0.0 collective-permute-start
  6.8 0.7 %broadcast_in_dim.2.mean_ref = bf16[1,2048]{1,0:T(2,128)(2,1)S(1)} reshape(bf16[2048]{0:T(1024)(128)(2,1)} %param.6) | data formatting | bytes 8192 | tf_op jit(solution)/shard_map/broadcast_in_dim | solution.py:232
  7.5 0.8 %reshape.475 = s32[16,16]{1,0:T(8,128)S(1)} reshape(s32[256]{0:T(256)} %param.8) | data formatting | bytes 2048 | tf_op jit(solution)/shard_map/reshape | solution.py:230
  8.2 0.6 %gather_fusion = s32[16,16]{1,0:T(8,128)S(1)} fusion(s32[16,16]{1,0:T(8,128)S(1)} %reshape.475, s32[1024]{0:T(1024)S(1)} %pad_clamp_fusion), kind=kCustom, calls=%fused_computation | custom fusion | bytes 2112 | tf_op jit(solution)/shard_map/gather | solution.py:230
  8.8 0.1 reshape.486
  8.9 0.0 collective-permute-done
  9.0 1.6 %collective-permute-start.1 = (bf16[32,2048]{1,0:T(8,128)(2,1)S(1)}, bf16[32,2048]{1,0:T(8,128)(2,1)S(1)}, u32[]{:S(2)}, u32[]{:S(2)}) collective-permute-start(bf16[32,2048]{1,0:T(8,128)(2,1)S(1)} %pad_maximum_fusion), channel_id=1, source_target_pairs={{0,2},{1,3},{2,0},{3,1},{4,6},{5,7},{6,4},{7,5},{8,10},{9,11},{10,... | collective-permute-start | bytes 393224 | tf_op jit(solution)/shard_map/ppermute | solution.py:24
  10.6 0.3 collective-permute-start.2
  10.9 1.8 %collective-permute-start.3 = (bf16[32,2048]{1,0:T(8,128)(2,1)S(1)}, bf16[32,2048]{1,0:T(8,128)(2,1)S(1)}, u32[]{:S(2)}, u32[]{:S(2)}) collective-permute-start(bf16[32,2048]{1,0:T(8,128)(2,1)S(1)} %pad_maximum_fusion.2), channel_id=1, source_target_pairs={{0,6},{1,7},{2,4},{3,5},{4,2},{5,3},{6,0},{7,1},{8,14},{9,15},{10,... | collective-permute-start | bytes 393224 | tf_op jit(solution)/shard_map/ppermute | solution.py:24
  12.7 0.3 fusion.13.index_ref
  13.0 2.0 %collective-permute-done.1 = bf16[32,2048]{1,0:T(8,128)(2,1)S(1)} collective-permute-done((bf16[32,2048]{1,0:T(8,128)(2,1)S(1)}, bf16[32,2048]{1,0:T(8,128)(2,1)S(1)}, u32[]{:S(2)}, u32[]{:S(2)}) %collective-permute-start.1) | collective-permute-done | bytes 131104 | tf_op jit(solution)/shard_map/ppermute | solution.py:24
  15.0 2.6 %collective-permute-start.5 = (bf16[32,2048]{1,0:T(8,128)(2,1)S(1)}, bf16[32,2048]{1,0:T(8,128)(2,1)S(1)}, u32[]{:S(2)}, u32[]{:S(2)}) collective-permute-start(bf16[32,2048]{1,0:T(8,128)(2,1)S(1)} %get-tuple-element.28), channel_id=1, source_target_pairs={{0,10},{1,11},{2,8},{3,9},{4,14},{5,15},{6,12},{7,13},{8,2},{9,3},... | collective-permute-start | bytes 393224 | tf_op jit(solution)/shard_map/ppermute | solution.py:24
  17.6 0.0 collective-permute-done.2
  17.6 4.3 %collective-permute-start.9 = (bf16[16,2048]{1,0:T(8,128)(2,1)S(1)}, bf16[16,2048]{1,0:T(8,128)(2,1)S(1)}, u32[]{:S(2)}, u32[]{:S(2)}) collective-permute-start(bf16[16,2048]{1,0:T(8,128)(2,1)S(1)} %get-tuple-element.31), channel_id=1, source_target_pairs={{0,14},{1,15},{2,12},{3,13},{4,10},{5,11},{6,8},{7,9},{8,6},{9,7},... | collective-permute-start | bytes 196616 | tf_op jit(solution)/shard_map/ppermute | solution.py:24
  21.9 0.4 collective-permute-done.3
  22.3 2.3 %collective-permute-start.10 = (bf16[16,2048]{1,0:T(8,128)(2,1)S(1)}, bf16[16,2048]{1,0:T(8,128)(2,1)S(1)}, u32[]{:S(2)}, u32[]{:S(2)}) collective-permute-start(bf16[16,2048]{1,0:T(8,128)(2,1)S(1)} %get-tuple-element.33), channel_id=1, source_target_pairs={{0,15},{1,14},{2,13},{3,12},{4,11},{5,10},{6,9},{7,8},{8,7},{9,6},... | collective-permute-start | bytes 196616 | tf_op jit(solution)/shard_map/ppermute | solution.py:24
  24.7 0.0 collective-permute-done.4
  24.7 0.5 %collective-permute-start.7 = (bf16[16,2048]{1,0:T(8,128)(2,1)S(1)}, bf16[16,2048]{1,0:T(8,128)(2,1)S(1)}, u32[]{:S(2)}, u32[]{:S(2)}) collective-permute-start(bf16[16,2048]{1,0:T(8,128)(2,1)S(1)} %get-tuple-element.64), channel_id=1, source_target_pairs={{0,1},{1,0},{2,3},{3,2},{4,5},{5,4},{6,7},{7,6},{8,9},{9,8},{10,11... | collective-permute-start | bytes 196616 | tf_op jit(solution)/shard_map/ppermute | solution.py:24
  25.3 3.5 %shard_map.56 = (bf16[2048,2048]{1,0:T(8,128)(2,1)S(1)}, bf16[16,2048]{1,0:T(8,128)(2,1)S(1)}) custom-call(bf16[2048,2048]{1,0:T(8,128)(2,1)} %chol_ref.1, bf16[1,2048]{1,0:T(2,128)(2,1)S(1)} %broadcast_in_dim.2.mean_ref), custom_call_target="tpu_custom_call" | custom-call | bytes 8388608 | tf_op jit(solution)/shard_map/pallas_call | solution.py:102
  28.8 0.0 collective-permute-done.5
  28.8 0.0 collective-permute-done.6
  28.9 0.1 collective-permute-start.8
  29.0 0.0 collective-permute-done.7
  29.0 1.3 %collective-permute-done.8 = bf16[32,2048]{1,0:T(8,128)(2,1)S(1)} collective-permute-done((bf16[32,2048]{1,0:T(8,128)(2,1)S(1)}, bf16[32,2048]{1,0:T(8,128)(2,1)S(1)}, u32[]{:S(2)}, u32[]{:S(2)}) %collective-permute-start.8) | collective-permute-done | bytes 131104 | tf_op jit(solution)/shard_map/ppermute | solution.py:24
  30.3 0.0 collective-permute-done.9
  30.3 0.0 collective-permute-done.10
  30.3 0.0 copy-start.1
  30.3 2.8 %shard_map.57 = (f32[128,2048]{1,0:T(8,128)S(1)}, bf16[128,2048]{1,0:T(8,128)(2,1)S(1)}, f32[1,2048]{1,0:T(1,128)S(1)}) custom-call(s32[256,1]{1,0:T(8,128)S(1)} %fusion.13.index_ref, bf16[256,2048]{1,0:T(8,128)(2,1)S(1)} %constant_dynamic-update-slice_fusion.rows_ref, bf16[2048,2048]{1,0:T(8,128)(2,1)S(1)} %get-tuple-element.37.chol_ref, ...), custom_call_target="tpu_custom_call" | custom-call | flops 2415919104 | bytes 11010048 | tf_op jit(solution)/shard_map/pallas_call | solution.py:137
  33.1 0.2 collective-permute-start.11
  33.4 0.4 collective-permute-start.12
  33.7 1.4 %collective-permute-done.12 = f32[16,128]{1,0:T(8,128)S(1)} collective-permute-done((f32[16,128]{1,0:T(8,128)S(1)}, f32[16,128]{1,0:T(8,128)S(1)}, u32[]{:S(2)}, u32[]{:S(2)}) %collective-permute-start.12) | collective-permute-done | bytes 8224 | tf_op jit(solution)/shard_map/ppermute | solution.py:24
  35.1 0.0 collective-permute-done.11
  35.1 0.1 convert_add_fusion
  35.3 0.1 convert.24
  35.3 0.1 slice_bitcast_fusion.4
  35.4 0.1 fusion.4
  35.5 1.3 %collective-permute-start.13 = (f16[48,2176]{1,0:T(8,128)(2,1)S(1)}, f16[48,2176]{1,0:T(8,128)(2,1)S(1)}, u32[]{:S(2)}, u32[]{:S(2)}) collective-permute-start(f16[48,2176]{1,0:T(8,128)(2,1)S(1)} %fusion.4), channel_id=1, source_target_pairs={{0,2},{1,5},{2,0},{3,7},{4,6},{5,1},{6,4},{7,3},{8,10},{9,13},{10,... | collective-permute-start | bytes 626696 | tf_op jit(solution)/shard_map/ppermute | solution.py:184
  36.8 0.4 collective-permute-start.15
  37.2 2.0 %collective-permute-start.16 = (f16[16,2176]{1,0:T(8,128)(2,1)S(1)}, f16[16,2176]{1,0:T(8,128)(2,1)S(1)}, u32[]{:S(2)}, u32[]{:S(2)}) collective-permute-start(f16[16,2176]{1,0:T(8,128)(2,1)S(1)} %get-tuple-element.42), channel_id=1, source_target_pairs={{0,6},{1,7},{2,4},{3,5},{4,2},{5,3},{6,0},{7,1},{8,14},{9,15},{10,... | collective-permute-start | bytes 208904 | tf_op jit(solution)/shard_map/ppermute | solution.py:184
  39.1 2.2 %collective-permute-done.13 = f16[48,2176]{1,0:T(8,128)(2,1)S(1)} collective-permute-done((f16[48,2176]{1,0:T(8,128)(2,1)S(1)}, f16[48,2176]{1,0:T(8,128)(2,1)S(1)}, u32[]{:S(2)}, u32[]{:S(2)}) %collective-permute-start.13) | collective-permute-done | bytes 208928 | tf_op jit(solution)/shard_map/ppermute | solution.py:184
  41.4 0.6 %collective-permute-done.15 = f16[16,2176]{1,0:T(8,128)(2,1)S(1)} collective-permute-done((f16[16,2176]{1,0:T(8,128)(2,1)S(1)}, f16[16,2176]{1,0:T(8,128)(2,1)S(1)}, u32[]{:S(2)}, u32[]{:S(2)}) %collective-permute-start.15) | collective-permute-done | bytes 69664 | tf_op jit(solution)/shard_map/ppermute | solution.py:184
  42.0 1.4 %collective-permute-done.16 = f16[16,2176]{1,0:T(8,128)(2,1)S(1)} collective-permute-done((f16[16,2176]{1,0:T(8,128)(2,1)S(1)}, f16[16,2176]{1,0:T(8,128)(2,1)S(1)}, u32[]{:S(2)}, u32[]{:S(2)}) %collective-permute-start.16) | collective-permute-done | bytes 69664 | tf_op jit(solution)/shard_map/ppermute | solution.py:184
  43.5 1.7 %collective-permute-start.17 = (f16[16,2176]{1,0:T(8,128)(2,1)S(1)}, f16[16,2176]{1,0:T(8,128)(2,1)S(1)}, u32[]{:S(2)}, u32[]{:S(2)}) collective-permute-start(f16[16,2176]{1,0:T(8,128)(2,1)S(1)} %get-tuple-element.43), channel_id=1, source_target_pairs={{0,8},{1,9},{2,10},{3,11},{4,12},{5,13},{6,14},{7,15},{8,0},{9,1},... | collective-permute-start | bytes 208904 | tf_op jit(solution)/shard_map/ppermute | solution.py:24
  45.2 0.8 %collective-permute-start.14 = (f16[16,2048]{1,0:T(8,128)(2,1)S(1)}, f16[16,2048]{1,0:T(8,128)(2,1)S(1)}, u32[]{:S(2)}, u32[]{:S(2)}) collective-permute-start(f16[16,2048]{1,0:T(8,128)(2,1)S(1)} %fusion.17), channel_id=1, source_target_pairs={{0,4},{1,3},{2,6},{3,1},{4,0},{5,7},{6,2},{7,5},{8,12},{9,11},{10,... | collective-permute-start | bytes 196616 | tf_op jit(solution)/shard_map/ppermute | solution.py:184
  46.0 3.6 %collective-permute-done.17 = f16[16,2176]{1,0:T(8,128)(2,1)S(1)} collective-permute-done((f16[16,2176]{1,0:T(8,128)(2,1)S(1)}, f16[16,2176]{1,0:T(8,128)(2,1)S(1)}, u32[]{:S(2)}, u32[]{:S(2)}) %collective-permute-start.17) | collective-permute-done | bytes 69664 | tf_op jit(solution)/shard_map/ppermute | solution.py:24
  49.6 0.4 collective-permute-done.14
  50.1 0.0 copy-done.1
  50.1 0.7 %fusion.16 = f32[16,2048]{1,0:T(8,128)} fusion(f32[16,2048]{1,0:T(8,128)S(1)} %copy-done.1, f32[16,2176]{1,0:T(8,128)S(1)} %convert_element_type.36, f32[48,2176]{1,0:T(8,128)S(1)} %convert_element_type.30, f32[4,2,16,2048]{3,2,1,0:T(8,128)S(1)} %bitcast.31, f16[16,2048]{1,0:T(8,128)(2,1)S(1)} %collective-permute-done.14, f32[2048]{0:T(1024)S(1)} %fusion.23), kind=kLoop, calls=%fused_computation.34 | loop fusion | flops 196608 | bytes 729088 | tf_op jit(solution)/shard_map/sub | solution.py:250
  (26 shorter events, 0.4 us)
Async XLA Ops:
  0.0 1.2 %copy-start = (bf16[16,32768]{1,0:T(8,128)(2,1)S(1)}, bf16[16,32768]{1,0:T(8,128)(2,1)}, u32[]{:S(2)}) copy-start(bf16[16,32768]{1,0:T(8,128)(2,1)} %greens_ref.1) | copy-start | bytes 3145732
  1.3 23.4 %collective-permute-start.4 = (bf16[32,2048]{1,0:T(8,128)(2,1)S(1)}, bf16[32,2048]{1,0:T(8,128)(2,1)S(1)}, u32[]{:S(2)}, u32[]{:S(2)}) collective-permute-start(bf16[32,2048]{1,0:T(8,128)(2,1)S(1)} %get-tuple-element.26), channel_id=1, source_target_pairs={{0,8},{1,9},{2,10},{3,11},{4,12},{5,13},{6,14},{7,15},{8,0},{9,1},... | collective-permute-start | bytes 393224 | tf_op jit(solution)/shard_map/ppermute | solution.py:24
  5.4 23.4 %collective-permute-start.6 = (bf16[32,2048]{1,0:T(8,128)(2,1)S(1)}, bf16[32,2048]{1,0:T(8,128)(2,1)S(1)}, u32[]{:S(2)}, u32[]{:S(2)}) collective-permute-start(bf16[32,2048]{1,0:T(8,128)(2,1)S(1)} %get-tuple-element.29), channel_id=1, source_target_pairs={{0,12},{1,13},{2,14},{3,15},{4,8},{5,9},{6,10},{7,11},{8,4},{9,5},... | collective-permute-start | bytes 393224 | tf_op jit(solution)/shard_map/ppermute | solution.py:24
  6.7 2.2 %collective-permute-start = (bf16[64,2048]{1,0:T(8,128)(2,1)S(1)}, bf16[64,2048]{1,0:T(8,128)(2,1)S(1)}, u32[]{:S(2)}, u32[]{:S(2)}) collective-permute-start(bf16[64,2048]{1,0:T(8,128)(2,1)S(1)} %get-tuple-element.25), channel_id=1, source_target_pairs={{0,1},{1,0},{2,3},{3,2},{4,5},{5,4},{6,7},{7,6},{8,9},{9,8},{10,11... | collective-permute-start | bytes 786440 | tf_op jit(solution)/shard_map/ppermute | solution.py:24
  9.0 6.0 %collective-permute-start.1 = (bf16[32,2048]{1,0:T(8,128)(2,1)S(1)}, bf16[32,2048]{1,0:T(8,128)(2,1)S(1)}, u32[]{:S(2)}, u32[]{:S(2)}) collective-permute-start(bf16[32,2048]{1,0:T(8,128)(2,1)S(1)} %pad_maximum_fusion), channel_id=1, source_target_pairs={{0,2},{1,3},{2,0},{3,1},{4,6},{5,7},{6,4},{7,5},{8,10},{9,11},{10,... | collective-permute-start | bytes 393224 | tf_op jit(solution)/shard_map/ppermute | solution.py:24
  10.6 7.0 %collective-permute-start.2 = (bf16[32,2048]{1,0:T(8,128)(2,1)S(1)}, bf16[32,2048]{1,0:T(8,128)(2,1)S(1)}, u32[]{:S(2)}, u32[]{:S(2)}) collective-permute-start(bf16[32,2048]{1,0:T(8,128)(2,1)S(1)} %pad_maximum_fusion.1), channel_id=1, source_target_pairs={{0,4},{1,5},{2,6},{3,7},{4,0},{5,1},{6,2},{7,3},{8,12},{9,13},{10,... | collective-permute-start | bytes 393224 | tf_op jit(solution)/shard_map/ppermute | solution.py:24
  10.9 11.4 %collective-permute-start.3 = (bf16[32,2048]{1,0:T(8,128)(2,1)S(1)}, bf16[32,2048]{1,0:T(8,128)(2,1)S(1)}, u32[]{:S(2)}, u32[]{:S(2)}) collective-permute-start(bf16[32,2048]{1,0:T(8,128)(2,1)S(1)} %pad_maximum_fusion.2), channel_id=1, source_target_pairs={{0,6},{1,7},{2,4},{3,5},{4,2},{5,3},{6,0},{7,1},{8,14},{9,15},{10,... | collective-permute-start | bytes 393224 | tf_op jit(solution)/shard_map/ppermute | solution.py:24
  15.0 13.8 %collective-permute-start.5 = (bf16[32,2048]{1,0:T(8,128)(2,1)S(1)}, bf16[32,2048]{1,0:T(8,128)(2,1)S(1)}, u32[]{:S(2)}, u32[]{:S(2)}) collective-permute-start(bf16[32,2048]{1,0:T(8,128)(2,1)S(1)} %get-tuple-element.28), channel_id=1, source_target_pairs={{0,10},{1,11},{2,8},{3,9},{4,14},{5,15},{6,12},{7,13},{8,2},{9,3},... | collective-permute-start | bytes 393224 | tf_op jit(solution)/shard_map/ppermute | solution.py:24
  17.6 12.7 %collective-permute-start.9 = (bf16[16,2048]{1,0:T(8,128)(2,1)S(1)}, bf16[16,2048]{1,0:T(8,128)(2,1)S(1)}, u32[]{:S(2)}, u32[]{:S(2)}) collective-permute-start(bf16[16,2048]{1,0:T(8,128)(2,1)S(1)} %get-tuple-element.31), channel_id=1, source_target_pairs={{0,14},{1,15},{2,12},{3,13},{4,10},{5,11},{6,8},{7,9},{8,6},{9,7},... | collective-permute-start | bytes 196616 | tf_op jit(solution)/shard_map/ppermute | solution.py:24
  22.3 8.0 %collective-permute-start.10 = (bf16[16,2048]{1,0:T(8,128)(2,1)S(1)}, bf16[16,2048]{1,0:T(8,128)(2,1)S(1)}, u32[]{:S(2)}, u32[]{:S(2)}) collective-permute-start(bf16[16,2048]{1,0:T(8,128)(2,1)S(1)} %get-tuple-element.33), channel_id=1, source_target_pairs={{0,15},{1,14},{2,13},{3,12},{4,11},{5,10},{6,9},{7,8},{8,7},{9,6},... | collective-permute-start | bytes 196616 | tf_op jit(solution)/shard_map/ppermute | solution.py:24
  24.7 4.2 %collective-permute-start.7 = (bf16[16,2048]{1,0:T(8,128)(2,1)S(1)}, bf16[16,2048]{1,0:T(8,128)(2,1)S(1)}, u32[]{:S(2)}, u32[]{:S(2)}) collective-permute-start(bf16[16,2048]{1,0:T(8,128)(2,1)S(1)} %get-tuple-element.64), channel_id=1, source_target_pairs={{0,1},{1,0},{2,3},{3,2},{4,5},{5,4},{6,7},{7,6},{8,9},{9,8},{10,11... | collective-permute-start | bytes 196616 | tf_op jit(solution)/shard_map/ppermute | solution.py:24
  28.9 1.4 %collective-permute-start.8 = (bf16[32,2048]{1,0:T(8,128)(2,1)S(1)}, bf16[32,2048]{1,0:T(8,128)(2,1)S(1)}, u32[]{:S(2)}, u32[]{:S(2)}) collective-permute-start(bf16[32,2048]{1,0:T(8,128)(2,1)S(1)} %pad_maximum_fusion.3), channel_id=1, source_target_pairs={{0,1},{1,0},{2,3},{3,2},{4,5},{5,4},{6,7},{7,6},{8,9},{9,8},{10,11... | collective-permute-start | bytes 393224 | tf_op jit(solution)/shard_map/ppermute | solution.py:24
  30.3 19.7 %copy-start.1 = (f32[16,2048]{1,0:T(8,128)S(1)}, f32[16,2048]{1,0:T(8,128)}, u32[]{:S(2)}) copy-start(f32[16,2048]{1,0:T(8,128)} %param.9) | copy-start | bytes 393220
  33.1 2.0 %collective-permute-start.11 = (bf16[128,2048]{1,0:T(8,128)(2,1)S(1)}, bf16[128,2048]{1,0:T(8,128)(2,1)S(1)}, u32[]{:S(2)}, u32[]{:S(2)}) collective-permute-start(bf16[128,2048]{1,0:T(8,128)(2,1)S(1)} %get-tuple-element.39), channel_id=1, source_target_pairs={{0,1},{1,0},{2,3},{3,2},{4,5},{5,4},{6,7},{7,6},{8,9},{9,8},{10,11... | collective-permute-start | bytes 1572872 | tf_op jit(solution)/shard_map/ppermute | solution.py:24
  33.4 1.8 %collective-permute-start.12 = (f32[16,128]{1,0:T(8,128)S(1)}, f32[16,128]{1,0:T(8,128)S(1)}, u32[]{:S(2)}, u32[]{:S(2)}) collective-permute-start(f32[16,128]{1,0:T(8,128)S(1)} %bitcast.26), channel_id=1, source_target_pairs={{0,1},{1,0},{2,3},{3,2},{4,5},{5,4},{6,7},{7,6},{8,9},{9,8},{10,11... | collective-permute-start | bytes 24584 | tf_op jit(solution)/shard_map/ppermute | solution.py:24
  35.5 5.9 %collective-permute-start.13 = (f16[48,2176]{1,0:T(8,128)(2,1)S(1)}, f16[48,2176]{1,0:T(8,128)(2,1)S(1)}, u32[]{:S(2)}, u32[]{:S(2)}) collective-permute-start(f16[48,2176]{1,0:T(8,128)(2,1)S(1)} %fusion.4), channel_id=1, source_target_pairs={{0,2},{1,5},{2,0},{3,7},{4,6},{5,1},{6,4},{7,3},{8,10},{9,13},{10,... | collective-permute-start | bytes 626696 | tf_op jit(solution)/shard_map/ppermute | solution.py:184
  36.8 5.2 %collective-permute-start.15 = (f16[16,2176]{1,0:T(8,128)(2,1)S(1)}, f16[16,2176]{1,0:T(8,128)(2,1)S(1)}, u32[]{:S(2)}, u32[]{:S(2)}) collective-permute-start(f16[16,2176]{1,0:T(8,128)(2,1)S(1)} %get-tuple-element.41), channel_id=1, source_target_pairs={{0,4},{1,3},{2,6},{3,1},{4,0},{5,7},{6,2},{7,5},{8,12},{9,11},{10,... | collective-permute-start | bytes 208904 | tf_op jit(solution)/shard_map/ppermute | solution.py:184
  37.2 6.3 %collective-permute-start.16 = (f16[16,2176]{1,0:T(8,128)(2,1)S(1)}, f16[16,2176]{1,0:T(8,128)(2,1)S(1)}, u32[]{:S(2)}, u32[]{:S(2)}) collective-permute-start(f16[16,2176]{1,0:T(8,128)(2,1)S(1)} %get-tuple-element.42), channel_id=1, source_target_pairs={{0,6},{1,7},{2,4},{3,5},{4,2},{5,3},{6,0},{7,1},{8,14},{9,15},{10,... | collective-permute-start | bytes 208904 | tf_op jit(solution)/shard_map/ppermute | solution.py:184
  43.5 6.1 %collective-permute-start.17 = (f16[16,2176]{1,0:T(8,128)(2,1)S(1)}, f16[16,2176]{1,0:T(8,128)(2,1)S(1)}, u32[]{:S(2)}, u32[]{:S(2)}) collective-permute-start(f16[16,2176]{1,0:T(8,128)(2,1)S(1)} %get-tuple-element.43), channel_id=1, source_target_pairs={{0,8},{1,9},{2,10},{3,11},{4,12},{5,13},{6,14},{7,15},{8,0},{9,1},... | collective-permute-start | bytes 208904 | tf_op jit(solution)/shard_map/ppermute | solution.py:24
  45.2 4.9 %collective-permute-start.14 = (f16[16,2048]{1,0:T(8,128)(2,1)S(1)}, f16[16,2048]{1,0:T(8,128)(2,1)S(1)}, u32[]{:S(2)}, u32[]{:S(2)}) collective-permute-start(f16[16,2048]{1,0:T(8,128)(2,1)S(1)} %fusion.17), channel_id=1, source_target_pairs={{0,4},{1,3},{2,6},{3,1},{4,0},{5,7},{6,2},{7,5},{8,12},{9,11},{10,... | collective-permute-start | bytes 196616 | tf_op jit(solution)/shard_map/ppermute | solution.py:184

commit v10 on v9

--- a/solution.py
+++ b/solution.py
@@ -74,15 +74,17 @@
         got[m] = swap(message, 2 * m, n)
     last = [after(x, got[w]) for x, w in zip(last, (2, 3))]
     last = [swap(x, n - 2 + j, n) for j, x in enumerate(last)]
-    far = [got[m] for m in range(half, 2 * half - 1)]
-    passed = [swap(jnp.concatenate([x[own:] for x in part]), 1, n) for part in (far[:1], far[1:])]
+    far = [got[m] for first in (0, 1) for m in range(half + first, 2 * half - 1, 2)]
+    early = half // 2
+    passed = [swap(jnp.concatenate([x[own:] for x in part]), 1, n) for part in (far[:early], far[early:])]
     rows = [got[m] for m in range(half)] + [x[:own] for x in far] + passed + last
     return jnp.concatenate(rows), got[1]
 
 
 def place_of_source(source, n):
     half = n // 4
-    far = n // 2 + (source % 2) * (half - 1) + source // 2 - half
+    chip = source // 2 - half
+    far = n // 2 + (source % 2) * (half - 1) + chip % 2 * (half // 2) + chip // 2
     return jnp.where((source < n // 2) | (source >= n - 2), source, far)
 
 

time: 51 us -> 51 us (level)
  transfers between devices with their start and end apart: 18 -> 18, of which waited for: 9 -> 9; matrix products, arithmetic and copies ran while one was open for 5% -> 6% of each run, Pallas kernels for 7% -> 7%
where the time goes in v10:
time: 51 us; the launch traced here: 50.8 us
  starting transfers between devices  25.8 us (51%)
  waiting for transfers between devices  13.2 us (26%)
  Pallas kernels  6.36 us (12%)
  local copies, waits for them, and re-layouts  3.54 us (7%)
  other arithmetic  1.59 us (3%)
    ppermute x14, starting transfers between devices, swap(): return lax.ppermute(x, 'chol', [(i, i ^ mask) for i in range(n)])  21.4 us
    ppermute x14, waiting for transfers between devices, swap(): return lax.ppermute(x, 'chol', [(i, i ^ mask) for i in range(n)])  8.45 us
    ppermute x4, waiting for transfers between devices, swap_of_four(): return lax.ppermute(x, 'chol', [(i, partner(i)) for i in range(n)])  4.79 us
    ppermute x4, starting transfers between devices, swap_of_four(): return lax.ppermute(x, 'chol', [(i, partner(i)) for i in range(n)])  4.38 us
    pallas_call x1, Pallas kernels, stage_chol(): pl.pallas_call(functools.partial(stage_kernel, parts), in_specs=[pl.Block...  3.5 us
    pallas_call x1, Pallas kernels, partial_bias(): pl.pallas_call(functools.partial(bias_kernel, tile), in_specs=[pl.BlockSp...  2.79 us
    unnamed x10, local copies, waits for them, and re-layouts  1.28 us
  transfers between devices with their start and end apart: 18, of which 9 were waited for; matrix products, arithmetic and copies ran while one was open for 6% of the time, Pallas kernels for 7%

profile of v10, /device:TPU:0, one launch (start us, length us, event | category | flops | bytes accessed | tf_op | source)
XLA Modules:
  0.0 50.8 jit_solution(17865287588391224632)
XLA Ops:
  0.0 0.0 copy-start
  0.0 1.2 %copy-done = bf16[16,32768]{1,0:T(8,128)(2,1)S(1)} copy-done((bf16[16,32768]{1,0:T(8,128)(2,1)S(1)}, bf16[16,32768]{1,0:T(8,128)(2,1)}, u32[]{:S(2)}) %copy-start) | copy-done | bytes 1048600
  1.2 0.1 shard_map.55
  1.3 4.1 %collective-permute-start.4 = (bf16[32,2048]{1,0:T(8,128)(2,1)S(1)}, bf16[32,2048]{1,0:T(8,128)(2,1)S(1)}, u32[]{:S(2)}, u32[]{:S(2)}) collective-permute-start(bf16[32,2048]{1,0:T(8,128)(2,1)S(1)} %get-tuple-element.26), channel_id=1, source_target_pairs={{0,8},{1,9},{2,10},{3,11},{4,12},{5,13},{6,14},{7,15},{8,0},{9,1},... | collective-permute-start | bytes 393224 | tf_op jit(solution)/shard_map/ppermute | solution.py:24
  5.4 1.3 %collective-permute-start.5 = (bf16[32,2048]{1,0:T(8,128)(2,1)S(1)}, bf16[32,2048]{1,0:T(8,128)(2,1)S(1)}, u32[]{:S(2)}, u32[]{:S(2)}) collective-permute-start(bf16[32,2048]{1,0:T(8,128)(2,1)S(1)} %get-tuple-element.27), channel_id=1, source_target_pairs={{0,12},{1,13},{2,14},{3,15},{4,8},{5,9},{6,10},{7,11},{8,4},{9,5},... | collective-permute-start | bytes 393224 | tf_op jit(solution)/shard_map/ppermute | solution.py:24
  6.7 0.0 collective-permute-start
  6.8 0.7 %broadcast_in_dim.2.mean_ref = bf16[1,2048]{1,0:T(2,128)(2,1)S(1)} reshape(bf16[2048]{0:T(1024)(128)(2,1)} %param.6) | data formatting | bytes 8192 | tf_op jit(solution)/shard_map/broadcast_in_dim | solution.py:234
  7.5 0.8 %reshape.545 = s32[16,16]{1,0:T(8,128)S(1)} reshape(s32[256]{0:T(256)} %param.8) | data formatting | bytes 2048 | tf_op jit(solution)/shard_map/reshape | solution.py:232
  8.2 0.6 %gather_fusion = s32[16,16]{1,0:T(8,128)S(1)} fusion(s32[16,16]{1,0:T(8,128)S(1)} %reshape.545, s32[1024]{0:T(1024)S(1)} %pad_clamp_fusion), kind=kCustom, calls=%fused_computation | custom fusion | bytes 2112 | tf_op jit(solution)/shard_map/gather | solution.py:232
  8.8 0.1 reshape.556
  8.9 0.0 collective-permute-done
  9.0 1.6 %collective-permute-start.1 = (bf16[32,2048]{1,0:T(8,128)(2,1)S(1)}, bf16[32,2048]{1,0:T(8,128)(2,1)S(1)}, u32[]{:S(2)}, u32[]{:S(2)}) collective-permute-start(bf16[32,2048]{1,0:T(8,128)(2,1)S(1)} %pad_maximum_fusion), channel_id=1, source_target_pairs={{0,2},{1,3},{2,0},{3,1},{4,6},{5,7},{6,4},{7,5},{8,10},{9,11},{10,... | collective-permute-start | bytes 393224 | tf_op jit(solution)/shard_map/ppermute | solution.py:24
  10.6 0.3 collective-permute-start.2
  10.9 1.8 %collective-permute-start.3 = (bf16[32,2048]{1,0:T(8,128)(2,1)S(1)}, bf16[32,2048]{1,0:T(8,128)(2,1)S(1)}, u32[]{:S(2)}, u32[]{:S(2)}) collective-permute-start(bf16[32,2048]{1,0:T(8,128)(2,1)S(1)} %pad_maximum_fusion.2), channel_id=1, source_target_pairs={{0,6},{1,7},{2,4},{3,5},{4,2},{5,3},{6,0},{7,1},{8,14},{9,15},{10,... | collective-permute-start | bytes 393224 | tf_op jit(solution)/shard_map/ppermute | solution.py:24
  12.7 0.4 fusion.13.index_ref
  13.1 1.9 %collective-permute-done.1 = bf16[32,2048]{1,0:T(8,128)(2,1)S(1)} collective-permute-done((bf16[32,2048]{1,0:T(8,128)(2,1)S(1)}, bf16[32,2048]{1,0:T(8,128)(2,1)S(1)}, u32[]{:S(2)}, u32[]{:S(2)}) %collective-permute-start.1) | collective-permute-done | bytes 131104 | tf_op jit(solution)/shard_map/ppermute | solution.py:24
  15.0 2.6 %collective-permute-start.6 = (bf16[32,2048]{1,0:T(8,128)(2,1)S(1)}, bf16[32,2048]{1,0:T(8,128)(2,1)S(1)}, u32[]{:S(2)}, u32[]{:S(2)}) collective-permute-start(bf16[32,2048]{1,0:T(8,128)(2,1)S(1)} %get-tuple-element.29), channel_id=1, source_target_pairs={{0,10},{1,11},{2,8},{3,9},{4,14},{5,15},{6,12},{7,13},{8,2},{9,3},... | collective-permute-start | bytes 393224 | tf_op jit(solution)/shard_map/ppermute | solution.py:24
  17.6 0.0 collective-permute-done.2
  17.6 4.3 %collective-permute-start.9 = (bf16[16,2048]{1,0:T(8,128)(2,1)S(1)}, bf16[16,2048]{1,0:T(8,128)(2,1)S(1)}, u32[]{:S(2)}, u32[]{:S(2)}) collective-permute-start(bf16[16,2048]{1,0:T(8,128)(2,1)S(1)} %get-tuple-element.31), channel_id=1, source_target_pairs={{0,14},{1,15},{2,12},{3,13},{4,10},{5,11},{6,8},{7,9},{8,6},{9,7},... | collective-permute-start | bytes 196616 | tf_op jit(solution)/shard_map/ppermute | solution.py:24
  21.9 0.4 collective-permute-done.3
  22.3 2.3 %collective-permute-start.10 = (bf16[16,2048]{1,0:T(8,128)(2,1)S(1)}, bf16[16,2048]{1,0:T(8,128)(2,1)S(1)}, u32[]{:S(2)}, u32[]{:S(2)}) collective-permute-start(bf16[16,2048]{1,0:T(8,128)(2,1)S(1)} %get-tuple-element.33), channel_id=1, source_target_pairs={{0,15},{1,14},{2,13},{3,12},{4,11},{5,10},{6,9},{7,8},{8,7},{9,6},... | collective-permute-start | bytes 196616 | tf_op jit(solution)/shard_map/ppermute | solution.py:24
  24.7 0.0 collective-permute-done.4
  24.7 0.0 collective-permute-done.5
  24.8 0.5 %collective-permute-start.7 = (bf16[32,2048]{1,0:T(8,128)(2,1)S(1)}, bf16[32,2048]{1,0:T(8,128)(2,1)S(1)}, u32[]{:S(2)}, u32[]{:S(2)}) collective-permute-start(bf16[32,2048]{1,0:T(8,128)(2,1)S(1)} %pad_maximum_fusion.3), channel_id=1, source_target_pairs={{0,1},{1,0},{2,3},{3,2},{4,5},{5,4},{6,7},{7,6},{8,9},{9,8},{10,11... | collective-permute-start | bytes 393224 | tf_op jit(solution)/shard_map/ppermute | solution.py:24
  25.3 3.5 %shard_map.56 = (bf16[2048,2048]{1,0:T(8,128)(2,1)S(1)}, bf16[16,2048]{1,0:T(8,128)(2,1)S(1)}) custom-call(bf16[2048,2048]{1,0:T(8,128)(2,1)} %chol_ref.1, bf16[1,2048]{1,0:T(2,128)(2,1)S(1)} %broadcast_in_dim.2.mean_ref), custom_call_target="tpu_custom_call" | custom-call | bytes 8388608 | tf_op jit(solution)/shard_map/pallas_call | solution.py:104
  28.8 0.0 collective-permute-done.6
  28.9 0.1 collective-permute-start.8
  29.0 0.0 collective-permute-done.7
  29.0 1.2 %collective-permute-done.8 = bf16[16,2048]{1,0:T(8,128)(2,1)S(1)} collective-permute-done((bf16[16,2048]{1,0:T(8,128)(2,1)S(1)}, bf16[16,2048]{1,0:T(8,128)(2,1)S(1)}, u32[]{:S(2)}, u32[]{:S(2)}) %collective-permute-start.8) | collective-permute-done | bytes 65568 | tf_op jit(solution)/shard_map/ppermute | solution.py:24
  30.2 0.0 collective-permute-done.9
  30.2 0.0 collective-permute-done.10
  30.2 0.0 copy-start.1
  30.2 2.8 %shard_map.57 = (f32[128,2048]{1,0:T(8,128)S(1)}, bf16[128,2048]{1,0:T(8,128)(2,1)S(1)}, f32[1,2048]{1,0:T(1,128)S(1)}) custom-call(s32[256,1]{1,0:T(8,128)S(1)} %fusion.13.index_ref, bf16[256,2048]{1,0:T(8,128)(2,1)S(1)} %constant_dynamic-update-slice_fusion.rows_ref, bf16[2048,2048]{1,0:T(8,128)(2,1)S(1)} %get-tuple-element.37.chol_ref, ...), custom_call_target="tpu_custom_call" | custom-call | flops 2415919104 | bytes 11010048 | tf_op jit(solution)/shard_map/pallas_call | solution.py:139
  33.0 0.2 collective-permute-start.11
  33.3 0.4 collective-permute-start.12
  33.6 1.4 %collective-permute-done.12 = f32[16,128]{1,0:T(8,128)S(1)} collective-permute-done((f32[16,128]{1,0:T(8,128)S(1)}, f32[16,128]{1,0:T(8,128)S(1)}, u32[]{:S(2)}, u32[]{:S(2)}) %collective-permute-start.12) | collective-permute-done | bytes 8224 | tf_op jit(solution)/shard_map/ppermute | solution.py:24
  35.0 0.0 collective-permute-done.11
  35.0 0.1 convert_add_fusion
  35.2 0.1 convert.24
  35.2 0.1 slice_bitcast_fusion.4
  35.3 0.1 fusion.4
  35.4 1.3 %collective-permute-start.13 = (f16[48,2176]{1,0:T(8,128)(2,1)S(1)}, f16[48,2176]{1,0:T(8,128)(2,1)S(1)}, u32[]{:S(2)}, u32[]{:S(2)}) collective-permute-start(f16[48,2176]{1,0:T(8,128)(2,1)S(1)} %fusion.4), channel_id=1, source_target_pairs={{0,2},{1,5},{2,0},{3,7},{4,6},{5,1},{6,4},{7,3},{8,10},{9,13},{10,... | collective-permute-start | bytes 626696 | tf_op jit(solution)/shard_map/ppermute | solution.py:186
  36.7 0.5 collective-permute-start.15
  37.2 1.9 %collective-permute-start.16 = (f16[16,2176]{1,0:T(8,128)(2,1)S(1)}, f16[16,2176]{1,0:T(8,128)(2,1)S(1)}, u32[]{:S(2)}, u32[]{:S(2)}) collective-permute-start(f16[16,2176]{1,0:T(8,128)(2,1)S(1)} %get-tuple-element.42), channel_id=1, source_target_pairs={{0,6},{1,7},{2,4},{3,5},{4,2},{5,3},{6,0},{7,1},{8,14},{9,15},{10,... | collective-permute-start | bytes 208904 | tf_op jit(solution)/shard_map/ppermute | solution.py:186
  39.0 2.3 %collective-permute-done.13 = f16[48,2176]{1,0:T(8,128)(2,1)S(1)} collective-permute-done((f16[48,2176]{1,0:T(8,128)(2,1)S(1)}, f16[48,2176]{1,0:T(8,128)(2,1)S(1)}, u32[]{:S(2)}, u32[]{:S(2)}) %collective-permute-start.13) | collective-permute-done | bytes 208928 | tf_op jit(solution)/shard_map/ppermute | solution.py:186
  41.4 0.5 %collective-permute-done.15 = f16[16,2176]{1,0:T(8,128)(2,1)S(1)} collective-permute-done((f16[16,2176]{1,0:T(8,128)(2,1)S(1)}, f16[16,2176]{1,0:T(8,128)(2,1)S(1)}, u32[]{:S(2)}, u32[]{:S(2)}) %collective-permute-start.15) | collective-permute-done | bytes 69664 | tf_op jit(solution)/shard_map/ppermute | solution.py:186
  41.9 1.4 %collective-permute-done.16 = f16[16,2176]{1,0:T(8,128)(2,1)S(1)} collective-permute-done((f16[16,2176]{1,0:T(8,128)(2,1)S(1)}, f16[16,2176]{1,0:T(8,128)(2,1)S(1)}, u32[]{:S(2)}, u32[]{:S(2)}) %collective-permute-start.16) | collective-permute-done | bytes 69664 | tf_op jit(solution)/shard_map/ppermute | solution.py:186
  43.4 1.8 %collective-permute-start.17 = (f16[16,2176]{1,0:T(8,128)(2,1)S(1)}, f16[16,2176]{1,0:T(8,128)(2,1)S(1)}, u32[]{:S(2)}, u32[]{:S(2)}) collective-permute-start(f16[16,2176]{1,0:T(8,128)(2,1)S(1)} %get-tuple-element.43), channel_id=1, source_target_pairs={{0,8},{1,9},{2,10},{3,11},{4,12},{5,13},{6,14},{7,15},{8,0},{9,1},... | collective-permute-start | bytes 208904 | tf_op jit(solution)/shard_map/ppermute | solution.py:24
  45.2 0.8 %collective-permute-start.14 = (f16[16,2048]{1,0:T(8,128)(2,1)S(1)}, f16[16,2048]{1,0:T(8,128)(2,1)S(1)}, u32[]{:S(2)}, u32[]{:S(2)}) collective-permute-start(f16[16,2048]{1,0:T(8,128)(2,1)S(1)} %fusion.19), channel_id=1, source_target_pairs={{0,4},{1,3},{2,6},{3,1},{4,0},{5,7},{6,2},{7,5},{8,12},{9,11},{10,... | collective-permute-start | bytes 196616 | tf_op jit(solution)/shard_map/ppermute | solution.py:186
  46.0 3.6 %collective-permute-done.17 = f16[16,2176]{1,0:T(8,128)(2,1)S(1)} collective-permute-done((f16[16,2176]{1,0:T(8,128)(2,1)S(1)}, f16[16,2176]{1,0:T(8,128)(2,1)S(1)}, u32[]{:S(2)}, u32[]{:S(2)}) %collective-permute-start.17) | collective-permute-done | bytes 69664 | tf_op jit(solution)/shard_map/ppermute | solution.py:24
  49.5 0.5 %collective-permute-done.14 = f16[16,2048]{1,0:T(8,128)(2,1)S(1)} collective-permute-done((f16[16,2048]{1,0:T(8,128)(2,1)S(1)}, f16[16,2048]{1,0:T(8,128)(2,1)S(1)}, u32[]{:S(2)}, u32[]{:S(2)}) %collective-permute-start.14) | collective-permute-done | bytes 65568 | tf_op jit(solution)/shard_map/ppermute | solution.py:186
  50.1 0.0 copy-done.1
  50.1 0.7 %fusion.18 = f32[16,2048]{1,0:T(8,128)} fusion(f32[16,2048]{1,0:T(8,128)S(1)} %copy-done.1, f32[16,2176]{1,0:T(8,128)S(1)} %convert_element_type.36, f32[48,2176]{1,0:T(8,128)S(1)} %convert_element_type.30, f32[4,2,16,2048]{3,2,1,0:T(8,128)S(1)} %bitcast.31, f16[16,2048]{1,0:T(8,128)(2,1)S(1)} %collective-permute-done.14, f32[2048]{0:T(1024)S(1)} %fusion.28), kind=kLoop, calls=%fused_computation.41 | loop fusion | flops 196608 | bytes 729088 | tf_op jit(solution)/shard_map/sub | solution.py:252
  (26 shorter events, 0.4 us)
Async XLA Ops:
  0.0 1.2 %copy-start = (bf16[16,32768]{1,0:T(8,128)(2,1)S(1)}, bf16[16,32768]{1,0:T(8,128)(2,1)}, u32[]{:S(2)}) copy-start(bf16[16,32768]{1,0:T(8,128)(2,1)} %greens_ref.1) | copy-start | bytes 3145732
  1.3 23.4 %collective-permute-start.4 = (bf16[32,2048]{1,0:T(8,128)(2,1)S(1)}, bf16[32,2048]{1,0:T(8,128)(2,1)S(1)}, u32[]{:S(2)}, u32[]{:S(2)}) collective-permute-start(bf16[32,2048]{1,0:T(8,128)(2,1)S(1)} %get-tuple-element.26), channel_id=1, source_target_pairs={{0,8},{1,9},{2,10},{3,11},{4,12},{5,13},{6,14},{7,15},{8,0},{9,1},... | collective-permute-start | bytes 393224 | tf_op jit(solution)/shard_map/ppermute | solution.py:24
  5.4 19.3 %collective-permute-start.5 = (bf16[32,2048]{1,0:T(8,128)(2,1)S(1)}, bf16[32,2048]{1,0:T(8,128)(2,1)S(1)}, u32[]{:S(2)}, u32[]{:S(2)}) collective-permute-start(bf16[32,2048]{1,0:T(8,128)(2,1)S(1)} %get-tuple-element.27), channel_id=1, source_target_pairs={{0,12},{1,13},{2,14},{3,15},{4,8},{5,9},{6,10},{7,11},{8,4},{9,5},... | collective-permute-start | bytes 393224 | tf_op jit(solution)/shard_map/ppermute | solution.py:24
  6.7 2.2 %collective-permute-start = (bf16[64,2048]{1,0:T(8,128)(2,1)S(1)}, bf16[64,2048]{1,0:T(8,128)(2,1)S(1)}, u32[]{:S(2)}, u32[]{:S(2)}) collective-permute-start(bf16[64,2048]{1,0:T(8,128)(2,1)S(1)} %get-tuple-element.25), channel_id=1, source_target_pairs={{0,1},{1,0},{2,3},{3,2},{4,5},{5,4},{6,7},{7,6},{8,9},{9,8},{10,11... | collective-permute-start | bytes 786440 | tf_op jit(solution)/shard_map/ppermute | solution.py:24
  9.0 6.0 %collective-permute-start.1 = (bf16[32,2048]{1,0:T(8,128)(2,1)S(1)}, bf16[32,2048]{1,0:T(8,128)(2,1)S(1)}, u32[]{:S(2)}, u32[]{:S(2)}) collective-permute-start(bf16[32,2048]{1,0:T(8,128)(2,1)S(1)} %pad_maximum_fusion), channel_id=1, source_target_pairs={{0,2},{1,3},{2,0},{3,1},{4,6},{5,7},{6,4},{7,5},{8,10},{9,11},{10,... | collective-permute-start | bytes 393224 | tf_op jit(solution)/shard_map/ppermute | solution.py:24
  10.6 7.0 %collective-permute-start.2 = (bf16[32,2048]{1,0:T(8,128)(2,1)S(1)}, bf16[32,2048]{1,0:T(8,128)(2,1)S(1)}, u32[]{:S(2)}, u32[]{:S(2)}) collective-permute-start(bf16[32,2048]{1,0:T(8,128)(2,1)S(1)} %pad_maximum_fusion.1), channel_id=1, source_target_pairs={{0,4},{1,5},{2,6},{3,7},{4,0},{5,1},{6,2},{7,3},{8,12},{9,13},{10,... | collective-permute-start | bytes 393224 | tf_op jit(solution)/shard_map/ppermute | solution.py:24
  10.9 11.4 %collective-permute-start.3 = (bf16[32,2048]{1,0:T(8,128)(2,1)S(1)}, bf16[32,2048]{1,0:T(8,128)(2,1)S(1)}, u32[]{:S(2)}, u32[]{:S(2)}) collective-permute-start(bf16[32,2048]{1,0:T(8,128)(2,1)S(1)} %pad_maximum_fusion.2), channel_id=1, source_target_pairs={{0,6},{1,7},{2,4},{3,5},{4,2},{5,3},{6,0},{7,1},{8,14},{9,15},{10,... | collective-permute-start | bytes 393224 | tf_op jit(solution)/shard_map/ppermute | solution.py:24
  15.0 13.8 %collective-permute-start.6 = (bf16[32,2048]{1,0:T(8,128)(2,1)S(1)}, bf16[32,2048]{1,0:T(8,128)(2,1)S(1)}, u32[]{:S(2)}, u32[]{:S(2)}) collective-permute-start(bf16[32,2048]{1,0:T(8,128)(2,1)S(1)} %get-tuple-element.29), channel_id=1, source_target_pairs={{0,10},{1,11},{2,8},{3,9},{4,14},{5,15},{6,12},{7,13},{8,2},{9,3},... | collective-permute-start | bytes 393224 | tf_op jit(solution)/shard_map/ppermute | solution.py:24
  17.6 12.6 %collective-permute-start.9 = (bf16[16,2048]{1,0:T(8,128)(2,1)S(1)}, bf16[16,2048]{1,0:T(8,128)(2,1)S(1)}, u32[]{:S(2)}, u32[]{:S(2)}) collective-permute-start(bf16[16,2048]{1,0:T(8,128)(2,1)S(1)} %get-tuple-element.31), channel_id=1, source_target_pairs={{0,14},{1,15},{2,12},{3,13},{4,10},{5,11},{6,8},{7,9},{8,6},{9,7},... | collective-permute-start | bytes 196616 | tf_op jit(solution)/shard_map/ppermute | solution.py:24
  22.3 7.9 %collective-permute-start.10 = (bf16[16,2048]{1,0:T(8,128)(2,1)S(1)}, bf16[16,2048]{1,0:T(8,128)(2,1)S(1)}, u32[]{:S(2)}, u32[]{:S(2)}) collective-permute-start(bf16[16,2048]{1,0:T(8,128)(2,1)S(1)} %get-tuple-element.33), channel_id=1, source_target_pairs={{0,15},{1,14},{2,13},{3,12},{4,11},{5,10},{6,9},{7,8},{8,7},{9,6},... | collective-permute-start | bytes 196616 | tf_op jit(solution)/shard_map/ppermute | solution.py:24
  24.8 4.2 %collective-permute-start.7 = (bf16[32,2048]{1,0:T(8,128)(2,1)S(1)}, bf16[32,2048]{1,0:T(8,128)(2,1)S(1)}, u32[]{:S(2)}, u32[]{:S(2)}) collective-permute-start(bf16[32,2048]{1,0:T(8,128)(2,1)S(1)} %pad_maximum_fusion.3), channel_id=1, source_target_pairs={{0,1},{1,0},{2,3},{3,2},{4,5},{5,4},{6,7},{7,6},{8,9},{9,8},{10,11... | collective-permute-start | bytes 393224 | tf_op jit(solution)/shard_map/ppermute | solution.py:24
  28.9 1.3 %collective-permute-start.8 = (bf16[16,2048]{1,0:T(8,128)(2,1)S(1)}, bf16[16,2048]{1,0:T(8,128)(2,1)S(1)}, u32[]{:S(2)}, u32[]{:S(2)}) collective-permute-start(bf16[16,2048]{1,0:T(8,128)(2,1)S(1)} %get-tuple-element.60), channel_id=1, source_target_pairs={{0,1},{1,0},{2,3},{3,2},{4,5},{5,4},{6,7},{7,6},{8,9},{9,8},{10,11... | collective-permute-start | bytes 196616 | tf_op jit(solution)/shard_map/ppermute | solution.py:24
  30.2 19.8 %copy-start.1 = (f32[16,2048]{1,0:T(8,128)S(1)}, f32[16,2048]{1,0:T(8,128)}, u32[]{:S(2)}) copy-start(f32[16,2048]{1,0:T(8,128)} %param.9) | copy-start | bytes 393220
  33.0 2.0 %collective-permute-start.11 = (bf16[128,2048]{1,0:T(8,128)(2,1)S(1)}, bf16[128,2048]{1,0:T(8,128)(2,1)S(1)}, u32[]{:S(2)}, u32[]{:S(2)}) collective-permute-start(bf16[128,2048]{1,0:T(8,128)(2,1)S(1)} %get-tuple-element.39), channel_id=1, source_target_pairs={{0,1},{1,0},{2,3},{3,2},{4,5},{5,4},{6,7},{7,6},{8,9},{9,8},{10,11... | collective-permute-start | bytes 1572872 | tf_op jit(solution)/shard_map/ppermute | solution.py:24
  33.3 1.8 %collective-permute-start.12 = (f32[16,128]{1,0:T(8,128)S(1)}, f32[16,128]{1,0:T(8,128)S(1)}, u32[]{:S(2)}, u32[]{:S(2)}) collective-permute-start(f32[16,128]{1,0:T(8,128)S(1)} %bitcast.26), channel_id=1, source_target_pairs={{0,1},{1,0},{2,3},{3,2},{4,5},{5,4},{6,7},{7,6},{8,9},{9,8},{10,11... | collective-permute-start | bytes 24584 | tf_op jit(solution)/shard_map/ppermute | solution.py:24
  35.4 6.0 %collective-permute-start.13 = (f16[48,2176]{1,0:T(8,128)(2,1)S(1)}, f16[48,2176]{1,0:T(8,128)(2,1)S(1)}, u32[]{:S(2)}, u32[]{:S(2)}) collective-permute-start(f16[48,2176]{1,0:T(8,128)(2,1)S(1)} %fusion.4), channel_id=1, source_target_pairs={{0,2},{1,5},{2,0},{3,7},{4,6},{5,1},{6,4},{7,3},{8,10},{9,13},{10,... | collective-permute-start | bytes 626696 | tf_op jit(solution)/shard_map/ppermute | solution.py:186
  36.7 5.2 %collective-permute-start.15 = (f16[16,2176]{1,0:T(8,128)(2,1)S(1)}, f16[16,2176]{1,0:T(8,128)(2,1)S(1)}, u32[]{:S(2)}, u32[]{:S(2)}) collective-permute-start(f16[16,2176]{1,0:T(8,128)(2,1)S(1)} %get-tuple-element.41), channel_id=1, source_target_pairs={{0,4},{1,3},{2,6},{3,1},{4,0},{5,7},{6,2},{7,5},{8,12},{9,11},{10,... | collective-permute-start | bytes 208904 | tf_op jit(solution)/shard_map/ppermute | solution.py:186
  37.2 6.2 %collective-permute-start.16 = (f16[16,2176]{1,0:T(8,128)(2,1)S(1)}, f16[16,2176]{1,0:T(8,128)(2,1)S(1)}, u32[]{:S(2)}, u32[]{:S(2)}) collective-permute-start(f16[16,2176]{1,0:T(8,128)(2,1)S(1)} %get-tuple-element.42), channel_id=1, source_target_pairs={{0,6},{1,7},{2,4},{3,5},{4,2},{5,3},{6,0},{7,1},{8,14},{9,15},{10,... | collective-permute-start | bytes 208904 | tf_op jit(solution)/shard_map/ppermute | solution.py:186
  43.4 6.1 %collective-permute-start.17 = (f16[16,2176]{1,0:T(8,128)(2,1)S(1)}, f16[16,2176]{1,0:T(8,128)(2,1)S(1)}, u32[]{:S(2)}, u32[]{:S(2)}) collective-permute-start(f16[16,2176]{1,0:T(8,128)(2,1)S(1)} %get-tuple-element.43), channel_id=1, source_target_pairs={{0,8},{1,9},{2,10},{3,11},{4,12},{5,13},{6,14},{7,15},{8,0},{9,1},... | collective-permute-start | bytes 208904 | tf_op jit(solution)/shard_map/ppermute | solution.py:24
  45.2 4.9 %collective-permute-start.14 = (f16[16,2048]{1,0:T(8,128)(2,1)S(1)}, f16[16,2048]{1,0:T(8,128)(2,1)S(1)}, u32[]{:S(2)}, u32[]{:S(2)}) collective-permute-start(f16[16,2048]{1,0:T(8,128)(2,1)S(1)} %fusion.19), channel_id=1, source_target_pairs={{0,4},{1,3},{2,6},{3,1},{4,0},{5,7},{6,2},{7,5},{8,12},{9,11},{10,... | collective-permute-start | bytes 196616 | tf_op jit(solution)/shard_map/ppermute | solution.py:186

commit v11 on v9

--- a/solution.py
+++ b/solution.py
@@ -213,6 +213,13 @@
     chips = n // 2
     radices = stage_radices(chips)
 
+    mean_row = mean_greens[None, :]
+    if chips <= DIRECT_CHIPS:
+        rows, ended = collect_walkers(greens, n)
+        mean_row = after(mean_row, ended)
+        walker_order = after(walker_order, ended)
+    else:
+        rows = lax.all_to_all(greens, "chol", split_axis=1, concat_axis=0, tiled=True)
     place = jnp.arange(n, dtype=jnp.int32)
     relative, weight, left = place // chips, 2, place % chips
     for stage, radix in enumerate(radices):
@@ -228,15 +235,9 @@
         relative = jnp.where(other, jnp.bitwise_xor(relative, 6), relative)
     owners = jnp.bitwise_xor(relative, me)
     index = walker_order.reshape(n, own)[owners].reshape(-1)
-
-    mean_row = mean_greens[None, :]
     if chips <= DIRECT_CHIPS:
-        rows, ended = collect_walkers(greens, n)
-        mean_row = after(mean_row, ended)
         source = jnp.bitwise_xor(index // own, me)
         index = place_of_source(source, n) * own + index % own
-    else:
-        rows = lax.all_to_all(greens, "chol", split_axis=1, concat_axis=0, tiled=True)
     chol, means = stage_chol(chol_vectors, mean_row)
     keep, send, mean = partial_bias(index[:, None], after(rows, means), chol, means, 512)
     mean = mean.reshape(own, -1)

time: 51 us -> 51 us (level)
    ppermute x14, waiting for transfers between devices: 8.76 us -> 9.31 us  [swap(): return lax.ppermute(x, 'chol', [(i, i ^ mask) for i in range(n)])]
where the time goes in v11:
time: 51 us; the launch traced here: 50.8 us
  starting transfers between devices  25.4 us (50%)
  waiting for transfers between devices  13.7 us (27%)
  Pallas kernels  6.36 us (12%)
  local copies, waits for them, and re-layouts  3.54 us (7%)
  other arithmetic  1.47 us (3%)
    ppermute x14, starting transfers between devices, swap(): return lax.ppermute(x, 'chol', [(i, i ^ mask) for i in range(n)])  21 us
    ppermute x14, waiting for transfers between devices, swap(): return lax.ppermute(x, 'chol', [(i, i ^ mask) for i in range(n)])  9.31 us
    ppermute x4, waiting for transfers between devices, swap_of_four(): return lax.ppermute(x, 'chol', [(i, partner(i)) for i in range(n)])  4.44 us
    ppermute x4, starting transfers between devices, swap_of_four(): return lax.ppermute(x, 'chol', [(i, partner(i)) for i in range(n)])  4.38 us
    pallas_call x1, Pallas kernels, stage_chol(): pl.pallas_call(functools.partial(stage_kernel, parts), in_specs=[pl.Block...  3.5 us
    pallas_call x1, Pallas kernels, partial_bias(): pl.pallas_call(functools.partial(bias_kernel, tile), in_specs=[pl.BlockSp...  2.79 us
    unnamed x10, local copies, waits for them, and re-layouts  1.29 us
  transfers between devices with their start and end apart: 18, of which 9 were waited for; matrix products, arithmetic and copies ran while one was open for 5% of the time, Pallas kernels for 7%

profile of v11, /device:TPU:0, one launch (start us, length us, event | category | flops | bytes accessed | tf_op | source)
XLA Modules:
  0.0 50.8 jit_solution(18198051223758289718)
XLA Ops:
  0.0 0.0 copy-start
  0.0 1.2 %copy-done = bf16[16,32768]{1,0:T(8,128)(2,1)S(1)} copy-done((bf16[16,32768]{1,0:T(8,128)(2,1)S(1)}, bf16[16,32768]{1,0:T(8,128)(2,1)}, u32[]{:S(2)}) %copy-start) | copy-done | bytes 1048600
  1.2 0.1 shard_map.55
  1.3 4.1 %collective-permute-start.4 = (bf16[32,2048]{1,0:T(8,128)(2,1)S(1)}, bf16[32,2048]{1,0:T(8,128)(2,1)S(1)}, u32[]{:S(2)}, u32[]{:S(2)}) collective-permute-start(bf16[32,2048]{1,0:T(8,128)(2,1)S(1)} %get-tuple-element.28), channel_id=1, source_target_pairs={{0,8},{1,9},{2,10},{3,11},{4,12},{5,13},{6,14},{7,15},{8,0},{9,1},... | collective-permute-start | bytes 393224 | tf_op jit(solution)/shard_map/ppermute | solution.py:24
  5.4 1.3 %collective-permute-start.6 = (bf16[32,2048]{1,0:T(8,128)(2,1)S(1)}, bf16[32,2048]{1,0:T(8,128)(2,1)S(1)}, u32[]{:S(2)}, u32[]{:S(2)}) collective-permute-start(bf16[32,2048]{1,0:T(8,128)(2,1)S(1)} %get-tuple-element.31), channel_id=1, source_target_pairs={{0,12},{1,13},{2,14},{3,15},{4,8},{5,9},{6,10},{7,11},{8,4},{9,5},... | collective-permute-start | bytes 393224 | tf_op jit(solution)/shard_map/ppermute | solution.py:24
  6.7 0.0 collective-permute-start
  6.8 1.5 %collective-permute-done = bf16[64,2048]{1,0:T(8,128)(2,1)S(1)} collective-permute-done((bf16[64,2048]{1,0:T(8,128)(2,1)S(1)}, bf16[64,2048]{1,0:T(8,128)(2,1)S(1)}, u32[]{:S(2)}, u32[]{:S(2)}) %collective-permute-start) | collective-permute-done | bytes 262176 | tf_op jit(solution)/shard_map/ppermute | solution.py:24
  8.3 1.6 %collective-permute-start.1 = (bf16[32,2048]{1,0:T(8,128)(2,1)S(1)}, bf16[32,2048]{1,0:T(8,128)(2,1)S(1)}, u32[]{:S(2)}, u32[]{:S(2)}) collective-permute-start(bf16[32,2048]{1,0:T(8,128)(2,1)S(1)} %pad_maximum_fusion), channel_id=1, source_target_pairs={{0,2},{1,3},{2,0},{3,1},{4,6},{5,7},{6,4},{7,5},{8,10},{9,11},{10,... | collective-permute-start | bytes 393224 | tf_op jit(solution)/shard_map/ppermute | solution.py:24
  9.9 0.3 collective-permute-start.2
  10.2 1.8 %collective-permute-start.3 = (bf16[32,2048]{1,0:T(8,128)(2,1)S(1)}, bf16[32,2048]{1,0:T(8,128)(2,1)S(1)}, u32[]{:S(2)}, u32[]{:S(2)}) collective-permute-start(bf16[32,2048]{1,0:T(8,128)(2,1)S(1)} %pad_maximum_fusion.2), channel_id=1, source_target_pairs={{0,6},{1,7},{2,4},{3,5},{4,2},{5,3},{6,0},{7,1},{8,14},{9,15},{10,... | collective-permute-start | bytes 393224 | tf_op jit(solution)/shard_map/ppermute | solution.py:24
  12.1 0.7 %broadcast_in_dim.2.mean_ref = bf16[1,2048]{1,0:T(2,128)(2,1)S(1)} reshape(bf16[2048]{0:T(1024)(128)(2,1)} %param.6) | data formatting | bytes 8192 | tf_op jit(solution)/shard_map/broadcast_in_dim | solution.py:216
  12.8 1.2 %collective-permute-done.1 = bf16[32,2048]{1,0:T(8,128)(2,1)S(1)} collective-permute-done((bf16[32,2048]{1,0:T(8,128)(2,1)S(1)}, bf16[32,2048]{1,0:T(8,128)(2,1)S(1)}, u32[]{:S(2)}, u32[]{:S(2)}) %collective-permute-start.1) | collective-permute-done | bytes 131104 | tf_op jit(solution)/shard_map/ppermute | solution.py:24
  13.9 0.8 %reshape.475 = s32[16,16]{1,0:T(8,128)S(1)} reshape(s32[256]{0:T(256)} %param.8) | data formatting | bytes 2048 | tf_op jit(solution)/shard_map/reshape | solution.py:237
  14.7 0.6 %gather_fusion = s32[16,16]{1,0:T(8,128)S(1)} fusion(s32[16,16]{1,0:T(8,128)S(1)} %reshape.475, s32[1024]{0:T(1024)S(1)} %pad_clamp_fusion), kind=kCustom, calls=%fused_computation | custom fusion | bytes 2112 | tf_op jit(solution)/shard_map/gather | solution.py:237
  15.3 0.1 reshape.486
  15.4 2.7 %collective-permute-start.5 = (bf16[32,2048]{1,0:T(8,128)(2,1)S(1)}, bf16[32,2048]{1,0:T(8,128)(2,1)S(1)}, u32[]{:S(2)}, u32[]{:S(2)}) collective-permute-start(bf16[32,2048]{1,0:T(8,128)(2,1)S(1)} %get-tuple-element.30), channel_id=1, source_target_pairs={{0,10},{1,11},{2,8},{3,9},{4,14},{5,15},{6,12},{7,13},{8,2},{9,3},... | collective-permute-start | bytes 393224 | tf_op jit(solution)/shard_map/ppermute | solution.py:24
  18.1 0.0 collective-permute-done.2
  18.1 3.9 %collective-permute-start.9 = (bf16[16,2048]{1,0:T(8,128)(2,1)S(1)}, bf16[16,2048]{1,0:T(8,128)(2,1)S(1)}, u32[]{:S(2)}, u32[]{:S(2)}) collective-permute-start(bf16[16,2048]{1,0:T(8,128)(2,1)S(1)} %get-tuple-element.33), channel_id=1, source_target_pairs={{0,14},{1,15},{2,12},{3,13},{4,10},{5,11},{6,8},{7,9},{8,6},{9,7},... | collective-permute-start | bytes 196616 | tf_op jit(solution)/shard_map/ppermute | solution.py:24
  22.0 0.0 collective-permute-done.3
  22.0 2.6 %collective-permute-start.10 = (bf16[16,2048]{1,0:T(8,128)(2,1)S(1)}, bf16[16,2048]{1,0:T(8,128)(2,1)S(1)}, u32[]{:S(2)}, u32[]{:S(2)}) collective-permute-start(bf16[16,2048]{1,0:T(8,128)(2,1)S(1)} %get-tuple-element.35), channel_id=1, source_target_pairs={{0,15},{1,14},{2,13},{3,12},{4,11},{5,10},{6,9},{7,8},{8,7},{9,6},... | collective-permute-start | bytes 196616 | tf_op jit(solution)/shard_map/ppermute | solution.py:24
  24.6 0.0 collective-permute-done.4
  24.6 0.6 %collective-permute-start.7 = (bf16[16,2048]{1,0:T(8,128)(2,1)S(1)}, bf16[16,2048]{1,0:T(8,128)(2,1)S(1)}, u32[]{:S(2)}, u32[]{:S(2)}) collective-permute-start(bf16[16,2048]{1,0:T(8,128)(2,1)S(1)} %get-tuple-element.66), channel_id=1, source_target_pairs={{0,1},{1,0},{2,3},{3,2},{4,5},{5,4},{6,7},{7,6},{8,9},{9,8},{10,11... | collective-permute-start | bytes 196616 | tf_op jit(solution)/shard_map/ppermute | solution.py:24
  25.2 3.5 %shard_map.56 = (bf16[2048,2048]{1,0:T(8,128)(2,1)S(1)}, bf16[16,2048]{1,0:T(8,128)(2,1)S(1)}) custom-call(bf16[2048,2048]{1,0:T(8,128)(2,1)} %chol_ref.1, bf16[1,2048]{1,0:T(2,128)(2,1)S(1)} %broadcast_in_dim.2.mean_ref), custom_call_target="tpu_custom_call" | custom-call | bytes 8388608 | tf_op jit(solution)/shard_map/pallas_call | solution.py:102
  28.7 0.3 fusion.13.index_ref
  29.0 0.0 collective-permute-done.5
  29.0 0.0 collective-permute-done.6
  29.1 0.1 collective-permute-start.8
  29.1 0.0 collective-permute-done.7
  29.2 1.3 %collective-permute-done.8 = bf16[32,2048]{1,0:T(8,128)(2,1)S(1)} collective-permute-done((bf16[32,2048]{1,0:T(8,128)(2,1)S(1)}, bf16[32,2048]{1,0:T(8,128)(2,1)S(1)}, u32[]{:S(2)}, u32[]{:S(2)}) %collective-permute-start.8) | collective-permute-done | bytes 131104 | tf_op jit(solution)/shard_map/ppermute | solution.py:24
  30.5 0.0 collective-permute-done.9
  30.5 0.0 collective-permute-done.10
  30.5 0.0 copy-start.1
  30.6 2.8 %shard_map.57 = (f32[128,2048]{1,0:T(8,128)S(1)}, bf16[128,2048]{1,0:T(8,128)(2,1)S(1)}, f32[1,2048]{1,0:T(1,128)S(1)}) custom-call(s32[256,1]{1,0:T(8,128)S(1)} %fusion.13.index_ref, bf16[256,2048]{1,0:T(8,128)(2,1)S(1)} %constant_dynamic-update-slice_fusion.rows_ref, bf16[2048,2048]{1,0:T(8,128)(2,1)S(1)} %get-tuple-element.39.chol_ref, ...), custom_call_target="tpu_custom_call" | custom-call | flops 2415919104 | bytes 11010048 | tf_op jit(solution)/shard_map/pallas_call | solution.py:137
  33.4 0.2 collective-permute-start.11
  33.6 0.4 collective-permute-start.12
  33.9 1.4 %collective-permute-done.12 = f32[16,128]{1,0:T(8,128)S(1)} collective-permute-done((f32[16,128]{1,0:T(8,128)S(1)}, f32[16,128]{1,0:T(8,128)S(1)}, u32[]{:S(2)}, u32[]{:S(2)}) %collective-permute-start.12) | collective-permute-done | bytes 8224 | tf_op jit(solution)/shard_map/ppermute | solution.py:24
  35.4 0.0 collective-permute-done.11
  35.4 0.1 convert_add_fusion
  35.5 0.1 convert.24
  35.6 0.1 slice_bitcast_fusion.4
  35.6 0.1 fusion.4
  35.7 1.3 %collective-permute-start.13 = (f16[48,2176]{1,0:T(8,128)(2,1)S(1)}, f16[48,2176]{1,0:T(8,128)(2,1)S(1)}, u32[]{:S(2)}, u32[]{:S(2)}) collective-permute-start(f16[48,2176]{1,0:T(8,128)(2,1)S(1)} %fusion.4), channel_id=1, source_target_pairs={{0,2},{1,5},{2,0},{3,7},{4,6},{5,1},{6,4},{7,3},{8,10},{9,13},{10,... | collective-permute-start | bytes 626696 | tf_op jit(solution)/shard_map/ppermute | solution.py:184
  37.1 0.3 collective-permute-start.15
  37.4 2.0 %collective-permute-start.16 = (f16[16,2176]{1,0:T(8,128)(2,1)S(1)}, f16[16,2176]{1,0:T(8,128)(2,1)S(1)}, u32[]{:S(2)}, u32[]{:S(2)}) collective-permute-start(f16[16,2176]{1,0:T(8,128)(2,1)S(1)} %get-tuple-element.44), channel_id=1, source_target_pairs={{0,6},{1,7},{2,4},{3,5},{4,2},{5,3},{6,0},{7,1},{8,14},{9,15},{10,... | collective-permute-start | bytes 208904 | tf_op jit(solution)/shard_map/ppermute | solution.py:184
  39.4 2.2 %collective-permute-done.13 = f16[48,2176]{1,0:T(8,128)(2,1)S(1)} collective-permute-done((f16[48,2176]{1,0:T(8,128)(2,1)S(1)}, f16[48,2176]{1,0:T(8,128)(2,1)S(1)}, u32[]{:S(2)}, u32[]{:S(2)}) %collective-permute-start.13) | collective-permute-done | bytes 208928 | tf_op jit(solution)/shard_map/ppermute | solution.py:184
  41.6 0.6 %collective-permute-done.15 = f16[16,2176]{1,0:T(8,128)(2,1)S(1)} collective-permute-done((f16[16,2176]{1,0:T(8,128)(2,1)S(1)}, f16[16,2176]{1,0:T(8,128)(2,1)S(1)}, u32[]{:S(2)}, u32[]{:S(2)}) %collective-permute-start.15) | collective-permute-done | bytes 69664 | tf_op jit(solution)/shard_map/ppermute | solution.py:184
  42.2 1.4 %collective-permute-done.16 = f16[16,2176]{1,0:T(8,128)(2,1)S(1)} collective-permute-done((f16[16,2176]{1,0:T(8,128)(2,1)S(1)}, f16[16,2176]{1,0:T(8,128)(2,1)S(1)}, u32[]{:S(2)}, u32[]{:S(2)}) %collective-permute-start.16) | collective-permute-done | bytes 69664 | tf_op jit(solution)/shard_map/ppermute | solution.py:184
  43.7 0.1 fusion.29
  43.7 1.4 %collective-permute-start.17 = (f16[16,2176]{1,0:T(8,128)(2,1)S(1)}, f16[16,2176]{1,0:T(8,128)(2,1)S(1)}, u32[]{:S(2)}, u32[]{:S(2)}) collective-permute-start(f16[16,2176]{1,0:T(8,128)(2,1)S(1)} %get-tuple-element.45), channel_id=1, source_target_pairs={{0,8},{1,9},{2,10},{3,11},{4,12},{5,13},{6,14},{7,15},{8,0},{9,1},... | collective-permute-start | bytes 208904 | tf_op jit(solution)/shard_map/ppermute | solution.py:24
  45.2 0.8 %collective-permute-start.14 = (f16[16,2048]{1,0:T(8,128)(2,1)S(1)}, f16[16,2048]{1,0:T(8,128)(2,1)S(1)}, u32[]{:S(2)}, u32[]{:S(2)}) collective-permute-start(f16[16,2048]{1,0:T(8,128)(2,1)S(1)} %fusion.17), channel_id=1, source_target_pairs={{0,4},{1,3},{2,6},{3,1},{4,0},{5,7},{6,2},{7,5},{8,12},{9,11},{10,... | collective-permute-start | bytes 196616 | tf_op jit(solution)/shard_map/ppermute | solution.py:184
  46.0 3.9 %collective-permute-done.17 = f16[16,2176]{1,0:T(8,128)(2,1)S(1)} collective-permute-done((f16[16,2176]{1,0:T(8,128)(2,1)S(1)}, f16[16,2176]{1,0:T(8,128)(2,1)S(1)}, u32[]{:S(2)}, u32[]{:S(2)}) %collective-permute-start.17) | collective-permute-done | bytes 69664 | tf_op jit(solution)/shard_map/ppermute | solution.py:24
  49.9 0.2 collective-permute-done.14
  50.0 0.0 copy-done.1
  50.0 0.7 %fusion.16 = f32[16,2048]{1,0:T(8,128)} fusion(f32[16,2048]{1,0:T(8,128)S(1)} %copy-done.1, f32[16,2176]{1,0:T(8,128)S(1)} %convert_element_type.36, f32[48,2176]{1,0:T(8,128)S(1)} %convert_element_type.30, f32[4,2,16,2048]{3,2,1,0:T(8,128)S(1)} %bitcast.31, f16[16,2048]{1,0:T(8,128)(2,1)S(1)} %collective-permute-done.14, f32[2048]{0:T(1024)S(1)} %fusion.23), kind=kLoop, calls=%fused_computation.34 | loop fusion | flops 196608 | bytes 729088 | tf_op jit(solution)/shard_map/sub | solution.py:251
  (25 shorter events, 0.3 us)
Async XLA Ops:
  0.0 1.2 %copy-start = (bf16[16,32768]{1,0:T(8,128)(2,1)S(1)}, bf16[16,32768]{1,0:T(8,128)(2,1)}, u32[]{:S(2)}) copy-start(bf16[16,32768]{1,0:T(8,128)(2,1)} %greens_ref.1) | copy-start | bytes 3145732
  1.3 23.3 %collective-permute-start.4 = (bf16[32,2048]{1,0:T(8,128)(2,1)S(1)}, bf16[32,2048]{1,0:T(8,128)(2,1)S(1)}, u32[]{:S(2)}, u32[]{:S(2)}) collective-permute-start(bf16[32,2048]{1,0:T(8,128)(2,1)S(1)} %get-tuple-element.28), channel_id=1, source_target_pairs={{0,8},{1,9},{2,10},{3,11},{4,12},{5,13},{6,14},{7,15},{8,0},{9,1},... | collective-permute-start | bytes 393224 | tf_op jit(solution)/shard_map/ppermute | solution.py:24
  5.4 23.6 %collective-permute-start.6 = (bf16[32,2048]{1,0:T(8,128)(2,1)S(1)}, bf16[32,2048]{1,0:T(8,128)(2,1)S(1)}, u32[]{:S(2)}, u32[]{:S(2)}) collective-permute-start(bf16[32,2048]{1,0:T(8,128)(2,1)S(1)} %get-tuple-element.31), channel_id=1, source_target_pairs={{0,12},{1,13},{2,14},{3,15},{4,8},{5,9},{6,10},{7,11},{8,4},{9,5},... | collective-permute-start | bytes 393224 | tf_op jit(solution)/shard_map/ppermute | solution.py:24
  6.7 1.5 %collective-permute-start = (bf16[64,2048]{1,0:T(8,128)(2,1)S(1)}, bf16[64,2048]{1,0:T(8,128)(2,1)S(1)}, u32[]{:S(2)}, u32[]{:S(2)}) collective-permute-start(bf16[64,2048]{1,0:T(8,128)(2,1)S(1)} %get-tuple-element.26), channel_id=1, source_target_pairs={{0,1},{1,0},{2,3},{3,2},{4,5},{5,4},{6,7},{7,6},{8,9},{9,8},{10,11... | collective-permute-start | bytes 786440 | tf_op jit(solution)/shard_map/ppermute | solution.py:24
  8.3 5.6 %collective-permute-start.1 = (bf16[32,2048]{1,0:T(8,128)(2,1)S(1)}, bf16[32,2048]{1,0:T(8,128)(2,1)S(1)}, u32[]{:S(2)}, u32[]{:S(2)}) collective-permute-start(bf16[32,2048]{1,0:T(8,128)(2,1)S(1)} %pad_maximum_fusion), channel_id=1, source_target_pairs={{0,2},{1,3},{2,0},{3,1},{4,6},{5,7},{6,4},{7,5},{8,10},{9,11},{10,... | collective-permute-start | bytes 393224 | tf_op jit(solution)/shard_map/ppermute | solution.py:24
  9.9 8.1 %collective-permute-start.2 = (bf16[32,2048]{1,0:T(8,128)(2,1)S(1)}, bf16[32,2048]{1,0:T(8,128)(2,1)S(1)}, u32[]{:S(2)}, u32[]{:S(2)}) collective-permute-start(bf16[32,2048]{1,0:T(8,128)(2,1)S(1)} %pad_maximum_fusion.1), channel_id=1, source_target_pairs={{0,4},{1,5},{2,6},{3,7},{4,0},{5,1},{6,2},{7,3},{8,12},{9,13},{10,... | collective-permute-start | bytes 393224 | tf_op jit(solution)/shard_map/ppermute | solution.py:24
  10.2 11.7 %collective-permute-start.3 = (bf16[32,2048]{1,0:T(8,128)(2,1)S(1)}, bf16[32,2048]{1,0:T(8,128)(2,1)S(1)}, u32[]{:S(2)}, u32[]{:S(2)}) collective-permute-start(bf16[32,2048]{1,0:T(8,128)(2,1)S(1)} %pad_maximum_fusion.2), channel_id=1, source_target_pairs={{0,6},{1,7},{2,4},{3,5},{4,2},{5,3},{6,0},{7,1},{8,14},{9,15},{10,... | collective-permute-start | bytes 393224 | tf_op jit(solution)/shard_map/ppermute | solution.py:24
  15.4 13.6 %collective-permute-start.5 = (bf16[32,2048]{1,0:T(8,128)(2,1)S(1)}, bf16[32,2048]{1,0:T(8,128)(2,1)S(1)}, u32[]{:S(2)}, u32[]{:S(2)}) collective-permute-start(bf16[32,2048]{1,0:T(8,128)(2,1)S(1)} %get-tuple-element.30), channel_id=1, source_target_pairs={{0,10},{1,11},{2,8},{3,9},{4,14},{5,15},{6,12},{7,13},{8,2},{9,3},... | collective-permute-start | bytes 393224 | tf_op jit(solution)/shard_map/ppermute | solution.py:24
  18.1 12.4 %collective-permute-start.9 = (bf16[16,2048]{1,0:T(8,128)(2,1)S(1)}, bf16[16,2048]{1,0:T(8,128)(2,1)S(1)}, u32[]{:S(2)}, u32[]{:S(2)}) collective-permute-start(bf16[16,2048]{1,0:T(8,128)(2,1)S(1)} %get-tuple-element.33), channel_id=1, source_target_pairs={{0,14},{1,15},{2,12},{3,13},{4,10},{5,11},{6,8},{7,9},{8,6},{9,7},... | collective-permute-start | bytes 196616 | tf_op jit(solution)/shard_map/ppermute | solution.py:24
  22.0 8.6 %collective-permute-start.10 = (bf16[16,2048]{1,0:T(8,128)(2,1)S(1)}, bf16[16,2048]{1,0:T(8,128)(2,1)S(1)}, u32[]{:S(2)}, u32[]{:S(2)}) collective-permute-start(bf16[16,2048]{1,0:T(8,128)(2,1)S(1)} %get-tuple-element.35), channel_id=1, source_target_pairs={{0,15},{1,14},{2,13},{3,12},{4,11},{5,10},{6,9},{7,8},{8,7},{9,6},... | collective-permute-start | bytes 196616 | tf_op jit(solution)/shard_map/ppermute | solution.py:24
  24.6 4.5 %collective-permute-start.7 = (bf16[16,2048]{1,0:T(8,128)(2,1)S(1)}, bf16[16,2048]{1,0:T(8,128)(2,1)S(1)}, u32[]{:S(2)}, u32[]{:S(2)}) collective-permute-start(bf16[16,2048]{1,0:T(8,128)(2,1)S(1)} %get-tuple-element.66), channel_id=1, source_target_pairs={{0,1},{1,0},{2,3},{3,2},{4,5},{5,4},{6,7},{7,6},{8,9},{9,8},{10,11... | collective-permute-start | bytes 196616 | tf_op jit(solution)/shard_map/ppermute | solution.py:24
  29.1 1.4 %collective-permute-start.8 = (bf16[32,2048]{1,0:T(8,128)(2,1)S(1)}, bf16[32,2048]{1,0:T(8,128)(2,1)S(1)}, u32[]{:S(2)}, u32[]{:S(2)}) collective-permute-start(bf16[32,2048]{1,0:T(8,128)(2,1)S(1)} %pad_maximum_fusion.3), channel_id=1, source_target_pairs={{0,1},{1,0},{2,3},{3,2},{4,5},{5,4},{6,7},{7,6},{8,9},{9,8},{10,11... | collective-permute-start | bytes 393224 | tf_op jit(solution)/shard_map/ppermute | solution.py:24
  30.5 19.5 %copy-start.1 = (f32[16,2048]{1,0:T(8,128)S(1)}, f32[16,2048]{1,0:T(8,128)}, u32[]{:S(2)}) copy-start(f32[16,2048]{1,0:T(8,128)} %param.9) | copy-start | bytes 393220
  33.4 2.0 %collective-permute-start.11 = (bf16[128,2048]{1,0:T(8,128)(2,1)S(1)}, bf16[128,2048]{1,0:T(8,128)(2,1)S(1)}, u32[]{:S(2)}, u32[]{:S(2)}) collective-permute-start(bf16[128,2048]{1,0:T(8,128)(2,1)S(1)} %get-tuple-element.41), channel_id=1, source_target_pairs={{0,1},{1,0},{2,3},{3,2},{4,5},{5,4},{6,7},{7,6},{8,9},{9,8},{10,11... | collective-permute-start | bytes 1572872 | tf_op jit(solution)/shard_map/ppermute | solution.py:24
  33.6 1.8 %collective-permute-start.12 = (f32[16,128]{1,0:T(8,128)S(1)}, f32[16,128]{1,0:T(8,128)S(1)}, u32[]{:S(2)}, u32[]{:S(2)}) collective-permute-start(f32[16,128]{1,0:T(8,128)S(1)} %bitcast.26), channel_id=1, source_target_pairs={{0,1},{1,0},{2,3},{3,2},{4,5},{5,4},{6,7},{7,6},{8,9},{9,8},{10,11... | collective-permute-start | bytes 24584 | tf_op jit(solution)/shard_map/ppermute | solution.py:24
  35.7 5.9 %collective-permute-start.13 = (f16[48,2176]{1,0:T(8,128)(2,1)S(1)}, f16[48,2176]{1,0:T(8,128)(2,1)S(1)}, u32[]{:S(2)}, u32[]{:S(2)}) collective-permute-start(f16[48,2176]{1,0:T(8,128)(2,1)S(1)} %fusion.4), channel_id=1, source_target_pairs={{0,2},{1,5},{2,0},{3,7},{4,6},{5,1},{6,4},{7,3},{8,10},{9,13},{10,... | collective-permute-start | bytes 626696 | tf_op jit(solution)/shard_map/ppermute | solution.py:184
  37.1 5.2 %collective-permute-start.15 = (f16[16,2176]{1,0:T(8,128)(2,1)S(1)}, f16[16,2176]{1,0:T(8,128)(2,1)S(1)}, u32[]{:S(2)}, u32[]{:S(2)}) collective-permute-start(f16[16,2176]{1,0:T(8,128)(2,1)S(1)} %get-tuple-element.43), channel_id=1, source_target_pairs={{0,4},{1,3},{2,6},{3,1},{4,0},{5,7},{6,2},{7,5},{8,12},{9,11},{10,... | collective-permute-start | bytes 208904 | tf_op jit(solution)/shard_map/ppermute | solution.py:184
  37.4 6.3 %collective-permute-start.16 = (f16[16,2176]{1,0:T(8,128)(2,1)S(1)}, f16[16,2176]{1,0:T(8,128)(2,1)S(1)}, u32[]{:S(2)}, u32[]{:S(2)}) collective-permute-start(f16[16,2176]{1,0:T(8,128)(2,1)S(1)} %get-tuple-element.44), channel_id=1, source_target_pairs={{0,6},{1,7},{2,4},{3,5},{4,2},{5,3},{6,0},{7,1},{8,14},{9,15},{10,... | collective-permute-start | bytes 208904 | tf_op jit(solution)/shard_map/ppermute | solution.py:184
  43.7 6.1 %collective-permute-start.17 = (f16[16,2176]{1,0:T(8,128)(2,1)S(1)}, f16[16,2176]{1,0:T(8,128)(2,1)S(1)}, u32[]{:S(2)}, u32[]{:S(2)}) collective-permute-start(f16[16,2176]{1,0:T(8,128)(2,1)S(1)} %get-tuple-element.45), channel_id=1, source_target_pairs={{0,8},{1,9},{2,10},{3,11},{4,12},{5,13},{6,14},{7,15},{8,0},{9,1},... | collective-permute-start | bytes 208904 | tf_op jit(solution)/shard_map/ppermute | solution.py:24
  45.2 4.9 %collective-permute-start.14 = (f16[16,2048]{1,0:T(8,128)(2,1)S(1)}, f16[16,2048]{1,0:T(8,128)(2,1)S(1)}, u32[]{:S(2)}, u32[]{:S(2)}) collective-permute-start(f16[16,2048]{1,0:T(8,128)(2,1)S(1)} %fusion.17), channel_id=1, source_target_pairs={{0,4},{1,3},{2,6},{3,1},{4,0},{5,7},{6,2},{7,5},{8,12},{9,11},{10,... | collective-permute-start | bytes 196616 | tf_op jit(solution)/shard_map/ppermute | solution.py:184
